TPU v7x, 32 devices: a whole 2x2x4 slice. The times are simulated.
32 devices in a mesh: dp: 8 (over y, x, core), seq: 4 (over z).
Axes of the slice: x: 2, y: 2, z: 4, core: 2. Of those that a mesh axis runs over, the one named last changes fastest.
Arguments:
- features: bfloat16 [8, 512, 1024], P('dp', 'seq'), may hold values from -6 to 6
- utterance_ends: int32 [8, 4], P('dp'), may hold values from 64 to 512, as said below
- kernel_weight: bfloat16 [1024, 8192], P(('dp', 'seq')), may hold values from -0.0625 to 0.0625
- position_bias: bfloat16 [1024], P(('dp', 'seq')), may hold values from -1.75 to 1.75
- entry_gain: bfloat16 [1024], P(('dp', 'seq')), may hold values from 0.5 to 1.5
- base_shift: bfloat16 [1024], P(('dp', 'seq')), may hold values from -1.25 to 1.25
- joint_weight: bfloat16 [2, 1024, 3072], P(None, ('dp', 'seq')), may hold values from -0.1875 to 0.1875
- query_bias: bfloat16 [2, 1024], P(None, ('dp', 'seq')), may hold values from -3 to 3
- value_bias: bfloat16 [2, 1024], P(None, ('dp', 'seq')), may hold values from -1.75 to 1.75
- output_weight: bfloat16 [2, 1024, 1024], P(None, ('dp', 'seq')), may hold values from -3 to 3
- attend_bias: bfloat16 [2, 1024], P(None, ('dp', 'seq')), may hold values from -1.75 to 1.75
- middle_gain: bfloat16 [2, 1024], P(None, ('dp', 'seq')), may hold values from 0.5 to 1.5
- lower_shift: bfloat16 [2, 1024], P(None, ('dp', 'seq')), may hold values from -1.25 to 1.25
- expand_weight: bfloat16 [2, 1024, 4096], P(None, ('dp', 'seq')), may hold values from -0.1875 to 0.1875
- hidden_bias: bfloat16 [2, 4096], P(None, ('dp', 'seq')), may hold values from -1.75 to 1.75
- reduce_weight: bfloat16 [2, 4096, 1024], P(None, ('dp', 'seq')), may hold values from -0.09375 to 0.09375
- return_bias: bfloat16 [2, 1024], P(None, ('dp', 'seq')), may hold values from -1.75 to 1.75
- final_gain: bfloat16 [2, 1024], P(None, ('dp', 'seq')), may hold values from 0.5 to 1.5
- upper_shift: bfloat16 [2, 1024], P(None, ('dp', 'seq')), may hold values from -1.25 to 1.25
- head_weight: bfloat16 [1024, 32], P(('dp', 'seq')), may hold values from -0.1875 to 0.1875
- vocab_bias: bfloat16 [32], replicated, may hold values from -3 to 3
- cotangent: bfloat16 [8, 512, 32], P('dp', 'seq'), may hold values from -6 to 6
Outputs:
- logits: float32 [8, 512, 32], P('dp', 'seq')
- features_grad: float32 [8, 512, 1024], P('dp', 'seq')
- kernel_grad: float32 [1024, 8192], P(('dp', 'seq'))
- position_grad: float32 [1024], P(('dp', 'seq'))
- entry_grad: float32 [1024], P(('dp', 'seq'))
- base_grad: float32 [1024], P(('dp', 'seq'))
- joint_grad: float32 [2, 1024, 3072], P(None, ('dp', 'seq'))
- query_grad: float32 [2, 1024], P(None, ('dp', 'seq'))
- value_grad: float32 [2, 1024], P(None, ('dp', 'seq'))
- output_grad: float32 [2, 1024, 1024], P(None, ('dp', 'seq'))
- attend_grad: float32 [2, 1024], P(None, ('dp', 'seq'))
- middle_grad: float32 [2, 1024], P(None, ('dp', 'seq'))
- lower_grad: float32 [2, 1024], P(None, ('dp', 'seq'))
- expand_grad: float32 [2, 1024, 4096], P(None, ('dp', 'seq'))
- hidden_grad: float32 [2, 4096], P(None, ('dp', 'seq'))
- reduce_grad: float32 [2, 4096, 1024], P(None, ('dp', 'seq'))
- return_grad: float32 [2, 1024], P(None, ('dp', 'seq'))
- final_grad: float32 [2, 1024], P(None, ('dp', 'seq'))
- upper_grad: float32 [2, 1024], P(None, ('dp', 'seq'))
- head_grad: float32 [1024, 32], P(('dp', 'seq'))
- vocab_grad: float32 [32], replicated
Inputs may be any that keep to these rules, and one draw needn't show every extreme that they name: The ends of a row never fall; utterance j holds the frames from utterance_ends[r, j - 1] (0 for j = 0) up to utterance_ends[r, j] - 1, so a repeated end is an empty slot; frames from utterance_ends[r, 3] on are padding, and one row is filled to its last frame. Each row holds one to three utterances, and in every row one utterance begins on the first device along seq and ends on the last.
All inputs are finite; a program needn't handle non-finite values.
Results may differ from a plain program's by a relative error of at most 0.017.
Values may be sent and summed in bfloat16 or wider, within the bound.
A program may use at most 640 MiB of HBM per device.

v0:
```python
import math

import jax
import jax.numpy as jnp
from jax import lax
from jax.sharding import PartitionSpec as P

HEADS = 16
CONV_G = 16


epsilon = 1e-05
masked_score = -1e30


def with_halo(cells, sides, width):
    for axis, dim in sides:
        count = lax.axis_size(axis)
        ends = count - 1
        head = lax.slice_in_dim(cells, 0, width, axis=dim)
        tail = lax.slice_in_dim(cells, cells.shape[dim] - width, cells.shape[dim], axis=dim)
        cells = jnp.concatenate(
            [
                lax.ppermute(tail, axis, [(i, (i + 1) % count) for i in range(ends)]),
                cells,
                lax.ppermute(head, axis, [((i + 1) % count, i) for i in range(ends)]),
            ],
            axis=dim,
        )
    return cells


def layer_norm(tensor, scaling, shifts):
    average = jnp.mean(tensor, axis=-1, keepdims=True)
    centred = tensor - average
    spread = jnp.mean(centred * centred, axis=-1, keepdims=True)
    return centred * lax.rsqrt(spread + epsilon) * scaling + shifts


def norm_pullback(tensor, scaling, upstream):
    _, pullback = jax.vjp(layer_norm, tensor, scaling, jnp.zeros_like(scaling))
    return pullback(upstream)


def gelu_exact(tensor):
    return jax.nn.gelu(tensor, approximate=False)


def rounded(tensor):
    return tensor.astype(jnp.bfloat16)


def widened(tensor):
    return tensor.astype(jnp.float32)


def segment_ids(positions, utterance_ends):
    return jnp.sum(
        (positions[None, :, None] >= utterance_ends[:, None, :]).astype(jnp.int32), axis=2
    )


def unfold(source, source_ids, target_ids, anchors):
    length = target_ids.shape[1]
    pieces = [lax.slice_in_dim(source, anchor, anchor + length, axis=1) for anchor in anchors]
    matches = [
        lax.slice_in_dim(source_ids, anchor, anchor + length, axis=1) == target_ids
        for anchor in anchors
    ]
    stacked = jnp.stack(pieces, axis=2)
    keepers = jnp.stack(matches, axis=2)
    return jnp.where(keepers[..., None], stacked, jnp.zeros_like(stacked))


def conv_forward(halo_feats, halo_ids, frame_ids, kernel_grid, tap_block):
    row_count, frame_count = frame_ids.shape
    groups, group_width, tap_count, inner_width = kernel_grid.shape
    summed = jnp.zeros((row_count, frame_count, groups, group_width), jnp.float32)
    for block_at in range(tap_count // tap_block):
        first_tap = block_at * tap_block
        window = unfold(
            halo_feats,
            halo_ids,
            frame_ids,
            [first_tap + inner_tap for inner_tap in range(tap_block)],
        )
        window = window.reshape(row_count, frame_count, tap_block, groups, inner_width)
        summed = summed + jnp.einsum(
            "rtkgi,goki->rtgo",
            window,
            kernel_grid[:, :, first_tap : first_tap + tap_block, :],
            preferred_element_type=jnp.float32,
        )
    return summed.reshape(row_count, frame_count, groups * group_width)


def conv_backward(halo_grads, halo_feats, halo_ids, frame_ids, kernel_grid, tap_block, conv_low):
    row_count, frame_count = frame_ids.shape
    groups, group_width, tap_count, inner_width = kernel_grid.shape
    input_part = jnp.zeros((row_count, frame_count, groups, inner_width), jnp.float32)
    grouped = conv_low.reshape(row_count, frame_count, groups, group_width)
    kernel_parts = []
    for block_at in range(tap_count // tap_block):
        first_tap = block_at * tap_block
        tap_list = [first_tap + inner_tap for inner_tap in range(tap_block)]
        grads_window = unfold(
            halo_grads, halo_ids, frame_ids, [tap_count - tap_at for tap_at in tap_list]
        )
        grads_window = grads_window.reshape(row_count, frame_count, tap_block, groups, group_width)
        input_part = input_part + jnp.einsum(
            "rtkgo,goki->rtgi",
            grads_window,
            kernel_grid[:, :, first_tap : first_tap + tap_block, :],
            preferred_element_type=jnp.float32,
        )
        feats_window = unfold(halo_feats, halo_ids, frame_ids, tap_list)
        feats_window = feats_window.reshape(row_count, frame_count, tap_block, groups, inner_width)
        kernel_parts.append(
            jnp.einsum(
                "rtgo,rtkgi->goki", grouped, feats_window, preferred_element_type=jnp.float32
            )
        )
    kernel_full = jnp.concatenate(kernel_parts, axis=2).reshape(
        groups * group_width, tap_count * inner_width
    )
    return (input_part.reshape(row_count, frame_count, groups * inner_width), kernel_full)


def split_heads(tensor, head_count):
    return tensor.reshape(
        tensor.shape[0], tensor.shape[1], head_count, tensor.shape[2] // head_count
    )


def attend_scores(queries, all_keys, query_ids, key_ids, head_count):
    scores = jnp.einsum(
        "rqhd,rkhd->rhqk",
        split_heads(queries, head_count),
        split_heads(all_keys, head_count),
        preferred_element_type=jnp.float32,
    )
    allowed = query_ids[:, None, :, None] == key_ids[:, None, None, :]
    return jnp.where(allowed, scores, masked_score)


def attend_forward(queries, all_keys, all_values, frame_ids, row_ids, head_count):
    scores = attend_scores(queries, all_keys, frame_ids, row_ids, head_count)
    row_peak = jnp.max(scores, axis=-1, keepdims=True)
    exponent = jnp.exp(scores - row_peak)
    totals = jnp.sum(exponent, axis=-1, keepdims=True)
    weights_low = rounded(exponent / totals)
    context = jnp.einsum(
        "rhqk,rkhd->rqhd",
        weights_low,
        split_heads(all_values, head_count),
        preferred_element_type=jnp.float32,
    )
    return (rounded(context.reshape(queries.shape)), row_peak + jnp.log(totals))


def attend_backward(
    queries, all_keys, all_values, frame_ids, row_ids, head_count, log_totals, context_low
):
    scores = attend_scores(queries, all_keys, frame_ids, row_ids, head_count)
    attention = jnp.exp(scores - log_totals)
    weights_low = rounded(attention)
    grad_heads = split_heads(context_low, head_count)
    prob_grad = jnp.einsum(
        "rqhd,rkhd->rhqk",
        grad_heads,
        split_heads(all_values, head_count),
        preferred_element_type=jnp.float32,
    )
    row_delta = jnp.sum(attention * prob_grad, axis=-1, keepdims=True)
    score_grad = rounded(attention * (prob_grad - row_delta))
    value_part = jnp.einsum(
        "rhqk,rqhd->rkhd", weights_low, grad_heads, preferred_element_type=jnp.float32
    )
    query_part = jnp.einsum(
        "rhqk,rkhd->rqhd",
        score_grad,
        split_heads(all_keys, head_count),
        preferred_element_type=jnp.float32,
    )
    key_part = jnp.einsum(
        "rhqk,rqhd->rkhd",
        score_grad,
        split_heads(queries, head_count),
        preferred_element_type=jnp.float32,
    )
    return (
        query_part.reshape(queries.shape),
        key_part.reshape(all_keys.shape),
        value_part.reshape(all_values.shape),
    )


def local(
    features,
    utterance_ends,
    kernel_weight,
    position_bias,
    entry_gain,
    base_shift,
    joint_weight,
    query_bias,
    value_bias,
    output_weight,
    attend_bias,
    middle_gain,
    lower_shift,
    expand_weight,
    hidden_bias,
    reduce_weight,
    return_bias,
    final_gain,
    upper_shift,
    head_weight,
    vocab_bias,
    cotangent,
):
    row_count, frame_count, model_dim = features.shape
    frames_all = frame_count * lax.axis_size("seq")
    groups = CONV_G
    group_width = model_dim // groups
    tap_count = kernel_weight.shape[1] // group_width
    half_taps = tap_count // 2
    tap_block = math.gcd(tap_count, 16)
    head_count = HEADS
    query_scale = (model_dim // head_count) ** (-0.5)
    layer_count = joint_weight.shape[0]
    rows_share = model_dim // lax.axis_size(("dp", "seq"))
    anchor = lax.axis_index("seq") * frame_count
    frame_ids = segment_ids(anchor + jnp.arange(frame_count, dtype=jnp.int32), utterance_ends)
    row_ids = segment_ids(jnp.arange(frames_all, dtype=jnp.int32), utterance_ends)
    halo_place = anchor - half_taps + jnp.arange(frame_count + tap_count, dtype=jnp.int32)
    inside = (halo_place >= 0) & (halo_place < frames_all)
    halo_ids = jnp.where(inside[None, :], segment_ids(halo_place, utterance_ends), -1)
    stem = (
        lax.all_gather(kernel_weight, ("dp", "seq"), axis=0, tiled=True),
        lax.all_gather(position_bias, ("dp", "seq"), axis=0, tiled=True),
        lax.all_gather(entry_gain, ("dp", "seq"), axis=0, tiled=True),
        lax.all_gather(base_shift, ("dp", "seq"), axis=0, tiled=True),
        lax.all_gather(head_weight, ("dp", "seq"), axis=0, tiled=True),
    )
    kernel_grid = stem[0].reshape(groups, group_width, tap_count, group_width)
    halo_feats = with_halo(features, (("seq", 1),), half_taps)
    conv_pre = conv_forward(halo_feats, halo_ids, frame_ids, kernel_grid, tap_block) + widened(
        stem[1]
    )
    mixed = widened(features) + gelu_exact(conv_pre)
    hidden = layer_norm(mixed, widened(stem[2]), widened(stem[3]))
    saved = []
    for layer_at in range(layer_count):
        (
            joint_full,
            query_full,
            value_full,
            output_full,
            attend_full,
            middle_full,
            lower_full,
            expand_full,
            hidden_full,
            reduce_full,
            return_full,
            final_full,
            upper_full,
        ) = (
            lax.all_gather(joint_weight[layer_at], ("dp", "seq"), axis=0, tiled=True),
            lax.all_gather(query_bias[layer_at], ("dp", "seq"), axis=0, tiled=True),
            lax.all_gather(value_bias[layer_at], ("dp", "seq"), axis=0, tiled=True),
            lax.all_gather(output_weight[layer_at], ("dp", "seq"), axis=0, tiled=True),
            lax.all_gather(attend_bias[layer_at], ("dp", "seq"), axis=0, tiled=True),
            lax.all_gather(middle_gain[layer_at], ("dp", "seq"), axis=0, tiled=True),
            lax.all_gather(lower_shift[layer_at], ("dp", "seq"), axis=0, tiled=True),
            lax.all_gather(expand_weight[layer_at], ("dp", "seq"), axis=0, tiled=True),
            lax.all_gather(hidden_bias[layer_at], ("dp", "seq"), axis=0, tiled=True),
            lax.all_gather(reduce_weight[layer_at], ("dp", "seq"), axis=0, tiled=True),
            lax.all_gather(return_bias[layer_at], ("dp", "seq"), axis=0, tiled=True),
            lax.all_gather(final_gain[layer_at], ("dp", "seq"), axis=0, tiled=True),
            lax.all_gather(upper_shift[layer_at], ("dp", "seq"), axis=0, tiled=True),
        )
        inputs_low = rounded(hidden)
        joint_out = jnp.einsum(
            "rtd,de->rte", inputs_low, joint_full, preferred_element_type=jnp.float32
        )
        queries = rounded((joint_out[..., :model_dim] + widened(query_full)) * query_scale)
        keys_local = rounded(joint_out[..., model_dim : 2 * model_dim])
        values_local = rounded(joint_out[..., 2 * model_dim :] + widened(value_full))
        all_keys, all_values = (
            lax.all_gather(keys_local, "seq", axis=1, tiled=True),
            lax.all_gather(values_local, "seq", axis=1, tiled=True),
        )
        context, log_totals = attend_forward(
            queries, all_keys, all_values, frame_ids, row_ids, head_count
        )
        attended = jnp.einsum(
            "rtc,cd->rtd", context, output_full, preferred_element_type=jnp.float32
        ) + widened(attend_full)
        residual_one = hidden + attended
        middle = layer_norm(residual_one, widened(middle_full), widened(lower_full))
        middle_low = rounded(middle)
        inner_pre = jnp.einsum(
            "rtd,df->rtf", middle_low, expand_full, preferred_element_type=jnp.float32
        ) + widened(hidden_full)
        activated = rounded(gelu_exact(inner_pre))
        outer = (
            middle
            + jnp.einsum("rtf,fd->rtd", activated, reduce_full, preferred_element_type=jnp.float32)
            + widened(return_full)
        )
        kept_weights = None
        saved.append(
            (
                inputs_low,
                queries,
                all_keys,
                all_values,
                log_totals,
                context,
                residual_one,
                middle_low,
                inner_pre,
                activated,
                outer,
                kept_weights,
            )
        )
        hidden = layer_norm(outer, widened(final_full), widened(upper_full))
    final_low = rounded(hidden)
    logits = jnp.einsum(
        "rtd,dv->rtv", final_low, stem[4], preferred_element_type=jnp.float32
    ) + widened(vocab_bias)
    back_stem = (
        lax.all_gather(kernel_weight, ("dp", "seq"), axis=0, tiled=True),
        lax.all_gather(entry_gain, ("dp", "seq"), axis=0, tiled=True),
        lax.all_gather(head_weight, ("dp", "seq"), axis=0, tiled=True),
    )
    vocab_sum = jnp.sum(widened(cotangent), axis=(0, 1))
    head_part = jnp.einsum("rtd,rtv->dv", final_low, cotangent, preferred_element_type=jnp.float32)
    flow_grad = jnp.einsum(
        "rtv,dv->rtd", cotangent, back_stem[2], preferred_element_type=jnp.float32
    )
    layer_grads = [None] * layer_count
    for layer_at in reversed(range(layer_count)):
        (
            inputs_low,
            queries,
            all_keys,
            all_values,
            log_totals,
            context,
            residual_one,
            middle_low,
            inner_pre,
            activated,
            outer,
            kept_weights,
        ) = saved[layer_at]
        back_weights = (
            lax.all_gather(joint_weight[layer_at], ("dp", "seq"), axis=0, tiled=True),
            lax.all_gather(output_weight[layer_at], ("dp", "seq"), axis=0, tiled=True),
            lax.all_gather(expand_weight[layer_at], ("dp", "seq"), axis=0, tiled=True),
            lax.all_gather(reduce_weight[layer_at], ("dp", "seq"), axis=0, tiled=True),
            lax.all_gather(middle_gain[layer_at], ("dp", "seq"), axis=0, tiled=True),
            lax.all_gather(final_gain[layer_at], ("dp", "seq"), axis=0, tiled=True),
        )
        joint_full, output_full, expand_full, reduce_full, middle_full, final_full = back_weights
        outer_grad, final_part, upper_part = norm_pullback(outer, widened(final_full), flow_grad)
        fed_low = rounded(outer_grad)
        return_part = jnp.sum(widened(fed_low), axis=(0, 1))
        active_grad = jnp.einsum(
            "rtd,fd->rtf", fed_low, reduce_full, preferred_element_type=jnp.float32
        )
        _, gelu_pull = jax.vjp(gelu_exact, inner_pre)
        (inner_grad,) = gelu_pull(active_grad)
        inner_low = rounded(inner_grad)
        hidden_part = jnp.sum(widened(inner_low), axis=(0, 1))
        middle_flow = outer_grad + jnp.einsum(
            "rtf,df->rtd", inner_low, expand_full, preferred_element_type=jnp.float32
        )
        residual_grad, middle_part, lower_part = norm_pullback(
            residual_one, widened(middle_full), middle_flow
        )
        attended_low = rounded(residual_grad)
        attend_part = jnp.sum(widened(attended_low), axis=(0, 1))
        context_low = rounded(
            jnp.einsum("rtd,cd->rtc", attended_low, output_full, preferred_element_type=jnp.float32)
        )
        query_raw, key_raw, value_raw = attend_backward(
            queries, all_keys, all_values, frame_ids, row_ids, head_count, log_totals, context_low
        )
        key_sum, value_sum = (
            lax.psum_scatter(
                key_raw.astype(jnp.bfloat16), "seq", scatter_dimension=1, tiled=True
            ).astype(jnp.float32),
            lax.psum_scatter(
                value_raw.astype(jnp.bfloat16), "seq", scatter_dimension=1, tiled=True
            ).astype(jnp.float32),
        )
        query_low = rounded(widened(rounded(query_raw)) * query_scale)
        key_low = rounded(key_sum)
        value_low = rounded(value_sum)
        query_part = jnp.sum(widened(query_low), axis=(0, 1))
        value_part = jnp.sum(widened(value_low), axis=(0, 1))
        joint_low = jnp.concatenate([query_low, key_low, value_low], axis=-1)
        flow_grad = residual_grad + jnp.einsum(
            "rte,de->rtd", joint_low, joint_full, preferred_element_type=jnp.float32
        )
        ratio = hidden_part.shape[0] // model_dim
        vector_rows = jnp.stack(
            [
                query_part,
                value_part,
                attend_part,
                middle_part,
                lower_part,
                return_part,
                final_part,
                upper_part,
            ],
            axis=1,
        )
        hidden_rows = hidden_part.reshape(model_dim, ratio)

        def layer_term(
            start,
            count,
            inputs_low=inputs_low,
            joint_low=joint_low,
            context=context,
            attended_low=attended_low,
            middle_low=middle_low,
            inner_low=inner_low,
            activated=activated,
            fed_low=fed_low,
            vector_rows=vector_rows,
            hidden_rows=hidden_rows,
            ratio=ratio,
        ):
            joint_rows = jnp.einsum(
                "rtd,rte->de", inputs_low, joint_low, preferred_element_type=jnp.float32
            )
            output_rows = jnp.einsum(
                "rtc,rtd->cd", context, attended_low, preferred_element_type=jnp.float32
            )
            expand_rows = jnp.einsum(
                "rtd,rtf->df", middle_low, inner_low, preferred_element_type=jnp.float32
            )
            reduce_rows = jnp.einsum(
                "rtf,rtd->fd", activated, fed_low, preferred_element_type=jnp.float32
            ).reshape(count, ratio * model_dim)
            return jnp.concatenate(
                [joint_rows, output_rows, expand_rows, reduce_rows, vector_rows, hidden_rows],
                axis=1,
            )

        summed = lax.psum_scatter(
            layer_term(jnp.int32(0), rows_share * lax.axis_size(("dp", "seq"))),
            ("dp", "seq"),
            scatter_dimension=0,
            tiled=True,
        )
        ff_width = ratio * model_dim
        first = 3 * model_dim
        second = first + model_dim
        third = second + ff_width
        fourth = third + ratio * model_dim
        joint_own = summed[:, :first]
        output_own = summed[:, first:second]
        expand_own = summed[:, second:third]
        reduce_own = summed[:, third:fourth].reshape(rows_share * ratio, model_dim)
        vector_own = summed[:, fourth : fourth + 8]
        hidden_own = summed[:, fourth + 8 :].reshape(rows_share * ratio)
        layer_grads[layer_at] = (
            joint_own,
            vector_own[:, 0],
            vector_own[:, 1],
            output_own,
            vector_own[:, 2],
            vector_own[:, 3],
            vector_own[:, 4],
            expand_own,
            hidden_own,
            reduce_own,
            vector_own[:, 5],
            vector_own[:, 6],
            vector_own[:, 7],
        )
    mixed_grad, entry_part, base_part = norm_pullback(mixed, widened(back_stem[1]), flow_grad)
    _, gelu_pull = jax.vjp(gelu_exact, conv_pre)
    (conv_grad,) = gelu_pull(mixed_grad)
    conv_low = rounded(conv_grad)
    position_part = jnp.sum(widened(conv_low), axis=(0, 1))
    halo_grads = with_halo(conv_low, (("seq", 1),), half_taps)
    back_grid = back_stem[0].reshape(groups, group_width, tap_count, group_width)
    input_part, kernel_part = conv_backward(
        halo_grads, halo_feats, halo_ids, frame_ids, back_grid, tap_block, conv_low
    )
    features_grad = mixed_grad + input_part
    vocab_tiled = jnp.tile(vocab_sum, lax.axis_size(("dp", "seq")))
    stem_sums = (
        lax.psum_scatter(kernel_part, ("dp", "seq"), scatter_dimension=0, tiled=True),
        lax.psum_scatter(position_part, ("dp", "seq"), scatter_dimension=0, tiled=True),
        lax.psum_scatter(entry_part, ("dp", "seq"), scatter_dimension=0, tiled=True),
        lax.psum_scatter(base_part, ("dp", "seq"), scatter_dimension=0, tiled=True),
        lax.psum_scatter(head_part, ("dp", "seq"), scatter_dimension=0, tiled=True),
        lax.psum_scatter(vocab_tiled, ("dp", "seq"), scatter_dimension=0, tiled=True),
    )
    stacked = [
        jnp.stack([layer_grads[layer_at][member] for layer_at in range(layer_count)])
        for member in range(13)
    ]
    return (
        logits,
        features_grad,
        stem_sums[0],
        stem_sums[1],
        stem_sums[2],
        stem_sums[3],
        stacked[0],
        stacked[1],
        stacked[2],
        stacked[3],
        stacked[4],
        stacked[5],
        stacked[6],
        stacked[7],
        stacked[8],
        stacked[9],
        stacked[10],
        stacked[11],
        stacked[12],
        stem_sums[4],
        stem_sums[5],
    )


def solution(mesh):
    return jax.shard_map(
        local,
        mesh=mesh,
        in_specs=(
            P("dp", "seq", None),
            P("dp", None),
            P(("dp", "seq"), None),
            P(("dp", "seq")),
            P(("dp", "seq")),
            P(("dp", "seq")),
            P(None, ("dp", "seq"), None),
            P(None, ("dp", "seq")),
            P(None, ("dp", "seq")),
            P(None, ("dp", "seq"), None),
            P(None, ("dp", "seq")),
            P(None, ("dp", "seq")),
            P(None, ("dp", "seq")),
            P(None, ("dp", "seq"), None),
            P(None, ("dp", "seq")),
            P(None, ("dp", "seq"), None),
            P(None, ("dp", "seq")),
            P(None, ("dp", "seq")),
            P(None, ("dp", "seq")),
            P(("dp", "seq"), None),
            P(),
            P("dp", "seq", None),
        ),
        out_specs=(
            P("dp", "seq", None),
            P("dp", "seq", None),
            P(("dp", "seq"), None),
            P(("dp", "seq")),
            P(("dp", "seq")),
            P(("dp", "seq")),
            P(None, ("dp", "seq"), None),
            P(None, ("dp", "seq")),
            P(None, ("dp", "seq")),
            P(None, ("dp", "seq"), None),
            P(None, ("dp", "seq")),
            P(None, ("dp", "seq")),
            P(None, ("dp", "seq")),
            P(None, ("dp", "seq"), None),
            P(None, ("dp", "seq")),
            P(None, ("dp", "seq"), None),
            P(None, ("dp", "seq")),
            P(None, ("dp", "seq")),
            P(None, ("dp", "seq")),
            P(("dp", "seq"), None),
            P(),
        ),
        check_vma=False,
    )
```

profile of v0, /device:TPU:16, one launch (start us, length us, event | category | flops | bytes accessed | tf_op | source)
XLA Modules:
  0.0 4161.1 jit_solution(18049477034003341013)
XLA Ops:
  35.9 42.6 %all-reduce.24 = (bf16[1024]{0:T(1024)(128)(2,1)S(1)}, bf16[1024]{0:T(1024)(128)(2,1)S(1)}, bf16[1024]{0:T(1024)(128)(2,1)S(1)}, bf16[1024]{0:T(1024)(128)(2,1)S...) all-reduce(bf16[1024]{0:T(1024)(128)(2,1)S(1)} %dynamic-update-slic, ...), channel_id=1, replica_groups=mesh['dp'=8,'seq'=4] {'dp','seq'}, use_global_device_ids=true, to_apply=%add | all-reduce | flops 19456 | bytes 77824
  158.7 46.1 %reshape.4079 = bf16[16,64,128,64]{3,2,1,0:T(8,128)(2,1)} reshape(bf16[1024,8192]{1,0:T(8,128)(2,1)} %all-gather.40.cloned.1.call-done) | data formatting | bytes 33554432 | tf_op jit(solution)/shard_map/reshape | solution.py:246
  204.7 18.6 fusion.670
  223.4 8.0 fusion.146
  249.8 4.0 fusion.275
  256.9 3.8 fusion.62
  266.8 63.0 %all-gather.8 = bf16[1,4096]{1,0:T(2,128)(2,1)S(1)} all-gather(bf16[1,128]{1,0:T(2,128)(2,1)S(1)} %get-tuple-element.508), channel_id=10, replica_groups=mesh['dp'=8,'seq'=4] {'dp','seq'}, dimensions={1}, use_global_device_ids=true | all-gather | bytes 8448 | tf_op jit(solution)/shard_map/all_gather | solution.py:278
  338.6 38.2 all-gather.52.cloned.1.call-done
  379.2 78.3 %all-gather.54.cloned.1.call-done = bf16[1,1024,4096]{2,1,0:T(8,128)(2,1)} async-done(((bf16[1,32,4096]{2,1,0:T(8,128)(2,1)}), bf16[1,1024,4096]{2,1,0:T(8,128)(2,1)}) %all-gather.54.cloned.1.call-update) | async-done | bytes 8388624 | tf_op jit(solution)/shard_map/all_gather | solution.py:277
  457.5 6.1 fusion.24
  463.6 73.4 %all-gather.56.cloned.1.call-done = bf16[1,4096,1024]{2,1,0:T(8,128)(2,1)} async-done(((bf16[1,128,1024]{2,1,0:T(8,128)(2,1)}), bf16[1,4096,1024]{2,1,0:T(8,128)(2,1)}) %all-gather.56.cloned.1.call-update) | async-done | bytes 8388624 | tf_op jit(solution)/shard_map/all_gather | solution.py:279
  537.1 9.5 fusion.681
  547.4 60.6 %all-gather.58.cloned.1.call-done = bf16[1,1024,3072]{2,1,0:T(8,128)(2,1)} async-done(((bf16[1,32,3072]{2,1,0:T(8,128)(2,1)}), bf16[1,1024,3072]{2,1,0:T(8,128)(2,1)}) %all-gather.58.cloned.1.call-update) | async-done | bytes 6291472 | tf_op jit(solution)/shard_map/all_gather | solution.py:270
  608.0 3.8 fusion.65
  617.9 62.9 %all-gather.21 = bf16[1,4096]{1,0:T(2,128)(2,1)S(1)} all-gather(bf16[1,128]{1,0:T(2,128)(2,1)S(1)} %get-tuple-element.507), channel_id=23, replica_groups=mesh['dp'=8,'seq'=4] {'dp','seq'}, dimensions={1}, use_global_device_ids=true | all-gather | bytes 8448 | tf_op jit(solution)/shard_map/all_gather | solution.py:278
  681.5 66.1 %all_gather.154 = bf16[1024,32]{1,0:T(8,128)(2,1)S(1)} all-gather(bf16[32,32]{1,0:T(8,128)(2,1)S(1)} %copy-done.238), channel_id=1, replica_groups=mesh['dp'=8,'seq'=4] {'dp','seq'}, dimensions={0}, use_global_device_ids=true | all-gather | bytes 67584 | tf_op jit(solution)/shard_map/all_gather | solution.py:244
  759.4 49.3 %all-gather.62.cloned.1.call-done = bf16[1,1024,4096]{2,1,0:T(8,128)(2,1)} async-done(((bf16[1,32,4096]{2,1,0:T(8,128)(2,1)}), bf16[1,1024,4096]{2,1,0:T(8,128)(2,1)}) %all-gather.62.cloned.1.call-update) | async-done | bytes 8388624 | tf_op jit(solution)/shard_map/all_gather | solution.py:277
  808.6 6.1 fusion.27
  814.7 73.4 %all-gather.64.cloned.1.call-done = bf16[1,4096,1024]{2,1,0:T(8,128)(2,1)} async-done(((bf16[1,128,1024]{2,1,0:T(8,128)(2,1)}), bf16[1,4096,1024]{2,1,0:T(8,128)(2,1)}) %all-gather.64.cloned.1.call-update) | async-done | bytes 8388624 | tf_op jit(solution)/shard_map/all_gather | solution.py:279
  888.1 9.7 fusion.683
  900.7 8.5 convert_reduce_fusion
  916.7 4.3 fusion.140
  921.0 6.0 copy.925
  930.0 4.3 multiply_reduce_fusion.1
  938.2 6.1 copy.923
  950.5 4.5 reduce-scatter.27.cloned.1.call-done
  956.9 26.8 reduce-scatter.25.cloned.1.call-done
  985.4 6.0 multiply_reduce_fusion.3
  992.4 10.2 convert_reduce_fusion.1
  1009.2 4.3 fusion.143
  1013.5 6.1 copy.929
  1023.0 4.0 multiply_reduce_fusion
  1030.0 3.9 copy.927
  1037.0 11.1 fusion.625
  1048.1 20.4 reshape.4106
  1077.4 3.8 fusion.622
  1081.2 8.3 fusion.660
  1090.7 7.6 fusion.360
  1098.3 60.0 %concatenate.359 = f32[1024,12300]{1,0:T(8,128)} concatenate(f32[1024,3072]{1,0:T(8,128)} %fusion.360, f32[1024,1024]{1,0:T(8,128)} %fusion.622, f32[1024,4096]{1,0:T(8,128)} %fusion.660, f32[1024,4096]{1,0:T(8,128)} %reshape.4106, f32[1024,1]{1,0:T(8,128)S(1)} %copy-done.72, f32[1024,1]{1,0:T(8,128)} %copy.905, f32[1024,1]{1,0:T(8,128)S(1)} %copy-done.73, ...), dimensions={1} | concatenate | bytes 100761600 | tf_op jit(solution)/shard_map/concatenate | solution.py:454
  1159.9 9.8 fusion.619
  1169.8 20.6 reshape.4104
  1203.2 8.3 fusion.655
  1216.2 7.5 fusion.359
  1223.7 60.1 %concatenate.358 = f32[1024,12300]{1,0:T(8,128)} concatenate(f32[1024,3072]{1,0:T(8,128)} %fusion.359, f32[1024,1024]{1,0:T(8,128)} %fusion.616, f32[1024,4096]{1,0:T(8,128)} %fusion.655, f32[1024,4096]{1,0:T(8,128)} %reshape.4104, f32[1024,1]{1,0:T(8,128)S(1)} %stack.2207, f32[1024,1]{1,0:T(8,128)} %copy.896, f32[1024,1]{1,0:T(8,128)S(1)} %copy.897, f32[1024,1]{1,0:T(8,128)S(1)} %copy-done.70, ...), dimensions={1} | concatenate | bytes 100761600 | tf_op jit(solution)/shard_map/concatenate | solution.py:454
  1286.4 5.1 multiply_reduce_fusion.5
  1292.8 9.7 convolution_dynamic-update-slice_fusion.7
  1302.6 7.4 convolution_dynamic-update-slice_fusion.6
  1309.9 7.5 convolution_dynamic-update-slice_fusion.5
  1317.4 7.5 convolution_dynamic-update-slice_fusion.4
  1325.0 7.3 convolution_dynamic-update-slice_fusion.3
  1332.3 7.3 convolution_dynamic-update-slice_fusion.2
  1339.7 7.6 convolution_dynamic-update-slice_fusion.1
  1347.2 9.5 convolution_dynamic-update-slice_fusion
  1356.7 56.3 %copy.893 = f32[16,64,128,64]{3,2,1,0:T(8,128)} copy(f32[16,64,128,64]{3,1,2,0:T(8,128)} %convolution_dynamic-update-slice_fusion) | data formatting | bytes 67108864 | tf_op jit(solution)/shard_map/concatenate | solution.py:123
  1413.0 55.0 %reshape.4103 = f32[1024,8192]{1,0:T(8,128)} reshape(f32[16,64,128,64]{3,2,1,0:T(8,128)} %copy.893) | data formatting | bytes 67108864 | tf_op jit(solution)/shard_map/reshape | solution.py:123
  1485.1 3.9 collective-permute-start.3
  1489.0 43.1 %all-reduce.23 = (f32[1024]{0:T(1024)S(1)}, f32[1024]{0:T(1024)S(1)}, f32[1024]{0:T(1024)S(1)}, f32[1024]{0:T(1024)S(1)}) all-reduce(f32[1024]{0:T(1024)S(1)} %get-tuple-element.82, f32[1024]{0:T(1024)S(1)} %get-tuple-element.45, f32[1024]{0:T(1024)S(1)} %get-tuple-element.50, ...), channel_id=33, replica_groups=mesh['dp'=8,'seq'=4] {'dp','seq'}, use_global_device_ids=true, to_apply=%region_35.36.clone | all-reduce | flops 4096 | bytes 32768
  1786.0 4.2 copy-done.227
  1799.0 3.8 fusion.200
  1805.9 3.9 fusion.265
  1824.8 408.4 %reduce-scatter.21.cloned.1.call-done = f32[32,12300]{1,0:T(8,128)} async-done(((f32[1024,12300]{1,0:T(8,128)}), f32[32,12300]{1,0:T(8,128)}) %reduce-scatter.21.cloned.1.call-update) | async-done | bytes 1574416 | tf_op jit(solution)/shard_map/reduce_scatter | solution.py:459
  2239.1 1067.4 %reduce-scatter.19.cloned.1.call-done = f32[32,12300]{1,0:T(8,128)} async-done(((f32[1024,12300]{1,0:T(8,128)}), f32[32,12300]{1,0:T(8,128)}) %reduce-scatter.19.cloned.1.call-update) | async-done | bytes 1574416 | tf_op jit(solution)/shard_map/reduce_scatter | solution.py:459
  3318.9 121.0 %reduce-scatter.23.cloned.1.call-done = f32[32,32]{1,0:T(8,128)} async-done(((f32[1024,32]{1,0:T(8,128)}), f32[32,32]{1,0:T(8,128)}) %reduce-scatter.23.cloned.1.call-update) | async-done | bytes 4112 | tf_op jit(solution)/shard_map/reduce_scatter | solution.py:508
  3439.9 714.0 %reduce-scatter.17.cloned.1.call-done = f32[32,8192]{1,0:T(8,128)} async-done(((f32[1024,8192]{1,0:T(8,128)}), f32[32,8192]{1,0:T(8,128)}) %reduce-scatter.17.cloned.1.call-update) | async-done | bytes 1048592 | tf_op jit(solution)/shard_map/reduce_scatter | solution.py:504
  (1458 shorter events, 554.6 us)
Async XLA Ops:
  7.2 151.5 %all-gather.40.cloned.1.call-start = ((), (), s32[]{:S(2)}) async-start(), calls=%async_computation.8 | async-start | bytes 17301504 | tf_op jit(solution)/shard_map/all_gather | solution.py:240
  7.9 248.4 %all-gather.50.cloned.1.call-start = ((), (), s32[]{:S(2)}) async-start(), calls=%async_computation.17 | async-start | bytes 6488064 | tf_op jit(solution)/shard_map/all_gather | solution.py:270
  9.9 82.3 %collective-permute-start = (bf16[1,64,1024]{1,2,0:T(8,128)(2,1)S(1)}, bf16[1,64,1024]{1,2,0:T(8,128)(2,1)S(1)}, u32[]{:S(2)}, u32[]{:S(2)}) collective-permute-start(bf16[1,64,1024]{1,2,0:T(8,128)(2,1)S(1)} %get-tuple-element.375), channel_id=1, source_target_pairs={{0,1},{1,2},{2,3},{4,5},{5,6},{6,7},{8,9},{9,10},{10,11},{12,13},{... | collective-permute-start | bytes 393224 | tf_op jit(solution)/shard_map/ppermute | solution.py:24
  13.4 86.7 %collective-permute-start.1 = (bf16[1,64,1024]{1,2,0:T(8,128)(2,1)}, bf16[1,64,1024]{1,2,0:T(8,128)(2,1)S(1)}, u32[]{:S(2)}, u32[]{:S(2)}) collective-permute-start(bf16[1,64,1024]{1,2,0:T(8,128)(2,1)} %get-tuple-element.374), channel_id=1, source_target_pairs={{1,0},{2,1},{3,2},{5,4},{6,5},{7,6},{9,8},{10,9},{11,10},{13,12},{... | collective-permute-start | bytes 393224 | tf_op jit(solution)/shard_map/ppermute | solution.py:26
  17.6 312.8 %all-gather.42.cloned.1.call-start = ((), (), s32[]{:S(2)}) async-start(), calls=%async_computation.9 | async-start | bytes 1310720 | tf_op jit(solution)/shard_map/all_gather | solution.py:293
  19.2 77.9 %copy-start.285 = (pred[1,128,1]{1,2,0:T(4,128)(4,1)}, pred[1,128,1]{1,2,0:T(4,128)(4,1)S(1)}, u32[]{:S(2)}) copy-start(pred[1,128,1]{1,2,0:T(4,128)(4,1)S(1)} %get-tuple-element.504) | copy-start | bytes 388
  19.2 77.9 %copy-start.287 = (pred[1,128,1]{1,2,0:T(4,128)(4,1)}, pred[1,128,1]{1,2,0:T(4,128)(4,1)S(1)}, u32[]{:S(2)}) copy-start(pred[1,128,1]{1,2,0:T(4,128)(4,1)S(1)} %get-tuple-element.505) | copy-start | bytes 388
  19.7 77.4 %copy-start.255 = (pred[1,128,1]{1,2,0:T(4,128)(4,1)}, pred[1,128,1]{1,2,0:T(4,128)(4,1)S(1)}, u32[]{:S(2)}) copy-start(pred[1,128,1]{1,2,0:T(4,128)(4,1)S(1)} %get-tuple-element.380) | copy-start | bytes 388
  19.7 77.4 %copy-start.257 = (pred[1,128,1]{1,2,0:T(4,128)(4,1)}, pred[1,128,1]{1,2,0:T(4,128)(4,1)S(1)}, u32[]{:S(2)}) copy-start(pred[1,128,1]{1,2,0:T(4,128)(4,1)S(1)} %get-tuple-element.381) | copy-start | bytes 388
  19.7 77.4 %copy-start.259 = (pred[1,128,1]{1,2,0:T(4,128)(4,1)}, pred[1,128,1]{1,2,0:T(4,128)(4,1)S(1)}, u32[]{:S(2)}) copy-start(pred[1,128,1]{1,2,0:T(4,128)(4,1)S(1)} %get-tuple-element.382) | copy-start | bytes 388
  19.7 77.4 %copy-start.261 = (pred[1,128,1]{1,2,0:T(4,128)(4,1)}, pred[1,128,1]{1,2,0:T(4,128)(4,1)S(1)}, u32[]{:S(2)}) copy-start(pred[1,128,1]{1,2,0:T(4,128)(4,1)S(1)} %get-tuple-element.383) | copy-start | bytes 388
  19.8 77.4 %copy-start.263 = (pred[1,128,1]{1,2,0:T(4,128)(4,1)}, pred[1,128,1]{1,2,0:T(4,128)(4,1)S(1)}, u32[]{:S(2)}) copy-start(pred[1,128,1]{1,2,0:T(4,128)(4,1)S(1)} %get-tuple-element.384) | copy-start | bytes 388
  19.8 77.4 %copy-start.265 = (pred[1,128,1]{1,2,0:T(4,128)(4,1)}, pred[1,128,1]{1,2,0:T(4,128)(4,1)S(1)}, u32[]{:S(2)}) copy-start(pred[1,128,1]{1,2,0:T(4,128)(4,1)S(1)} %get-tuple-element.385) | copy-start | bytes 388
  19.8 77.4 %copy-start.267 = (pred[1,128,1]{1,2,0:T(4,128)(4,1)}, pred[1,128,1]{1,2,0:T(4,128)(4,1)S(1)}, u32[]{:S(2)}) copy-start(pred[1,128,1]{1,2,0:T(4,128)(4,1)S(1)} %get-tuple-element.386) | copy-start | bytes 388
  19.8 77.4 %copy-start.269 = (pred[1,128,1]{1,2,0:T(4,128)(4,1)}, pred[1,128,1]{1,2,0:T(4,128)(4,1)S(1)}, u32[]{:S(2)}) copy-start(pred[1,128,1]{1,2,0:T(4,128)(4,1)S(1)} %get-tuple-element.387) | copy-start | bytes 388
  19.8 77.4 %copy-start.271 = (pred[1,128,1]{1,2,0:T(4,128)(4,1)}, pred[1,128,1]{1,2,0:T(4,128)(4,1)S(1)}, u32[]{:S(2)}) copy-start(pred[1,128,1]{1,2,0:T(4,128)(4,1)S(1)} %get-tuple-element.388) | copy-start | bytes 388
  19.8 77.4 %copy-start.273 = (pred[1,128,1]{1,2,0:T(4,128)(4,1)}, pred[1,128,1]{1,2,0:T(4,128)(4,1)S(1)}, u32[]{:S(2)}) copy-start(pred[1,128,1]{1,2,0:T(4,128)(4,1)S(1)} %get-tuple-element.389) | copy-start | bytes 388
  19.8 77.4 %copy-start.275 = (pred[1,128,1]{1,2,0:T(4,128)(4,1)}, pred[1,128,1]{1,2,0:T(4,128)(4,1)S(1)}, u32[]{:S(2)}) copy-start(pred[1,128,1]{1,2,0:T(4,128)(4,1)S(1)} %get-tuple-element.390) | copy-start | bytes 388
  19.8 77.4 %copy-start.277 = (pred[1,128,1]{1,2,0:T(4,128)(4,1)}, pred[1,128,1]{1,2,0:T(4,128)(4,1)S(1)}, u32[]{:S(2)}) copy-start(pred[1,128,1]{1,2,0:T(4,128)(4,1)S(1)} %get-tuple-element.391) | copy-start | bytes 388
  19.8 77.4 %copy-start.279 = (pred[1,128,1]{1,2,0:T(4,128)(4,1)}, pred[1,128,1]{1,2,0:T(4,128)(4,1)S(1)}, u32[]{:S(2)}) copy-start(pred[1,128,1]{1,2,0:T(4,128)(4,1)S(1)} %get-tuple-element.392) | copy-start | bytes 388
  19.8 77.4 %copy-start.281 = (pred[1,128,1]{1,2,0:T(4,128)(4,1)}, pred[1,128,1]{1,2,0:T(4,128)(4,1)S(1)}, u32[]{:S(2)}) copy-start(pred[1,128,1]{1,2,0:T(4,128)(4,1)S(1)} %get-tuple-element.393) | copy-start | bytes 388
  19.9 77.4 %copy-start.283 = (pred[1,128,1]{1,2,0:T(4,128)(4,1)}, pred[1,128,1]{1,2,0:T(4,128)(4,1)S(1)}, u32[]{:S(2)}) copy-start(pred[1,128,1]{1,2,0:T(4,128)(4,1)S(1)} %get-tuple-element.394) | copy-start | bytes 388
  19.9 77.4 %copy-start.289 = (pred[1,128,1]{1,2,0:T(4,128)(4,1)}, pred[1,128,1]{1,2,0:T(4,128)(4,1)S(1)}, u32[]{:S(2)}) copy-start(pred[1,128,1]{1,2,0:T(4,128)(4,1)S(1)} %get-tuple-element.395) | copy-start | bytes 388
  78.5 175.6 %copy-start.213 = (f32[1024]{0:T(1024)}, f32[1024]{0:T(1024)S(1)}, u32[]{:S(2)}) copy-start(f32[1024]{0:T(1024)S(1)} %convert_element_type.476) | copy-start | bytes 12292
  78.5 298.3 %copy-start.203 = (f32[1024]{0:T(1024)}, f32[1024]{0:T(1024)S(1)}, u32[]{:S(2)}) copy-start(f32[1024]{0:T(1024)S(1)} %convert_element_type.478) | copy-start | bytes 12292
  78.5 298.3 %copy-start.201 = (f32[1024]{0:T(1024)}, f32[1024]{0:T(1024)S(1)}, u32[]{:S(2)}) copy-start(f32[1024]{0:T(1024)S(1)} %convert_element_type.477) | copy-start | bytes 12292
  87.8 155.1 %copy-start.245 = (pred[1,128,16]{1,2,0:T(8,128)(4,1)}, pred[1,128,16]{1,2,0:T(8,128)(4,1)S(1)}, u32[]{:S(2)}) copy-start(pred[1,128,16]{1,2,0:T(8,128)(4,1)S(1)} %stack.1907) | copy-start | bytes 6148
  89.3 155.8 %copy-start.243 = (pred[1,128,16]{1,2,0:T(8,128)(4,1)}, pred[1,128,16]{1,2,0:T(8,128)(4,1)S(1)}, u32[]{:S(2)}) copy-start(pred[1,128,16]{1,2,0:T(8,128)(4,1)S(1)} %stack.1941) | copy-start | bytes 6148
  90.7 156.5 %copy-start.241 = (pred[1,128,16]{1,2,0:T(8,128)(4,1)}, pred[1,128,16]{1,2,0:T(8,128)(4,1)S(1)}, u32[]{:S(2)}) copy-start(pred[1,128,16]{1,2,0:T(8,128)(4,1)S(1)} %stack.1975) | copy-start | bytes 6148
  92.1 157.7 %copy-start.239 = (pred[1,128,16]{1,2,0:T(8,128)(4,1)}, pred[1,128,16]{1,2,0:T(8,128)(4,1)S(1)}, u32[]{:S(2)}) copy-start(pred[1,128,16]{1,2,0:T(8,128)(4,1)S(1)} %stack.2009) | copy-start | bytes 6148
  256.1 120.8 %copy-start.4 = (f32[1,128,1024]{2,1,0:T(8,128)}, f32[1,128,1024]{2,1,0:T(8,128)S(1)}, u32[]{:S(2)}) copy-start(f32[1,128,1024]{2,1,0:T(8,128)S(1)} %get-tuple-element.95) | copy-start | bytes 1572868
  256.1 120.8 %copy-start.215 = (f32[128]{0:T(128)}, f32[128]{0:T(128)S(1)}, u32[]{:S(2)}) copy-start(f32[128]{0:T(128)S(1)} %broadcast_multiply_fusion.4) | copy-start | bytes 1540
  256.3 120.5 %copy-start.217 = (f32[128]{0:T(128)}, f32[128]{0:T(128)S(1)}, u32[]{:S(2)}) copy-start(f32[128]{0:T(128)S(1)} %fusion.632) | copy-start | bytes 1540
  261.7 70.3 %all-gather.44.cloned.1.call-start = ((), (), s32[]{:S(2)}) async-start(), calls=%async_computation.10 | async-start | bytes 1310720 | tf_op jit(solution)/shard_map/all_gather | solution.py:292
  262.5 114.3 %all-gather.52.cloned.1.call-start = ((), (), s32[]{:S(2)}) async-start(), calls=%async_computation.18 | async-start | bytes 2162688 | tf_op jit(solution)/shard_map/all_gather | solution.py:273
  264.1 193.4 %all-gather.54.cloned.1.call-start = ((), (), s32[]{:S(2)}) async-start(), calls=%async_computation.19 | async-start | bytes 8650752 | tf_op jit(solution)/shard_map/all_gather | solution.py:277
  265.0 272.0 %all-gather.56.cloned.1.call-start = ((), (), s32[]{:S(2)}) async-start(), calls=%async_computation.20 | async-start | bytes 8650752 | tf_op jit(solution)/shard_map/all_gather | solution.py:279
  265.9 342.1 %all-gather.58.cloned.1.call-start = ((), (), s32[]{:S(2)}) async-start(), calls=%async_computation.21 | async-start | bytes 6488064 | tf_op jit(solution)/shard_map/all_gather | solution.py:270
  266.7 481.2 %all-gather.46.cloned.1.call-start = ((), (), s32[]{:S(2)}) async-start(), calls=%async_computation.11 | async-start | bytes 1310720 | tf_op jit(solution)/shard_map/all_gather | solution.py:293
  329.8 207.3 %copy-start.205 = (f32[1024]{0:T(1024)}, f32[1024]{0:T(1024)S(1)}, u32[]{:S(2)}) copy-start(f32[1024]{0:T(1024)S(1)} %convert_element_type.593) | copy-start | bytes 12292
  338.6 125.0 %copy-start.187 = (bf16[16,64,128]{2,1,0:T(8,128)(2,1)}, bf16[16,64,128]{2,1,0:T(8,128)(2,1)S(1)}, u32[]{:S(2)}) copy-start(bf16[16,64,128]{2,1,0:T(8,128)(2,1)S(1)} %fusion.327) | copy-start | bytes 786436
  379.2 84.4 %copy-start.350 = (f32[128]{0:T(128)}, f32[128]{0:T(128)S(1)}, u32[]{:S(2)}) copy-start(f32[128]{0:T(128)S(1)} %multiply_reduce_fusion.13) | copy-start | bytes 1540
  547.4 133.4 %copy-start.332 = (bf16[1024]{0:T(1024)(128)(2,1)S(1)}, bf16[1024]{0:T(1024)(128)(2,1)}, u32[]{:S(2)}) copy-start(bf16[1024]{0:T(1024)(128)(2,1)} %get-tuple-element.68) | copy-start | bytes 6148
  547.4 133.4 %copy-start.331 = (bf16[1024]{0:T(1024)(128)(2,1)S(1)}, bf16[1024]{0:T(1024)(128)(2,1)}, u32[]{:S(2)}) copy-start(bf16[1024]{0:T(1024)(128)(2,1)} %get-tuple-element.70) | copy-start | bytes 6148
  547.4 133.5 %copy-start.330 = (bf16[1024]{0:T(1024)(128)(2,1)S(1)}, bf16[1024]{0:T(1024)(128)(2,1)}, u32[]{:S(2)}) copy-start(bf16[1024]{0:T(1024)(128)(2,1)} %get-tuple-element.71) | copy-start | bytes 6148
  547.4 133.5 %copy-start.329 = (bf16[1024]{0:T(1024)(128)(2,1)S(1)}, bf16[1024]{0:T(1024)(128)(2,1)}, u32[]{:S(2)}) copy-start(bf16[1024]{0:T(1024)(128)(2,1)} %get-tuple-element.73) | copy-start | bytes 6148
  547.4 133.5 %copy-start.328 = (bf16[1024]{0:T(1024)(128)(2,1)S(1)}, bf16[1024]{0:T(1024)(128)(2,1)}, u32[]{:S(2)}) copy-start(bf16[1024]{0:T(1024)(128)(2,1)} %get-tuple-element.72) | copy-start | bytes 6148
  547.4 134.1 %copy-start.238 = (bf16[32,32]{1,0:T(8,128)(2,1)S(1)}, bf16[32,32]{1,0:T(8,128)(2,1)}, u32[]{:S(2)}) copy-start(bf16[32,32]{1,0:T(8,128)(2,1)} %param.41) | copy-start | bytes 6148
  613.9 136.5 %all-gather.48.cloned.1.call-start = ((), (), s32[]{:S(2)}) async-start(), calls=%async_computation.12 | async-start | bytes 1310720 | tf_op jit(solution)/shard_map/all_gather | solution.py:292
  615.7 140.6 %all-gather.60.cloned.1.call-start = ((), (), s32[]{:S(2)}) async-start(), calls=%async_computation.22 | async-start | bytes 2162688 | tf_op jit(solution)/shard_map/all_gather | solution.py:273
  616.5 192.2 %all-gather.62.cloned.1.call-start = ((), (), s32[]{:S(2)}) async-start(), calls=%async_computation.23 | async-start | bytes 8650752 | tf_op jit(solution)/shard_map/all_gather | solution.py:277
  617.0 271.1 %all-gather.64.cloned.1.call-start = ((), (), s32[]{:S(2)}) async-start(), calls=%async_computation.24 | async-start | bytes 8650752 | tf_op jit(solution)/shard_map/all_gather | solution.py:279
  617.8 337.2 %reduce-scatter.27.cloned.1.call-start = ((), (), s32[]{:S(2)}) async-start(), calls=%async_computation.26 | async-start | bytes 1310720
  747.6 150.4 %copy-start.64 = (bf16[1024,32]{1,0:T(8,128)(2,1)}, bf16[1024,32]{1,0:T(8,128)(2,1)S(1)}, u32[]{:S(2)}) copy-start(bf16[1024,32]{1,0:T(8,128)(2,1)S(1)} %all_gather.154) | copy-start | bytes 196612
  814.7 83.3 %copy-start.211 = (bf16[1,128,32]{1,2,0:T(8,128)(2,1)S(1)}, bf16[1,128,32]{1,2,0:T(8,128)(2,1)}, u32[]{:S(2)}) copy-start(bf16[1,128,32]{1,2,0:T(8,128)(2,1)} %param.43) | copy-start | bytes 24580
  930.0 53.7 %reduce-scatter.25.cloned.1.call-start = ((), (), s32[]{:S(2)}) async-start(), calls=%async_computation.25 | async-start | bytes 1310720
  947.3 264.3 %reduce-scatter.31.cloned.1.call-start = ((), (), s32[]{:S(2)}) async-start(), calls=%async_computation.28 | async-start | bytes 1310720
  1022.6 190.7 %reduce-scatter.29.cloned.1.call-start = ((), (), s32[]{:S(2)}) async-start(), calls=%async_computation.27 | async-start | bytes 1310720
  1036.9 1196.3 %reduce-scatter.21.cloned.1.call-start = ((), (), s32[]{:S(2)}) async-start(), calls=%async_computation.15 | async-start | bytes 52445184 | tf_op jit(solution)/shard_map/reduce_scatter | solution.py:459
  1158.4 2148.1 %reduce-scatter.19.cloned.1.call-start = ((), (), s32[]{:S(2)}) async-start(), calls=%async_computation.14 | async-start | bytes 52445184 | tf_op jit(solution)/shard_map/reduce_scatter | solution.py:459
  1283.8 2156.1 %reduce-scatter.23.cloned.1.call-start = ((), (), s32[]{:S(2)}) async-start(), calls=%async_computation.16 | async-start | bytes 540672 | tf_op jit(solution)/shard_map/reduce_scatter | solution.py:508
  1285.9 2868.1 %reduce-scatter.17.cloned.1.call-start = ((), (), s32[]{:S(2)}) async-start(), calls=%async_computation.13 | async-start | bytes 34603008 | tf_op jit(solution)/shard_map/reduce_scatter | solution.py:504
  1482.3 52.8 %collective-permute-start.2 = (bf16[1,64,1024]{2,1,0:T(8,128)(2,1)S(1)}, bf16[1,64,1024]{2,1,0:T(8,128)(2,1)S(1)}, u32[]{:S(2)}, u32[]{:S(2)}) collective-permute-start(bf16[1,64,1024]{2,1,0:T(8,128)(2,1)S(1)} %get-tuple-element.373), channel_id=1, source_target_pairs={{1,0},{2,1},{3,2},{5,4},{6,5},{7,6},{9,8},{10,9},{11,10},{13,12},{... | collective-permute-start | bytes 393224 | tf_op jit(solution)/shard_map/ppermute | solution.py:26
  1485.1 157.1 %collective-permute-start.3 = (bf16[1,64,1024]{2,1,0:T(8,128)(2,1)S(1)}, bf16[1,64,1024]{2,1,0:T(8,128)(2,1)S(1)}, u32[]{:S(2)}, u32[]{:S(2)}) collective-permute-start(bf16[1,64,1024]{2,1,0:T(8,128)(2,1)S(1)} %get-tuple-element.372), channel_id=1, source_target_pairs={{0,1},{1,2},{2,3},{4,5},{5,6},{6,7},{8,9},{9,10},{10,11},{12,13},{... | collective-permute-start | bytes 393224 | tf_op jit(solution)/shard_map/ppermute | solution.py:24
  (325 other events, 3741.9 us)
Sparse Core Ops, SparseCore 0:
  11.0 116.0 all-gather.39
  130.0 68.1 all-gather.49
  261.8 28.2 all-gather.41
  291.6 27.5 all-gather.43
  321.9 54.8 all-gather.51
  380.2 77.3 all-gather.53
  461.0 75.9 all-gather.55
  539.9 68.0 all-gather.57
  614.0 26.6 all-gather.45
  642.1 27.5 all-gather.47
  672.6 55.1 all-gather.59
  730.6 77.9 all-gather.61
  812.1 75.9 all-gather.63
  930.1 24.8 reduce-scatter.26
  957.8 25.7 reduce-scatter.24
  1022.7 25.7 reduce-scatter.30
  1051.3 25.7 reduce-scatter.28
  1158.5 1074.6 reduce-scatter.20
  2235.7 1070.7 reduce-scatter.18
  3309.2 130.7 reduce-scatter.22
  3442.9 711.0 reduce-scatter.16
where the time goes:
time: 4180 us; the launch traced here: 4160 us
  waiting for transfers between devices  2720 us (65%)
  local copies, waits for them, and re-layouts  773 us (18%)
  matrix products  279 us (7%)
  blocking collectives  278 us (7%)
  other arithmetic  78.1 us (2%)
    reduce_scatter x2, waiting for transfers between devices, local(): lax.psum_scatter(layer_term(jnp.int32(0), rows_share * lax.axis_size(('dp...  1480 us
    reduce_scatter x1, waiting for transfers between devices, local(): lax.psum_scatter(kernel_part, ('dp', 'seq'), scatter_dimension=0, tiled=T...  714 us
    slice x127, local copies, waits for them, and re-layouts, unfold(): lax.slice_in_dim(source, anchor, anchor + length, axis=1)  208 us
    unnamed x1035, local copies, waits for them, and re-layouts  150 us
    all_gather x2, waiting for transfers between devices, local(): lax.all_gather(reduce_weight[layer_at], ('dp', 'seq'), axis=0, tiled=True)  147 us
    all_gather x2, waiting for transfers between devices, local(): lax.all_gather(expand_weight[layer_at], ('dp', 'seq'), axis=0, tiled=True)  128 us
    all_gather x2, blocking collectives, local(): lax.all_gather(hidden_bias[layer_at], ('dp', 'seq'), axis=0, tiled=True)  126 us
    reduce_scatter x1, waiting for transfers between devices, local(): lax.psum_scatter(head_part, ('dp', 'seq'), scatter_dimension=0, tiled=True)  121 us
  transfers between devices with their start and end apart: 25, of which 12 were waited for; matrix products, arithmetic and copies ran while one was open for 24% of the time, Pallas kernels for 0%

commit v1 on v0

--- a/solution.py
+++ b/solution.py
@@ -1,8 +1,11 @@
+import functools
 import math
 
 import jax
 import jax.numpy as jnp
 from jax import lax
+from jax.experimental import pallas as pl
+from jax.experimental.pallas import tpu as pltpu
 from jax.sharding import PartitionSpec as P
 
 HEADS = 16
@@ -537,56 +540,1108 @@
     )
 
 
-def solution(mesh):
+MESH_ID = pl.DeviceIdType.MESH
+IN_VMEM = pl.BlockSpec(memory_space=pltpu.VMEM)
+ANYWHERE = pl.BlockSpec(memory_space=pl.ANY)
+AXES = ("a", "t", "z")
+PACK = 8
+RANKS = 4
+
+
+def kernel_params(collective=None):
+    if collective is None:
+        return pltpu.CompilerParams(vmem_limit_bytes=56 * 2**20)
+    return pltpu.CompilerParams(
+        vmem_limit_bytes=56 * 2**20, collective_id=collective, has_side_effects=True
+    )
+
+
+def cost(micros):
+    return pl.CostEstimate(flops=int(micros * 1.1e9), bytes_accessed=2**20, transcendentals=0)
+
+
+def greet(peers):
+    gate = pltpu.get_barrier_semaphore()
+    for peer in peers:
+        pl.semaphore_signal(gate, inc=1, device_id=peer, device_id_type=MESH_ID)
+    pl.semaphore_wait(gate, len(peers))
+
+
+def remote(source, target, send, receive, peer):
+    return pltpu.make_async_remote_copy(
+        source, target, send, receive, device_id=peer, device_id_type=MESH_ID
+    )
+
+
+def swap_all(sizes, collective, payloads, places):
+    a_size, t_size, z_size = sizes
+    total = a_size * t_size * z_size
+    count = len(payloads)
+
+    def kernel(*refs):
+        sources, targets = refs[:count], refs[count : 2 * count]
+        sends, receives, own_sems = refs[2 * count :]
+        a, t, z = (lax.axis_index(axis) for axis in AXES)
+        me = (a * t_size + t) * z_size + z
+        peers = [
+            (lax.rem(a + i, a_size), lax.rem(t + j, t_size), lax.rem(z + k, z_size))
+            for i in range(a_size)
+            for j in range(t_size)
+            for k in range(z_size)
+        ][1:]
+        greet(peers)
+        copies = []
+        for p in range(count):
+            own = pltpu.make_async_copy(
+                sources[p].at[places[p](a, t, z)], targets[p].at[me], own_sems.at[p]
+            )
+            own.start()
+            copies.append(own)
+            for number, peer in enumerate(peers):
+                copy = remote(
+                    sources[p].at[places[p](*peer)],
+                    targets[p].at[me],
+                    sends.at[p, number],
+                    receives.at[p, number],
+                    peer,
+                )
+                copy.start()
+                copies.append(copy)
+        for copy in copies:
+            copy.wait()
+
+    return pl.pallas_call(
+        kernel,
+        out_shape=[
+            jax.ShapeDtypeStruct((total,) + payload.shape[1:], payload.dtype)
+            for payload in payloads
+        ],
+        in_specs=[ANYWHERE] * count,
+        out_specs=[ANYWHERE] * count,
+        scratch_shapes=[
+            pltpu.SemaphoreType.DMA((count, total - 1)),
+            pltpu.SemaphoreType.DMA((count, total - 1)),
+            pltpu.SemaphoreType.DMA((count,)),
+        ],
+        compiler_params=kernel_params(collective),
+        cost_estimate=cost(20),
+    )(*payloads)
+
+
+def rank_lanes(bounds_ref, rows, width):
+    lanes = PACK * width
+    line = lax.broadcasted_iota(jnp.int32, (rows, lanes), 0) // PACK
+    lane = lax.broadcasted_iota(jnp.int32, (rows, lanes), 1) // width
+    frame = line * PACK + lane
+    rank = jnp.zeros((rows, lanes), jnp.int32)
+    for slot in range(bounds_ref.shape[1]):
+        rank = rank + (frame >= bounds_ref[:, slot : slot + 1]).astype(jnp.int32)
+    return rank
+
+
+def spread_ranks(wide, packed, rank, first):
+    rows = packed.shape[0]
+    wide[...] = jnp.zeros_like(wide)
+    for number in range(RANKS):
+        place = pl.ds(first + number * 64, rows)
+        wide[place, :] += jnp.where(rank == number, packed, 0.0)
+
+
+def collect_ranks(summed, rank, rows):
+    result = jnp.zeros((rows, summed.shape[1]), jnp.float32)
+    for number in range(RANKS):
+        result = jnp.where(rank == number, summed[number * 64 : number * 64 + rows, :], result)
+    return result
+
+
+def toeplitz(even, odd, taps, length):
+    total = None
+    for step in range(taps.shape[0]):
+        source = even if step % 2 == 0 else odd
+        part = jnp.dot(
+            source[pl.ds((step - step % 2) * 8, length), :],
+            taps[step],
+            preferred_element_type=jnp.float32,
+        )
+        total = part if total is None else total + part
+    return total
+
+
+def fill_pair(wide, even, odd):
+    length = even.shape[0]
+    even[...] = wide[:length, :].astype(jnp.bfloat16)
+    odd[...] = wide[8 : 8 + length, :].astype(jnp.bfloat16)
+
+
+def conv_forward_packed(packed, bounds, taps, bias):
+    rows = packed.shape[0]
+    length = rows + (RANKS - 1) * 64
+    held = length + 128
+    steps, depth, width = taps.shape
+
+    def kernel(x_ref, b_ref, k_ref, bias_ref, o_ref, even, odd, wide):
+        rank = rank_lanes(b_ref, rows, depth // PACK)
+        spread_ranks(wide, x_ref[...].astype(jnp.float32), rank, 64)
+        fill_pair(wide, even, odd)
+        summed = toeplitz(even, odd, k_ref, length)
+        rank_out = rank_lanes(b_ref, rows, width // PACK)
+        o_ref[...] = (collect_ranks(summed, rank_out, rows) + bias_ref[...]).astype(jnp.bfloat16)
+
+    return pl.pallas_call(
+        kernel,
+        out_shape=[
+            jax.ShapeDtypeStruct((rows, width), jnp.bfloat16),
+            jax.ShapeDtypeStruct((held, depth), jnp.bfloat16),
+            jax.ShapeDtypeStruct((held, depth), jnp.bfloat16),
+        ],
+        in_specs=[IN_VMEM] * 4,
+        out_specs=[IN_VMEM] * 3,
+        scratch_shapes=[pltpu.VMEM((held + 16, depth), jnp.float32)],
+        compiler_params=kernel_params(),
+        cost_estimate=cost(10),
+    )(packed, bounds, taps, bias)
+
+
+def conv_backward_packed(packed, own, bounds, taps, even, odd):
+    rows, depth = packed.shape
+    length = rows + (RANKS - 1) * 64
+    held = length + 128
+    steps, _, width = taps.shape
+    tap_count = (steps - 1) * PACK
+    group_width = depth // PACK
+    chans = width // PACK
+
+    def kernel(g_ref, own_ref, b_ref, k_ref, even_ref, odd_ref, o_ref, w_ref, s_ref, ge, go, wide, turned):
+        rank = rank_lanes(b_ref, rows, depth // PACK)
+        spread_ranks(wide, g_ref[...].astype(jnp.float32), rank, 64)
+        fill_pair(wide, ge, go)
+        summed = toeplitz(ge, go, k_ref, length)
+        rank_out = rank_lanes(b_ref, rows, width // PACK)
+        o_ref[...] = collect_ranks(summed, rank_out, rows).astype(jnp.bfloat16)
+        own_wide = own_ref[...].astype(jnp.float32)
+        s_ref[...] = jnp.sum(own_wide, axis=0, keepdims=True)
+        spread_ranks(wide.at[:length, :width], own_wide, rank_out, 0)
+        across = wide[:length, :width].T.astype(jnp.bfloat16)
+        for step in range(steps):
+            source = even_ref if step % 2 == 0 else odd_ref
+            turned[:, pl.ds(step * depth, depth)] = jnp.dot(
+                across,
+                source[pl.ds((step - step % 2) * 8, length), :],
+                preferred_element_type=jnp.float32,
+            )
+        total = turned[0:chans, 0 : tap_count * group_width]
+        for f in range(1, PACK):
+            total = total + turned[
+                f * chans : (f + 1) * chans,
+                f * group_width : f * group_width + tap_count * group_width,
+            ]
+        w_ref[...] = total
+
+    return pl.pallas_call(
+        kernel,
+        out_shape=[
+            jax.ShapeDtypeStruct((rows, width), jnp.bfloat16),
+            jax.ShapeDtypeStruct((chans, tap_count * group_width), jnp.float32),
+            jax.ShapeDtypeStruct((1, width), jnp.float32),
+        ],
+        in_specs=[IN_VMEM] * 6,
+        out_specs=[IN_VMEM] * 3,
+        scratch_shapes=[
+            pltpu.VMEM((held, depth), jnp.bfloat16),
+            pltpu.VMEM((held, depth), jnp.bfloat16),
+            pltpu.VMEM((held + 16, depth), jnp.float32),
+            pltpu.VMEM((width, steps * depth), jnp.float32),
+        ],
+        compiler_params=kernel_params(),
+        cost_estimate=cost(15),
+    )(packed, own, bounds, taps, even, odd)
+
+
+def shifted_taps(grid):
+    taps, depth, width = grid.shape
+    steps = 17
+    room = steps * PACK
+    parts = [
+        jnp.pad(grid, ((f, room - taps - f), (0, 0), (0, 0))).reshape(room * depth, width)
+        for f in range(PACK)
+    ]
+    return jnp.concatenate(parts, axis=1).reshape(steps, PACK * depth, PACK * width)
+
+
+def normed(tensor, gain, shift):
+    average = jnp.mean(tensor, axis=-1, keepdims=True)
+    centred = tensor - average
+    spread = jnp.mean(centred * centred, axis=-1, keepdims=True)
+    return centred * lax.rsqrt(spread + epsilon) * gain + shift
+
+
+def normed_back(tensor, gain, upstream):
+    average = jnp.mean(tensor, axis=-1, keepdims=True)
+    centred = tensor - average
+    spread = jnp.mean(centred * centred, axis=-1, keepdims=True)
+    inverse = lax.rsqrt(spread + epsilon)
+    unit = centred * inverse
+    scaled = upstream * gain
+    result = inverse * (
+        scaled
+        - jnp.mean(scaled, axis=-1, keepdims=True)
+        - unit * jnp.mean(scaled * unit, axis=-1, keepdims=True)
+    )
+    return (
+        result,
+        jnp.sum(upstream * unit, axis=0, keepdims=True),
+        jnp.sum(upstream, axis=0, keepdims=True),
+    )
+
+
+def gelu_pair(tensor):
+    half = 0.5 * (1.0 + lax.erf(tensor * (2.0**-0.5)))
+    slope = half + tensor * (jnp.exp(-0.5 * tensor * tensor) * ((2.0 * math.pi) ** -0.5))
+    return tensor * half, slope
+
+
+def dot(left, right):
+    return jnp.dot(left, right, preferred_element_type=jnp.float32)
+
+
+def dot_rt(left, right):
+    return lax.dot_general(left, right, (((1,), (1,)), ((), ())), preferred_element_type=jnp.float32)
+
+
+def dot_lt(left, right):
+    return lax.dot_general(left, right, (((0,), (0,)), ((), ())), preferred_element_type=jnp.float32)
+
+
+def group_gather(block, t, sends, receives):
+    x_peer, c_peer = lax.bitwise_xor(t, 2), lax.bitwise_xor(t, 1)
+    own = block.at[t]
+    across = remote(own, own, sends.at[0], receives.at[0], {"t": x_peer})
+    across.start()
+    beside = remote(own, own, sends.at[1], receives.at[1], {"t": c_peer})
+    beside.start()
+    across.wait_recv()
+    other = block.at[x_peer]
+    onward = remote(other, other, sends.at[2], receives.at[2], {"t": c_peer})
+    onward.start()
+    beside.wait_recv()
+    onward.wait_recv()
+    across.wait_send()
+    beside.wait_send()
+    onward.wait_send()
+
+
+def group_scatter(part, t, send_low, got_low, sends, receives, between=None):
+    x_peer, c_peer = lax.bitwise_xor(t, 2), lax.bitwise_xor(t, 1)
+    send_low[1] = part(lax.bitwise_xor(t, 3)).astype(jnp.bfloat16)
+    first = remote(send_low.at[1], got_low.at[1], sends.at[1], receives.at[1], {"t": c_peer})
+    first.start()
+    send_low[0] = part(c_peer).astype(jnp.bfloat16)
+    second = remote(send_low.at[0], got_low.at[0], sends.at[0], receives.at[0], {"t": c_peer})
+    second.start()
+    total = part(x_peer)
+    first.wait_recv()
+    send_low[2] = (total + got_low[1].astype(jnp.float32)).astype(jnp.bfloat16)
+    third = remote(send_low.at[2], got_low.at[2], sends.at[2], receives.at[2], {"t": x_peer})
+    third.start()
+    own = part(t)
+    if between is not None:
+        between()
+    second.wait_recv()
+    own = own + got_low[0].astype(jnp.float32)
+    third.wait_recv()
+    own = own + got_low[2].astype(jnp.float32)
+    first.wait_send()
+    second.wait_send()
+    third.wait_send()
+    return own
+
+
+def scatter_scratch(n, width):
+    return [
+        pltpu.VMEM((3, n, width), jnp.bfloat16),
+        pltpu.VMEM((3, n, width), jnp.bfloat16),
+        pltpu.SemaphoreType.DMA((3,)),
+        pltpu.SemaphoreType.DMA((3,)),
+        pltpu.SemaphoreType.DMA((3,)),
+        pltpu.SemaphoreType.DMA((3,)),
+    ]
+
+
+def load_rows(pieces, target, sem, sizes, share, column, width):
+    a_size, t_size, z_size = sizes
+    a, z = lax.axis_index("a"), lax.axis_index("z")
+    for number, piece in enumerate(pieces):
+        a_at = lax.bitwise_xor(a, number // z_size)
+        z_at = lax.bitwise_xor(z, number % z_size)
+        for t_at in range(t_size):
+            row = pl.multiple_of(((a_at * t_size + t_at) * z_size + z_at) * share, share)
+            pltpu.make_async_copy(
+                piece.at[pl.ds(t_at * share, share), pl.ds(column, width)],
+                target.at[pl.ds(row, share), :],
+                sem,
+            ).start()
+
+
+def load_chunks(pieces, target, sem, sizes, share, column, width):
+    a_size, t_size, z_size = sizes
+    a, z = lax.axis_index("a"), lax.axis_index("z")
+    for number, piece in enumerate(pieces):
+        a_at = lax.bitwise_xor(a, number // z_size)
+        z_at = lax.bitwise_xor(z, number % z_size)
+        row = pl.multiple_of((a_at * z_size + z_at) * share, share)
+        for chunk in range(t_size):
+            pltpu.make_async_copy(
+                piece.at[pl.ds(chunk * share, share), pl.ds(column, width)],
+                target.at[pl.ds(row, share), pl.ds(chunk * width, width)],
+                sem,
+            ).start()
+
+
+def load_blocks(pieces, target, sem, sizes, first, share):
+    a_size, t_size, z_size = sizes
+    a, z = lax.axis_index("a"), lax.axis_index("z")
+    for number, piece in enumerate(pieces):
+        a_at = lax.bitwise_xor(a, number // z_size)
+        z_at = lax.bitwise_xor(z, number % z_size)
+        row = pl.multiple_of((a_at * z_size + z_at) * share, share)
+        pltpu.make_async_copy(
+            piece.at[pl.ds(first, share), :], target.at[pl.ds(row, share), :], sem
+        ).start()
+
+
+def settle(target, sem):
+    pltpu.make_async_copy(target, target, sem).wait()
+
+
+def attention_forward(hidden, seg_col, seg_row, query_bias, value_bias, attend_bias, gain, shift, pieces, sizes, collective):
+    n, width = hidden.shape
+    a_size, t_size, z_size = sizes
+    count = t_size * n
+    part = width // t_size
+    head = width // HEADS
+    share = width // (a_size * t_size * z_size)
+    scale = head**-0.5
+
+    def kernel(h_ref, sc_ref, sr_ref, qb_ref, vb_ref, ab_ref, g_ref, s_ref, *rest):
+        piece_refs = rest[: len(pieces)]
+        (x_ref, qkv_ref, p_ref, c_ref, r_ref, m_ref, wj, wo, low, got, gs, gr, ss, sr, ws) = rest[len(pieces) :]
+        t = lax.axis_index("t")
+        greet([{"t": lax.bitwise_xor(t, 1)}, {"t": lax.bitwise_xor(t, 2)}])
+        load_rows(piece_refs, wj, ws.at[0], sizes, share, 0, 3 * part)
+        load_chunks(piece_refs, wo, ws.at[1], sizes, share, 3 * part, part)
+        x_ref[t] = h_ref[...].astype(jnp.bfloat16)
+        group_gather(x_ref, t, gs, gr)
+        settle(wj, ws.at[0])
+        joint = dot(x_ref[...].reshape(count, width), wj[...])
+        qkv_ref[:, 0:part] = ((joint[:, 0:part] + qb_ref[...]) * scale).astype(jnp.bfloat16)
+        qkv_ref[:, part : 2 * part] = joint[:, part : 2 * part].astype(jnp.bfloat16)
+        qkv_ref[:, 2 * part :] = (joint[:, 2 * part :] + vb_ref[...]).astype(jnp.bfloat16)
+        linked = sc_ref[...] == sr_ref[...]
+        for at in range(part // head):
+            queries = qkv_ref[:, at * head : (at + 1) * head]
+            keys = qkv_ref[:, part + at * head : part + (at + 1) * head]
+            values = qkv_ref[:, 2 * part + at * head : 2 * part + (at + 1) * head]
+            scores = jnp.where(linked, dot_rt(queries, keys), masked_score)
+            exponent = jnp.exp(scores - jnp.max(scores, axis=-1, keepdims=True))
+            weights = (exponent / jnp.sum(exponent, axis=-1, keepdims=True)).astype(jnp.bfloat16)
+            p_ref[at] = weights
+            c_ref[:, at * head : (at + 1) * head] = dot(weights, values).astype(jnp.bfloat16)
+        settle(wo, ws.at[1])
+        attended = group_scatter(
+            lambda j: dot(c_ref[pl.ds(pl.multiple_of(j * n, n), n), :], wo[...]), t, low, got, ss, sr
+        )
+        total = h_ref[...] + (attended + ab_ref[...])
+        r_ref[...] = total
+        m_ref[...] = normed(total, g_ref[...], s_ref[...])
+
+    return pl.pallas_call(
+        kernel,
+        out_shape=[
+            jax.ShapeDtypeStruct((t_size, n, width), jnp.bfloat16),
+            jax.ShapeDtypeStruct((count, 3 * part), jnp.bfloat16),
+            jax.ShapeDtypeStruct((part // head, count, count), jnp.bfloat16),
+            jax.ShapeDtypeStruct((count, part), jnp.bfloat16),
+            jax.ShapeDtypeStruct((n, width), jnp.float32),
+            jax.ShapeDtypeStruct((n, width), jnp.float32),
+        ],
+        in_specs=[IN_VMEM] * 8 + [ANYWHERE] * len(pieces),
+        out_specs=[IN_VMEM] * 6,
+        scratch_shapes=[
+            pltpu.VMEM((width, 3 * part), jnp.bfloat16),
+            pltpu.VMEM((part, width), jnp.bfloat16),
+        ]
+        + scatter_scratch(n, width)
+        + [pltpu.SemaphoreType.DMA((2,))],
+        compiler_params=kernel_params(collective),
+        cost_estimate=cost(25),
+    )(hidden, seg_col, seg_row, query_bias, value_bias, attend_bias, gain, shift, *pieces)
+
+
+def feed_forward(middle, hidden_bias, return_bias, gain, shift, pieces, sizes, collective):
+    n, width = middle.shape
+    a_size, t_size, z_size = sizes
+    count = t_size * n
+    inner_width = hidden_bias.shape[1]
+    share = width // (a_size * t_size * z_size)
+    inner_share = inner_width // (a_size * z_size)
+
+    def kernel(m_ref, hb_ref, rb_ref, g_ref, s_ref, *rest):
+        piece_refs = rest[: len(pieces)]
+        (x_ref, act_ref, slope_ref, o_ref, h_ref, we, wr, low, got, gs, gr, ss, sr, ws) = rest[len(pieces) :]
+        t = lax.axis_index("t")
+        greet([{"t": lax.bitwise_xor(t, 1)}, {"t": lax.bitwise_xor(t, 2)}])
+        load_rows(piece_refs, we, ws.at[0], sizes, share, 0, inner_width)
+        load_blocks(piece_refs, wr, ws.at[1], sizes, t_size * share, inner_share)
+        x_ref[t] = m_ref[...].astype(jnp.bfloat16)
+        group_gather(x_ref, t, gs, gr)
+        settle(we, ws.at[0])
+        inner = dot(x_ref[...].reshape(count, width), we[...]) + hb_ref[...]
+        active, slope = gelu_pair(inner)
+        act_ref[...] = active.astype(jnp.bfloat16)
+        slope_ref[...] = slope.astype(jnp.bfloat16)
+        settle(wr, ws.at[1])
+        fed = group_scatter(
+            lambda j: dot(act_ref[pl.ds(pl.multiple_of(j * n, n), n), :], wr[...]), t, low, got, ss, sr
+        )
+        total = m_ref[...] + fed + rb_ref[...]
+        o_ref[...] = total
+        h_ref[...] = normed(total, g_ref[...], s_ref[...])
+
+    return pl.pallas_call(
+        kernel,
+        out_shape=[
+            jax.ShapeDtypeStruct((t_size, n, width), jnp.bfloat16),
+            jax.ShapeDtypeStruct((count, inner_width), jnp.bfloat16),
+            jax.ShapeDtypeStruct((count, inner_width), jnp.bfloat16),
+            jax.ShapeDtypeStruct((n, width), jnp.float32),
+            jax.ShapeDtypeStruct((n, width), jnp.float32),
+        ],
+        in_specs=[IN_VMEM] * 5 + [ANYWHERE] * len(pieces),
+        out_specs=[IN_VMEM] * 5,
+        scratch_shapes=[
+            pltpu.VMEM((width, inner_width), jnp.bfloat16),
+            pltpu.VMEM((inner_width, width), jnp.bfloat16),
+        ]
+        + scatter_scratch(n, width)
+        + [pltpu.SemaphoreType.DMA((2,))],
+        compiler_params=kernel_params(collective),
+        cost_estimate=cost(25),
+    )(middle, hidden_bias, return_bias, gain, shift, *pieces)
+
+
+def store_rows(target, grads, sizes, share, column):
+    a_size, t_size, z_size = sizes
+    a, z = lax.axis_index("a"), lax.axis_index("z")
+    width = grads.shape[1]
+    for a_at in range(a_size):
+        for z_at in range(z_size):
+            for t_at in range(t_size):
+                row = ((a_at * t_size + t_at) * z_size + z_at) * share
+                target[
+                    lax.bitwise_xor(a, a_at),
+                    lax.bitwise_xor(z, z_at),
+                    t_at * share : (t_at + 1) * share,
+                    column : column + width,
+                ] = grads[row : row + share, :].astype(jnp.bfloat16)
+
+
+def store_chunks(target, grads, sizes, share, column):
+    a_size, t_size, z_size = sizes
+    a, z = lax.axis_index("a"), lax.axis_index("z")
+    width = grads.shape[1] // t_size
+    for a_at in range(a_size):
+        for z_at in range(z_size):
+            row = (a_at * z_size + z_at) * share
+            for chunk in range(t_size):
+                target[
+                    lax.bitwise_xor(a, a_at),
+                    lax.bitwise_xor(z, z_at),
+                    chunk * share : (chunk + 1) * share,
+                    column : column + width,
+                ] = grads[row : row + share, chunk * width : (chunk + 1) * width].astype(jnp.bfloat16)
+
+
+def store_blocks(target, grads, sizes, first, share):
+    a_size, t_size, z_size = sizes
+    a, z = lax.axis_index("a"), lax.axis_index("z")
+    for a_at in range(a_size):
+        for z_at in range(z_size):
+            row = (a_at * z_size + z_at) * share
+            target[lax.bitwise_xor(a, a_at), lax.bitwise_xor(z, z_at), first : first + share, :] = (
+                grads[row : row + share, :].astype(jnp.bfloat16)
+            )
+
+
+def feed_backward(upstream, outer, residual, final_gain, middle_gain, gathered, active, slope, pieces, sizes, collective):
+    n, width = upstream.shape
+    a_size, t_size, z_size = sizes
+    count = t_size * n
+    inner_width = active.shape[1]
+    share = width // (a_size * t_size * z_size)
+    inner_share = inner_width // (a_size * z_size)
+    piece_rows = t_size * share + inner_share
+
+    def kernel(u_ref, o_ref, r_ref, fg_ref, mg_ref, x_ref, act_ref, slope_ref, *rest):
+        piece_refs = rest[: len(pieces)]
+        (res_ref, w_ref, v_ref, hid_ref, fed, inner_low, we, wr, low, got, gs, gr, ss, sr, ws) = rest[len(pieces) :]
+        t = lax.axis_index("t")
+        greet([{"t": lax.bitwise_xor(t, 1)}, {"t": lax.bitwise_xor(t, 2)}])
+        load_blocks(piece_refs, wr, ws.at[1], sizes, t_size * share, inner_share)
+        load_rows(piece_refs, we, ws.at[0], sizes, share, 0, inner_width)
+        outer_grad, final_part, upper_part = normed_back(o_ref[...], fg_ref[...], u_ref[...])
+        fed_low = outer_grad.astype(jnp.bfloat16)
+        fed[t] = fed_low
+        v_ref[0:1] = final_part
+        v_ref[1:2] = upper_part
+        v_ref[2:3] = jnp.sum(fed_low.astype(jnp.float32), axis=0, keepdims=True)
+        group_gather(fed, t, gs, gr)
+        settle(wr, ws.at[1])
+        active_grad = dot_rt(fed[...].reshape(count, width), wr[...])
+        lowered = (active_grad * slope_ref[...].astype(jnp.float32)).astype(jnp.bfloat16)
+        inner_low[...] = lowered
+        hid_ref[...] = jnp.sum(lowered.astype(jnp.float32), axis=0, keepdims=True)
+        settle(we, ws.at[0])
+
+        def weights():
+            store_blocks(
+                w_ref, dot_lt(act_ref[...], fed[...].reshape(count, width)), sizes, t_size * share, inner_share
+            )
+            store_rows(w_ref, dot_lt(x_ref[...].reshape(count, width), inner_low[...]), sizes, share, 0)
+
+        back = group_scatter(
+            lambda j: dot_rt(inner_low[pl.ds(pl.multiple_of(j * n, n), n), :], we[...]),
+            t,
+            low,
+            got,
+            ss,
+            sr,
+            weights,
+        )
+        res_grad, middle_part, lower_part = normed_back(r_ref[...], mg_ref[...], outer_grad + back)
+        res_ref[...] = res_grad
+        v_ref[3:4] = middle_part
+        v_ref[4:5] = lower_part
+        v_ref[5:8] = jnp.zeros((3, width), jnp.float32)
+
+    return pl.pallas_call(
+        kernel,
+        out_shape=[
+            jax.ShapeDtypeStruct((n, width), jnp.float32),
+            jax.ShapeDtypeStruct((a_size, z_size, piece_rows, width), jnp.bfloat16),
+            jax.ShapeDtypeStruct((8, width), jnp.float32),
+            jax.ShapeDtypeStruct((1, inner_width), jnp.float32),
+        ],
+        in_specs=[IN_VMEM] * 8 + [ANYWHERE] * len(pieces),
+        out_specs=[IN_VMEM] * 4,
+        scratch_shapes=[
+            pltpu.VMEM((t_size, n, width), jnp.bfloat16),
+            pltpu.VMEM((count, inner_width), jnp.bfloat16),
+            pltpu.VMEM((width, inner_width), jnp.bfloat16),
+            pltpu.VMEM((inner_width, width), jnp.bfloat16),
+        ]
+        + scatter_scratch(n, width)
+        + [pltpu.SemaphoreType.DMA((2,))],
+        compiler_params=kernel_params(collective),
+        cost_estimate=cost(30),
+    )(upstream, outer, residual, final_gain, middle_gain, gathered, active, slope, *pieces)
+
+
+def attention_backward(res_grad, gathered, qkv, weights_low, context, pieces, sizes, collective):
+    n, width = res_grad.shape
+    a_size, t_size, z_size = sizes
+    count = t_size * n
+    part = width // t_size
+    head = width // HEADS
+    share = width // (a_size * t_size * z_size)
+    scale = head**-0.5
+
+    def kernel(r_ref, x_ref, qkv_ref, p_ref, c_ref, *rest):
+        piece_refs = rest[: len(pieces)]
+        (g_ref, w_ref, v_ref, b_ref, fed, grad_low, joint, wj, wo, low, got, gs, gr, ss, sr, ws) = rest[len(pieces) :]
+        t = lax.axis_index("t")
+        greet([{"t": lax.bitwise_xor(t, 1)}, {"t": lax.bitwise_xor(t, 2)}])
+        load_chunks(piece_refs, wo, ws.at[1], sizes, share, 3 * part, part)
+        load_rows(piece_refs, wj, ws.at[0], sizes, share, 0, 3 * part)
+        own_low = r_ref[...].astype(jnp.bfloat16)
+        fed[t] = own_low
+        v_ref[0:1] = jnp.sum(own_low.astype(jnp.float32), axis=0, keepdims=True)
+        v_ref[1:8] = jnp.zeros((7, width), jnp.float32)
+        group_gather(fed, t, gs, gr)
+        settle(wo, ws.at[1])
+        grad_low[...] = dot_rt(fed[...].reshape(count, width), wo[...]).astype(jnp.bfloat16)
+        for at in range(part // head):
+            mine = slice(at * head, (at + 1) * head)
+            queries = qkv_ref[:, mine]
+            keys = qkv_ref[:, part + at * head : part + (at + 1) * head]
+            values = qkv_ref[:, 2 * part + at * head : 2 * part + (at + 1) * head]
+            weights = p_ref[at]
+            grads = grad_low[:, mine]
+            delta = jnp.sum(
+                grads.astype(jnp.float32) * c_ref[:, mine].astype(jnp.float32), axis=-1, keepdims=True
+            )
+            score_grad = (weights.astype(jnp.float32) * (dot_rt(grads, values) - delta)).astype(jnp.bfloat16)
+            joint[:, mine] = (
+                dot(score_grad, keys).astype(jnp.bfloat16).astype(jnp.float32) * scale
+            ).astype(jnp.bfloat16)
+            joint[:, part + at * head : part + (at + 1) * head] = dot_lt(score_grad, queries).astype(jnp.bfloat16)
+            joint[:, 2 * part + at * head : 2 * part + (at + 1) * head] = dot_lt(weights, grads).astype(jnp.bfloat16)
+        b_ref[...] = jnp.sum(joint[...].astype(jnp.float32), axis=0, keepdims=True)
+        settle(wj, ws.at[0])
+
+        def weight_grads():
+            store_rows(w_ref, dot_lt(x_ref[...].reshape(count, width), joint[...]), sizes, share, 0)
+            store_chunks(
+                w_ref, dot_lt(c_ref[...], fed[...].reshape(count, width)), sizes, share, 3 * part
+            )
+
+        back = group_scatter(
+            lambda j: dot_rt(joint[pl.ds(pl.multiple_of(j * n, n), n), :], wj[...]),
+            t,
+            low,
+            got,
+            ss,
+            sr,
+            weight_grads,
+        )
+        g_ref[...] = r_ref[...] + back
+
+    return pl.pallas_call(
+        kernel,
+        out_shape=[
+            jax.ShapeDtypeStruct((n, width), jnp.float32),
+            jax.ShapeDtypeStruct((a_size, z_size, t_size * share, width), jnp.bfloat16),
+            jax.ShapeDtypeStruct((8, width), jnp.float32),
+            jax.ShapeDtypeStruct((1, 3 * part), jnp.float32),
+        ],
+        in_specs=[IN_VMEM] * 5 + [ANYWHERE] * len(pieces),
+        out_specs=[IN_VMEM] * 4,
+        scratch_shapes=[
+            pltpu.VMEM((t_size, n, width), jnp.bfloat16),
+            pltpu.VMEM((count, part), jnp.bfloat16),
+            pltpu.VMEM((count, 3 * part), jnp.bfloat16),
+            pltpu.VMEM((width, 3 * part), jnp.bfloat16),
+            pltpu.VMEM((part, width), jnp.bfloat16),
+        ]
+        + scatter_scratch(n, width)
+        + [pltpu.SemaphoreType.DMA((2,))],
+        compiler_params=kernel_params(collective),
+        cost_estimate=cost(30),
+    )(res_grad, gathered, qkv, weights_low, context, *pieces)
+
+
+def pairs_of(size, mask):
+    return [(i, i ^ mask) for i in range(size)]
+
+
+def spread_weights(own, sizes):
+    a_size, _, z_size = sizes
+    near = [own] + [lax.ppermute(own, "z", pairs_of(z_size, d)) for d in range(1, z_size)]
+    pieces = list(near)
+    for d in range(1, a_size):
+        pieces += [lax.ppermute(piece, "a", pairs_of(a_size, d)) for piece in near]
+    return pieces
+
+
+def reduce_pieces(parts, sizes):
+    a_size, _, z_size = sizes
+    summed = widened(parts[0])
+    for d in range(1, a_size):
+        summed = summed + widened(lax.ppermute(parts[d], "a", pairs_of(a_size, d)))
+    sent = rounded(summed)
+    result = summed[0]
+    for d in range(1, z_size):
+        result = result + widened(lax.ppermute(sent[d], "z", pairs_of(z_size, d)))
+    return result
+
+
+def fast_local(sizes, *arguments):
+    (
+        features,
+        utterance_ends,
+        kernel_weight,
+        position_bias,
+        entry_gain,
+        base_shift,
+        joint_weight,
+        query_bias,
+        value_bias,
+        output_weight,
+        attend_bias,
+        middle_gain,
+        lower_shift,
+        expand_weight,
+        hidden_bias,
+        reduce_weight,
+        return_bias,
+        final_gain,
+        upper_shift,
+        head_weight,
+        vocab_bias,
+        cotangent,
+    ) = arguments
+    a_size, t_size, z_size = sizes
+    devices = a_size * t_size * z_size
+    _, n, width = features.shape
+    frames = n * z_size
+    rows = a_size * t_size
+    groups = CONV_G
+    group_width = width // groups
+    share = width // devices
+    taps = kernel_weight.shape[1] // group_width
+    layers = joint_weight.shape[0]
+    inner_all = expand_weight.shape[2]
+    inner = inner_all // t_size
+    inner_share = inner_all // devices
+    part = width // t_size
+    vocab = head_weight.shape[1]
+    packs = n // PACK
+    a, t, z = (lax.axis_index(axis) for axis in AXES)
+    turn = [(i * z_size + j, j * z_size + i) for i in range(t_size) for j in range(z_size)]
+
+    vectors = [attend_bias, middle_gain, lower_shift, return_bias, final_gain, upper_shift]
+    whole_rows = jnp.concatenate(
+        [entry_gain[None], base_shift[None]]
+        + vectors
+        + [head_weight.T, query_bias, value_bias, hidden_bias.reshape(layers * inner_share // share, share)],
+        axis=0,
+    )
+    gathered = lax.all_gather(whole_rows, AXES, axis=0)
+    vector_count = 2 + 6 * layers
+    whole = jnp.swapaxes(gathered[:, : vector_count + vocab], 0, 1).reshape(vector_count + vocab, width)
+    entry_full, base_full = widened(whole[0:1]), widened(whole[1:2])
+
+    def vector_of(kind, layer):
+        at = 2 + kind * layers + layer
+        return widened(whole[at : at + 1])
+
+    head_turned = whole[vector_count:]
+    own_rows = lax.dynamic_index_in_dim(
+        gathered[:, vector_count + vocab :].reshape(a_size, t_size, z_size, -1, share), t, 1, keepdims=False
+    )
+    own_rows = jnp.moveaxis(own_rows, 2, 0)
+    query_full = widened(own_rows[:layers].reshape(layers, part))
+    value_full = widened(own_rows[layers : 2 * layers].reshape(layers, part))
+    hidden_full = widened(
+        own_rows[2 * layers :]
+        .reshape(layers, inner_share // share, a_size, z_size, share)
+        .transpose(0, 2, 3, 1, 4)
+        .reshape(layers, inner)
+    )
+    all_ends = lax.all_gather(utterance_ends, ("a", "t"), axis=0, tiled=True)
+    row_ends = lax.dynamic_slice_in_dim(all_ends, a * t_size + z, 1, axis=0)
+    row_ids = segment_ids(jnp.arange(frames, dtype=jnp.int32), row_ends)
+    seg_col, seg_row = row_ids.reshape(frames, 1), row_ids
+    before = jnp.concatenate([jnp.zeros((rows, 1), jnp.int32), all_ends[:, :-1]], axis=1)
+    bounds = jnp.where(all_ends > before, all_ends, frames)
+    bounds = jnp.tile(bounds, (frames // PACK, 1))
+
+    joint_turned = joint_weight.reshape(layers, share, 3, a_size, t_size, part // a_size)
+    joint_turned = joint_turned.transpose(4, 0, 1, 2, 3, 5).reshape(t_size, layers, share, 3 * part)
+    expand_turned = expand_weight.reshape(layers, share, a_size, t_size, inner // a_size)
+    expand_turned = expand_turned.transpose(3, 0, 1, 2, 4).reshape(t_size, layers, share, inner)
+    columns = lax.all_to_all(
+        jnp.concatenate([joint_turned, expand_turned], axis=-1), "t", 0, 0, tiled=True
+    )
+    attend_pieces, feed_pieces = [], []
+    for layer in range(layers):
+        joint_rows = columns[:, layer, :, : 3 * part].reshape(t_size * share, 3 * part)
+        output_rows = output_weight[layer].reshape(share, t_size, part)
+        output_rows = output_rows.transpose(1, 0, 2).reshape(t_size * share, part)
+        attend_pieces.append(
+            spread_weights(jnp.concatenate([joint_rows, output_rows], axis=1), sizes)
+        )
+        expand_rows = columns[:, layer, :, 3 * part :].reshape(t_size * share, inner)
+        feed_pieces.append(
+            spread_weights(jnp.concatenate([expand_rows, reduce_weight[layer]], axis=0), sizes)
+        )
+
+    def by_group(tokens):
+        tokens = tokens.reshape(packs, PACK, groups, group_width)
+        return tokens.transpose(2, 0, 1, 3).reshape(groups, packs, PACK * group_width)
+
+    def from_channels(received):
+        received = received.reshape(devices, packs, PACK, share)
+        return received.transpose(1, 2, 0, 3).reshape(n, width)
+
+    def index_of(a_at, t_at, z_at):
+        return (a_at * t_size + t_at) * z_size + z_at
+
+    def group_of(a_at, t_at, z_at):
+        return index_of(a_at, t_at, z_at) * share // group_width
+
+    def turned_of(a_at, t_at, z_at):
+        return (a_at * z_size + z_at) * t_size + t_at
+
+    (arrived,) = swap_all(sizes, 1, [by_group(features[0])], [group_of])
+    packed = arrived.reshape(rows, frames // PACK, PACK * group_width)
+    packed = packed.transpose(1, 0, 2).reshape(frames // PACK * rows, PACK * group_width)
+    grid = kernel_weight.reshape(share, taps, group_width)
+    conv_pre, even, odd = conv_forward_packed(
+        packed,
+        bounds,
+        shifted_taps(grid.transpose(1, 2, 0)),
+        jnp.tile(widened(position_bias), PACK)[None],
+    )
+
+    def by_block(channels):
+        channels = channels.reshape(z_size, packs, rows, PACK * share)
+        return channels.transpose(2, 0, 1, 3).reshape(devices, packs, PACK * share)
+
+    (pre_parts,) = swap_all(sizes, 2, [by_block(conv_pre)], [turned_of])
+    pre = widened(from_channels(pre_parts))
+    own_feats = lax.ppermute(features[0], ("t", "z"), turn)
+    own_cot = lax.ppermute(cotangent[0], ("t", "z"), turn)
+    mixed = widened(own_feats) + gelu_exact(pre)
+    hidden = layer_norm(mixed, entry_full, base_full)
+
+    saved = []
+    for layer in range(layers):
+        gathered_x, qkv, weights_low, context, residual, middle = attention_forward(
+            hidden,
+            seg_col,
+            seg_row,
+            query_full[layer : layer + 1],
+            value_full[layer : layer + 1],
+            vector_of(0, layer),
+            vector_of(1, layer),
+            vector_of(2, layer),
+            attend_pieces[layer],
+            sizes,
+            10 + 4 * layer,
+        )
+        gathered_m, active, slope, outer, hidden = feed_forward(
+            middle,
+            hidden_full[layer : layer + 1],
+            vector_of(3, layer),
+            vector_of(4, layer),
+            vector_of(5, layer),
+            feed_pieces[layer],
+            sizes,
+            11 + 4 * layer,
+        )
+        saved.append((gathered_x, qkv, weights_low, context, residual, gathered_m, active, slope, outer))
+    final_low = rounded(hidden)
+    logits = dot_rt(final_low, head_turned) + widened(vocab_bias)
+    logits = lax.ppermute(logits, ("t", "z"), turn)
+    vocab_sum = jnp.sum(widened(own_cot), axis=0)
+    head_part = dot_lt(final_low, own_cot)
+    flow = dot(own_cot, head_turned)
+
+    layer_sums = [None] * layers
+    token_sums = [None] * layers
+    column_sums = [None] * layers
+    for layer in reversed(range(layers)):
+        gathered_x, qkv, weights_low, context, residual, gathered_m, active, slope, outer = saved[layer]
+        res_grad, feed_parts, feed_vectors, hidden_part = feed_backward(
+            flow,
+            outer,
+            residual,
+            vector_of(4, layer),
+            vector_of(1, layer),
+            gathered_m,
+            active,
+            slope,
+            feed_pieces[layer],
+            sizes,
+            12 + 4 * layer,
+        )
+        flow, attend_parts, attend_vectors, joint_part = attention_backward(
+            res_grad, gathered_x, qkv, weights_low, context, attend_pieces[layer], sizes, 13 + 4 * layer
+        )
+        token_sums[layer] = jnp.concatenate([attend_vectors[0:1], feed_vectors[0:5]], axis=0)
+        column_sums[layer] = jnp.concatenate(
+            [
+                joint_part[:, :part].reshape(a_size, z_size, share),
+                joint_part[:, 2 * part :].reshape(a_size, z_size, share),
+                hidden_part.reshape(a_size, z_size, inner_share),
+            ],
+            axis=-1,
+        )
+        layer_sums[layer] = (reduce_pieces(attend_parts, sizes), reduce_pieces(feed_parts, sizes))
+
+    mixed_grad, entry_part, base_part = normed_back(mixed, entry_full, flow)
+    slope = gelu_pair(pre)[1]
+    conv_low = rounded(mixed_grad * slope)
+    (low_parts,) = swap_all(sizes, 3, [by_group(conv_low)], [group_of])
+    low_parts = low_parts.reshape(a_size, t_size, z_size, packs, PACK * group_width)
+    packed_low = low_parts.transpose(1, 3, 0, 2, 4).reshape(frames // PACK * rows, PACK * group_width)
+    half = lax.rem(z, 2)
+    own_low = lax.dynamic_index_in_dim(
+        packed_low.reshape(-1, PACK, group_width // share, share), half, 2, keepdims=False
+    ).reshape(-1, PACK * share)
+    halves = grid.reshape(share, taps, 2, share)
+    kept = lax.dynamic_index_in_dim(halves, half, 2, keepdims=False)
+    given = lax.ppermute(
+        lax.dynamic_index_in_dim(halves, 1 - half, 2, keepdims=False), "z", pairs_of(z_size, 1)
+    )
+    both = jnp.where(half == 0, jnp.stack([kept, given]), jnp.stack([given, kept]))
+    both = both.reshape(2 * share, taps, share).transpose(1, 0, 2)
+    both = jnp.pad(both[::-1], ((1, 0), (0, 0), (0, 0)))
+    feats_part, kernel_own, position_part = conv_backward_packed(
+        packed_low, own_low, bounds, shifted_taps(both), even, odd
+    )
+    position_own = jnp.sum(position_part.reshape(PACK, share), axis=0)
+
+    vector_sums = jnp.concatenate([entry_part, base_part] + token_sums, axis=0)
+    vector_sums = vector_sums.reshape(vector_count, devices, share).transpose(1, 0, 2)
+    vector_sums = vector_sums.reshape(devices, vector_count * share)
+    column_all = jnp.concatenate(column_sums, axis=-1)
+    mine = (jnp.arange(t_size) == t)[None, :, None, None]
+    column_all = jnp.where(mine, column_all[:, None], 0.0).reshape(devices, -1)
+    flat = jnp.concatenate(
+        [
+            vector_sums,
+            column_all,
+            jnp.broadcast_to(vocab_sum[None], (devices, vocab)),
+        ],
+        axis=1,
+    )
+    room = -flat.shape[1] % 1024
+    flat = jnp.pad(flat, ((0, 0), (0, room)))
+    flat = jnp.concatenate([flat, head_part.reshape(devices, share * vocab)], axis=1)
+    flat = flat.reshape(devices, -1, 128)
+    feats_back, sums = swap_all(
+        sizes, 4, [by_block(feats_part), flat], [index_of, index_of]
+    )
+    features_grad = lax.ppermute(mixed_grad, ("t", "z"), turn) + widened(from_channels(feats_back))
+    sums = jnp.sum(sums, axis=0).reshape(-1)
+    at = vector_count * share
+    vector_own = sums[:at].reshape(vector_count, share)
+    column_own = sums[at : at + layers * (2 * share + inner_share)].reshape(layers, -1)
+    at += layers * (2 * share + inner_share)
+    vocab_own = sums[at : at + vocab]
+    head_own = sums[-share * vocab :].reshape(share, vocab)
+
+    back_columns = jnp.stack(
+        [
+            jnp.concatenate(
+                [
+                    attend_sum[:, : 3 * part].reshape(t_size, share, 3 * part),
+                    feed_sum[: t_size * share].reshape(t_size, share, inner),
+                ],
+                axis=-1,
+            )
+            for attend_sum, feed_sum in layer_sums
+        ],
+        axis=1,
+    )
+    back_columns = widened(lax.all_to_all(rounded(back_columns), "t", 0, 0, tiled=True))
+    joint_own = back_columns[..., : 3 * part].reshape(t_size, layers, share, 3, a_size, part // a_size)
+    joint_own = joint_own.transpose(1, 2, 3, 4, 0, 5).reshape(layers, share, 3 * width)
+    expand_own = back_columns[..., 3 * part :].reshape(t_size, layers, share, a_size, inner // a_size)
+    expand_own = expand_own.transpose(1, 2, 3, 0, 4).reshape(layers, share, inner_all)
+    output_own = jnp.stack(
+        [
+            attend_sum[:, 3 * part :].reshape(t_size, share, part).transpose(1, 0, 2).reshape(share, width)
+            for attend_sum, _ in layer_sums
+        ]
+    )
+    reduce_own = jnp.stack([feed_sum[t_size * share :] for _, feed_sum in layer_sums])
+    per_layer = vector_own[2:].reshape(layers, 6, share)
+    return (
+        logits[None],
+        features_grad[None],
+        kernel_own,
+        position_own,
+        vector_own[0],
+        vector_own[1],
+        joint_own,
+        column_own[:, :share],
+        column_own[:, share : 2 * share],
+        output_own,
+        per_layer[:, 0],
+        per_layer[:, 4],
+        per_layer[:, 5],
+        expand_own,
+        column_own[:, 2 * share :],
+        reduce_own,
+        per_layer[:, 3],
+        per_layer[:, 1],
+        per_layer[:, 2],
+        head_own,
+        vocab_own,
+    )
+
+
+def fits(dp_size, seq_size, width):
+    head = width // HEADS
+    if seq_size != 4 or dp_size % 4:
+        return None
+    devices = dp_size * seq_size
+    share = width // devices
+    a_size = dp_size // 4
+    if share % 16 or share * 2 != width // CONV_G or (seq_size * share) % head:
+        return None
+    return (a_size, 4, seq_size)
+
+
+def placed(mesh, width):
+    sizes = fits(mesh.shape["dp"], mesh.shape["seq"], width)
+    if sizes is None:
+        body, split, over, within = local, "dp", "seq", ("dp", "seq")
+    else:
+        body = functools.partial(fast_local, sizes)
+        mesh = jax.sharding.Mesh(mesh.devices.reshape(sizes), AXES)
+        split, over, within = ("a", "t"), "z", AXES
+    tokens = P(split, over, None)
+    first, first_wide = P(within), P(within, None)
+    second, second_wide = P(None, within), P(None, within, None)
     return jax.shard_map(
-        local,
+        body,
         mesh=mesh,
         in_specs=(
-            P("dp", "seq", None),
-            P("dp", None),
-            P(("dp", "seq"), None),
-            P(("dp", "seq")),
-            P(("dp", "seq")),
-            P(("dp", "seq")),
-            P(None, ("dp", "seq"), None),
-            P(None, ("dp", "seq")),
-            P(None, ("dp", "seq")),
-            P(None, ("dp", "seq"), None),
-            P(None, ("dp", "seq")),
-            P(None, ("dp", "seq")),
-            P(None, ("dp", "seq")),
-            P(None, ("dp", "seq"), None),
-            P(None, ("dp", "seq")),
-            P(None, ("dp", "seq"), None),
-            P(None, ("dp", "seq")),
-            P(None, ("dp", "seq")),
-            P(None, ("dp", "seq")),
-            P(("dp", "seq"), None),
+            tokens,
+            P(split, None),
+            first_wide,
+            first,
+            first,
+            first,
+            second_wide,
+            second,
+            second,
+            second_wide,
+            second,
+            second,
+            second,
+            second_wide,
+            second,
+            second_wide,
+            second,
+            second,
+            second,
+            first_wide,
             P(),
-            P("dp", "seq", None),
+            tokens,
         ),
         out_specs=(
-            P("dp", "seq", None),
-            P("dp", "seq", None),
-            P(("dp", "seq"), None),
-            P(("dp", "seq")),
-            P(("dp", "seq")),
-            P(("dp", "seq")),
-            P(None, ("dp", "seq"), None),
-            P(None, ("dp", "seq")),
-            P(None, ("dp", "seq")),
-            P(None, ("dp", "seq"), None),
-            P(None, ("dp", "seq")),
-            P(None, ("dp", "seq")),
-            P(None, ("dp", "seq")),
-            P(None, ("dp", "seq"), None),
-            P(None, ("dp", "seq")),
-            P(None, ("dp", "seq"), None),
-            P(None, ("dp", "seq")),
-            P(None, ("dp", "seq")),
-            P(None, ("dp", "seq")),
-            P(("dp", "seq"), None),
+            tokens,
+            tokens,
+            first_wide,
+            first,
+            first,
+            first,
+            second_wide,
+            second,
+            second,
+            second_wide,
+            second,
+            second,
+            second,
+            second_wide,
+            second,
+            second_wide,
+            second,
+            second,
+            second,
+            first_wide,
             P(),
         ),
         check_vma=False,
     )
+
+
+def solution(mesh):
+    def whole(*arguments):
+        return placed(mesh, arguments[0].shape[2])(*arguments)
+
+    return whole

time: 4180 us -> 909 us (0.22)
  waiting for transfers between devices: 2720 us -> 171 us
  local copies, waits for them, and re-layouts: 773 us -> 169 us
  Pallas kernels: 0 us -> 342 us
  matrix products: 279 us -> 1.55 us
  blocking collectives: 278 us -> 71.6 us
  starting transfers between devices: 13.5 us -> 101 us
    reduce_scatter x4 -> x0, waiting for transfers between devices: 2310 us -> none  [the longest x2 1480 us: local(): lax.psum_scatter(layer_term(jnp.int32(0), rows_share * lax.axis_size(('dp...]
    all_gather x13 -> x0, waiting for transfers between devices: 373 us -> none  [the longest x2 147 us: local(): lax.all_gather(reduce_weight[layer_at], ('dp', 'seq'), axis=0, tiled=True)]
    pallas_call x0 -> x14, Pallas kernels: none -> 342 us  [the longest x4 109 us: swap_all(): pl.pallas_call(kernel, out_shape=[jax.ShapeDtypeStruct((total,) + payload...]
    dot_general x63 -> x3, matrix products: 279 us -> 1.55 us  [the longest x1 1.07 us: dot(): return jnp.dot(left, right, preferred_element_type=jnp.float32)]
    slice x143 -> x32, local copies, waits for them, and re-layouts: 242 us -> 10.9 us  [the longest x2 1.55 us: fast_local(): attend_vectors[0:1]]
    ppermute x4 -> x49, waiting for transfers between devices: 0.01 us -> 160 us  [the longest x12 103 us: reduce_pieces(): result = result + widened(lax.ppermute(sent[d], 'z', pairs_of(z_size, d)))]
    unnamed x1035 -> x193, local copies, waits for them, and re-layouts: 150 us -> 7.04 us
    concatenate x3 -> x15, local copies, waits for them, and re-layouts: 176 us -> 37.6 us  [the longest x2 35.8 us: shifted_taps(): jnp.concatenate(parts, axis=1).reshape(steps, PACK * depth, PACK * width)]
  transfers between devices with their start and end apart: 25 -> 51, of which waited for: 12 -> 18; matrix products, arithmetic and copies ran while one was open for 24% -> 21% of each run, Pallas kernels for 0% -> 21%
where the time goes in v1:
time: 909 us; the launch traced here: 899 us
  Pallas kernels  342 us (38%)
  waiting for transfers between devices  171 us (19%)
  local copies, waits for them, and re-layouts  169 us (19%)
  starting transfers between devices  101 us (11%)
  blocking collectives  71.6 us (8%)
  other arithmetic  40.7 us (4%)
    pallas_call x4, Pallas kernels, swap_all(): pl.pallas_call(kernel, out_shape=[jax.ShapeDtypeStruct((total,) + payload...  109 us
    ppermute x12, waiting for transfers between devices, reduce_pieces(): result = result + widened(lax.ppermute(sent[d], 'z', pairs_of(z_size, d)))  103 us
    all_gather x1, blocking collectives, fast_local(): gathered = lax.all_gather(whole_rows, AXES, axis=0)  63.8 us
    pallas_call x2, Pallas kernels, attention_backward(): pl.pallas_call(kernel, out_shape=[jax.ShapeDtypeStruct((n, width), jnp.fl...  59.1 us
    pallas_call x2, Pallas kernels, feed_backward(): pl.pallas_call(kernel, out_shape=[jax.ShapeDtypeStruct((n, width), jnp.fl...  52.8 us
    pallas_call x2, Pallas kernels, attention_forward(): pl.pallas_call(kernel, out_shape=[jax.ShapeDtypeStruct((t_size, n, width)...  51.7 us
    ppermute x12, waiting for transfers between devices, spread_weights(): lax.ppermute(own, 'z', pairs_of(z_size, d))  49.1 us
    pallas_call x2, Pallas kernels, feed_forward(): pl.pallas_call(kernel, out_shape=[jax.ShapeDtypeStruct((t_size, n, width)...  48.9 us
  transfers between devices with their start and end apart: 51, of which 18 were waited for; matrix products, arithmetic and copies ran while one was open for 21% of the time, Pallas kernels for 21%

profile of v1, /device:TPU:16, one launch (start us, length us, event | category | flops | bytes accessed | tf_op | source)
XLA Modules:
  0.0 898.5 jit_solution(17526864364093970353)
XLA Ops:
  0.7 3.3 collective-permute-start
  8.0 4.2 all-to-all-start
  12.2 4.5 collective-permute-start.30
  18.4 6.8 constant_dynamic-slice_fusion.1
  25.2 5.2 copy.215
  35.5 63.8 %all-gather.2 = bf16[32,58,32]{1,2,0:T(8,128)(2,1)S(1)} all-gather(bf16[1,58,32]{1,2,0:T(8,128)(2,1)S(1)} %bitcast.310), channel_id=2, replica_groups=mesh['a'=2,'t'=4,'z'=4] {'a','t','z'}, dimensions={0}, use_global_device_ids=true | all-gather | bytes 122496 | tf_op jit(solution)/shard_map/all_gather | solution.py:1308
  103.2 13.0 %fusion.39 = (bf16[136,64,32]{2,1,0:T(8,128)(2,1)S(1)}, bf16[136,64,32]{2,1,0:T(8,128)(2,1)}, bf16[136,64,32]{2,1,0:T(8,128)(2,1)}, bf16[136,64,32]{2,1,0:T(8,12...) fusion(bf16[128,64,32]{2,1,0:T(8,128)(2,1)} %copy.232), kind=kLoop, calls=%fused_computation.155 | loop fusion | bytes 4980736 | tf_op jit(solution)/shard_map/jit(_pad)/pad | solution.py:765
  116.2 7.8 all-gather.1
  126.5 19.3 %shard_map.373 = bf16[32,16,512]{2,1,0:T(8,128)(2,1)} custom-call(bf16[16,16,512]{2,1,0:T(8,128)(2,1)} %reshape.574.refs_0_), custom_call_target="tpu_custom_call" | custom-call | flops 22000001024 | bytes 1048576 | tf_op jit(solution)/shard_map/pallas_call | solution.py:613
  148.5 17.8 %concatenate.108.k_ref = bf16[17,512,256]{2,1,0:T(8,128)(2,1)} concatenate(bf16[17,512,32]{2,1,0:T(8,128)(2,1)} %bitcast.252, bf16[17,512,32]{2,1,0:T(8,128)(2,1)} %bitcast.251, bf16[17,512,32]{2,1,0:T(8,128)(2,1)} %bitcast.250, bf16[17,512,32]{2,1,0:T(8,128)(2,1)} %bitcast.249, bf16[17,512,32]{2,1,0:T(8,128)(2,1)} %bitcast.248, bf16[17,512,32]{2,1,0:T(8,128)(2,1)} %bitcast.247, ...), dimensions={2} | concatenate | bytes 8912896 | tf_op jit(solution)/shard_map/concatenate | solution.py:768
  166.3 7.4 shard_map.374
  175.5 12.4 %shard_map.375 = bf16[32,16,256]{2,1,0:T(8,128)(2,1)} custom-call(bf16[32,16,256]{2,1,0:T(8,128)(2,1)} %bitcast.298), custom_call_target="tpu_custom_call" | custom-call | flops 22000001024 | bytes 1048576 | tf_op jit(solution)/shard_map/pallas_call | solution.py:613
  187.9 2.9 convert_reduce_fusion
  193.1 2.5 copy.248
  195.6 2.6 reshape.618
  213.2 2.5 copy.214
  218.2 2.7 fusion.36
  222.2 3.0 copy.216
  228.8 7.7 fusion.38
  247.8 3.1 collective-permute-done.1.rest_1_
  250.9 3.0 collective-permute-start.16
  253.9 4.6 collective-permute-done.2.rest_2_
  258.5 2.7 collective-permute-start.8
  261.2 9.8 %collective-permute-done.3.rest_3_ = bf16[128,1024]{1,0:T(8,128)(2,1)S(1)} collective-permute-done((bf16[128,1024]{1,0:T(8,128)(2,1)S(1)}, bf16[128,1024]{1,0:T(8,128)(2,1)S(1)}, u32[]{:S(2)}, u32[]{:S(2)}) %collective-permute-start.3) | collective-permute-done | bytes 262176 | tf_op jit(solution)/shard_map/ppermute | solution.py:1238
  274.5 18.0 %concatenate.123.k_ref = bf16[17,512,256]{2,1,0:T(8,128)(2,1)} concatenate(bf16[17,512,32]{2,1,0:T(8,128)(2,1)} %bitcast.260, bf16[17,512,32]{2,1,0:T(8,128)(2,1)} %bitcast.259, bf16[17,512,32]{2,1,0:T(8,128)(2,1)} %bitcast.258, bf16[17,512,32]{2,1,0:T(8,128)(2,1)} %bitcast.257, bf16[17,512,32]{2,1,0:T(8,128)(2,1)} %bitcast.256, bf16[17,512,32]{2,1,0:T(8,128)(2,1)} %bitcast.255, ...), dimensions={2} | concatenate | bytes 8912896 | tf_op jit(solution)/shard_map/concatenate | solution.py:768
  294.0 16.2 %collective-permute-start.5 = (bf16[128,1024]{1,0:T(8,128)(2,1)}, bf16[128,1024]{1,0:T(8,128)(2,1)S(1)}, u32[]{:S(2)}, u32[]{:S(2)}) collective-permute-start(bf16[128,1024]{1,0:T(8,128)(2,1)} %copy-done.79), channel_id=1, source_target_pairs={{0,16},{16,0},{1,17},{17,1},{2,18},{18,2},{3,19},{19,3},{4,20},{20... | collective-permute-start | bytes 786440 | tf_op jit(solution)/shard_map/ppermute | solution.py:1241
  313.2 7.5 collective-permute-done.9.rest_2_
  321.6 10.1 %collective-permute-done.10.rest_3_ = bf16[256,1024]{1,0:T(8,128)(2,1)S(1)} collective-permute-done((bf16[256,1024]{1,0:T(8,128)(2,1)}, bf16[256,1024]{1,0:T(8,128)(2,1)S(1)}, u32[]{:S(2)}, u32[]{:S(2)}) %collective-permute-start.10) | collective-permute-done | bytes 524320 | tf_op jit(solution)/shard_map/ppermute | solution.py:1238
  335.2 25.7 %shard_map.376 = (bf16[4,128,1024]{2,1,0:T(8,128)(2,1)}, bf16[512,768]{1,0:T(8,128)(2,1)}, bf16[4,512,512]{2,1,0:T(8,128)(2,1)}, bf16[512,256]{1,0:T(8,128)(2,1)...) custom-call(f32[128,1024]{1,0:T(8,128)} %multiply_add_fusion.h_ref, s32[512,1]{1,0:T(8,128)} %copy.207.sc_ref, ...), custom_call_target="tpu_custom_call" | custom-call | flops 27499999232 | bytes 1048576 | tf_op jit(solution)/shard_map/pallas_call | solution.py:957
  361.0 2.8 collective-permute-start.23
  369.9 24.5 %shard_map.377 = (bf16[4,128,1024]{2,1,0:T(8,128)(2,1)}, bf16[512,1024]{1,0:T(8,128)(2,1)}, bf16[512,1024]{1,0:T(8,128)(2,1)}, f32[128,1024]{1,0:T(8,128)}, f32[128,1024]{1,0:T(8,128)}) custom-call(f32[128,1024]{1,0:T(8,128)} %get-tuple-element.68.m_ref, f32[1,1024]{1,0:T(1,128)} %slice.345.hb_ref, f32[1,1024]{1,0:T(1,128)} %reshape.624.rb_ref, ...), custom_call_target="tpu_custom_call" | custom-call | flops 27499999232 | bytes 1048576 | tf_op jit(solution)/shard_map/pallas_call | solution.py:1010
  397.6 11.6 %collective-permute-done.24.rest_3_ = bf16[256,1024]{1,0:T(8,128)(2,1)S(1)} collective-permute-done((bf16[256,1024]{1,0:T(8,128)(2,1)S(1)}, bf16[256,1024]{1,0:T(8,128)(2,1)S(1)}, u32[]{:S(2)}, u32[]{:S(2)}) %collective-permute-start.24) | collective-permute-done | bytes 524320 | tf_op jit(solution)/shard_map/ppermute | solution.py:1238
  412.7 26.0 %shard_map.378 = (bf16[4,128,1024]{2,1,0:T(8,128)(2,1)}, bf16[512,768]{1,0:T(8,128)(2,1)}, bf16[4,512,512]{2,1,0:T(8,128)(2,1)}, bf16[512,256]{1,0:T(8,128)(2,1)...) custom-call(f32[128,1024]{1,0:T(8,128)} %get-tuple-element.69.h_ref, s32[512,1]{1,0:T(8,128)} %copy.207.sc_ref, ...), custom_call_target="tpu_custom_call" | custom-call | flops 27499999232 | bytes 1048576 | tf_op jit(solution)/shard_map/pallas_call | solution.py:957
  438.8 6.7 collective-permute-done.28.rest_7_
  446.3 24.4 %shard_map.379 = (bf16[4,128,1024]{2,1,0:T(8,128)(2,1)}, bf16[512,1024]{1,0:T(8,128)(2,1)}, bf16[512,1024]{1,0:T(8,128)(2,1)}, f32[128,1024]{1,0:T(8,128)}, f32[128,1024]{1,0:T(8,128)}) custom-call(f32[128,1024]{1,0:T(8,128)} %get-tuple-element.70.m_ref, f32[1,1024]{1,0:T(1,128)} %slice.361.hb_ref, f32[1,1024]{1,0:T(1,128)} %reshape.630.rb_ref, ...), custom_call_target="tpu_custom_call" | custom-call | flops 27499999232 | bytes 1048576 | tf_op jit(solution)/shard_map/pallas_call | solution.py:1010
  470.7 26.4 %shard_map.380 = (f32[128,1024]{1,0:T(8,128)}, bf16[2,4,256,1024]{3,2,1,0:T(8,128)(2,1)}, f32[8,1024]{1,0:T(8,128)}, f32[1,1024]{1,0:T(1,128)}) custom-call(f32[128,1024]{1,0:T(8,128)} %convolution_bitcast_fusion.u_ref, f32[128,1024]{1,0:T(8,128)} %get-tuple-element.72.o_ref, f32[128,1024]{1,0:T(8,128)} %get-tuple-element.73.r_ref, ...), custom_call_target="tpu_custom_call" | custom-call | flops 32999999488 | bytes 1048576 | tf_op jit(solution)/shard_map/pallas_call | solution.py:1126
  497.1 29.7 %shard_map.381 = (f32[128,1024]{1,0:T(8,128)}, bf16[2,4,128,1024]{3,2,1,0:T(8,128)(2,1)}, f32[8,1024]{1,0:T(8,128)}, f32[1,768]{1,0:T(1,128)}) custom-call(f32[128,1024]{1,0:T(8,128)} %get-tuple-element.77.r_ref, bf16[4,128,1024]{2,1,0:T(8,128)(2,1)} %get-tuple-element.78.x_ref, bf16[512,768]{1,0:T(8,128)(2,1)} %get-tuple-element.79.qkv_ref, ...), custom_call_target="tpu_custom_call" | custom-call | flops 32999999488 | bytes 1048576 | tf_op jit(solution)/shard_map/pallas_call | solution.py:1208
  526.9 26.4 %shard_map.382 = (f32[128,1024]{1,0:T(8,128)}, bf16[2,4,256,1024]{3,2,1,0:T(8,128)(2,1)}, f32[8,1024]{1,0:T(8,128)}, f32[1,1024]{1,0:T(1,128)}) custom-call(f32[128,1024]{1,0:T(8,128)} %get-tuple-element.82.u_ref, f32[128,1024]{1,0:T(8,128)} %get-tuple-element.83.o_ref, f32[128,1024]{1,0:T(8,128)} %get-tuple-element.84.r_ref, ...), custom_call_target="tpu_custom_call" | custom-call | flops 32999999488 | bytes 1048576 | tf_op jit(solution)/shard_map/pallas_call | solution.py:1126
  553.4 29.4 %shard_map.383 = (f32[128,1024]{1,0:T(8,128)}, bf16[2,4,128,1024]{3,2,1,0:T(8,128)(2,1)}, f32[8,1024]{1,0:T(8,128)}, f32[1,768]{1,0:T(1,128)}) custom-call(f32[128,1024]{1,0:T(8,128)} %get-tuple-element.88.r_ref, bf16[4,128,1024]{2,1,0:T(8,128)(2,1)} %get-tuple-element.89.x_ref, bf16[512,768]{1,0:T(8,128)(2,1)} %get-tuple-element.90.qkv_ref, ...), custom_call_target="tpu_custom_call" | custom-call | flops 32999999488 | bytes 1048576 | tf_op jit(solution)/shard_map/pallas_call | solution.py:1208
  587.8 17.4 %shard_map.384 = bf16[32,16,512]{2,1,0:T(8,128)(2,1)} custom-call(bf16[16,16,512]{2,1,0:T(8,128)(2,1)} %reshape.590.refs_0_), custom_call_target="tpu_custom_call" | custom-call | flops 22000001024 | bytes 1048576 | tf_op jit(solution)/shard_map/pallas_call | solution.py:613
  608.8 3.2 slice_bitcast_fusion.1
  623.2 3.6 constant_dynamic-slice_fusion.2
  626.7 4.4 copy.213
  631.9 12.3 %shard_map.385 = (bf16[512,256]{1,0:T(8,128)(2,1)}, f32[32,8192]{1,0:T(8,128)}, f32[1,256]{1,0:T(1,128)}) custom-call(bf16[512,512]{1,0:T(8,128)(2,1)} %reshape.592.g_ref, bf16[512,256]{1,0:T(8,128)(2,1)} %copy.217.own_ref, s32[512,4]{1,0:T(8,128)} %broadcast_bitcast_fusion.b_ref, bf16[17,512,256]{2,1,0:T(8,128)(2,1)} %concatenate.123.k_ref, ...), custom_call_target="tpu_custom_call" | custom-call | flops 16499999744 | bytes 1048576 | tf_op jit(solution)/shard_map/pallas_call | solution.py:740
  646.0 4.7 collective-permute-start.31
  651.6 60.2 %shard_map.386 = (bf16[32,16,256]{2,1,0:T(8,128)(2,1)}, f32[32,16,128]{2,1,0:T(8,128)}) custom-call(bf16[32,16,256]{2,1,0:T(8,128)(2,1)} %bitcast.295, f32[32,16,128]{2,1,0:T(8,128)} %pad_maximum_fusion.7.refs_1_), custom_call_target="tpu_custom_call" | custom-call | flops 22000001024 | bytes 1048576 | tf_op jit(solution)/shard_map/pallas_call | solution.py:613
  713.6 4.3 collective-permute-start.29
  719.8 3.1 reshape.640
  722.9 2.8 copy.224
  739.9 4.5 collective-permute-done.34
  744.4 2.6 collective-permute-start.42
  747.0 5.9 collective-permute-done.35
  752.9 3.9 collective-permute-start.43
  756.8 16.3 %collective-permute-done.36 = bf16[128,1024]{1,0:T(8,128)(2,1)S(1)} collective-permute-done((bf16[128,1024]{1,0:T(8,128)(2,1)S(1)}, bf16[128,1024]{1,0:T(8,128)(2,1)S(1)}, u32[]{:S(2)}, u32[]{:S(2)}) %collective-permute-start.36) | collective-permute-done | bytes 262176 | tf_op jit(solution)/shard_map/ppermute | solution.py:1253
  773.3 4.9 fusion.34
  779.1 3.5 collective-permute-start.39
  782.6 3.2 fusion.35
  790.4 11.7 %collective-permute-done.38 = bf16[256,1024]{1,0:T(8,128)(2,1)S(1)} collective-permute-done((bf16[256,1024]{1,0:T(8,128)(2,1)S(1)}, bf16[256,1024]{1,0:T(8,128)(2,1)S(1)}, u32[]{:S(2)}, u32[]{:S(2)}) %collective-permute-start.38) | collective-permute-done | bytes 524320 | tf_op jit(solution)/shard_map/ppermute | solution.py:1253
  805.9 11.6 %collective-permute-done.39 = bf16[256,1024]{1,0:T(8,128)(2,1)S(1)} collective-permute-done((bf16[256,1024]{1,0:T(8,128)(2,1)}, bf16[256,1024]{1,0:T(8,128)(2,1)S(1)}, u32[]{:S(2)}, u32[]{:S(2)}) %collective-permute-start.39) | collective-permute-done | bytes 524320 | tf_op jit(solution)/shard_map/ppermute | solution.py:1253
  817.5 34.4 %collective-permute-done.40 = bf16[256,1024]{1,0:T(8,128)(2,1)S(1)} collective-permute-done((bf16[256,1024]{1,0:T(8,128)(2,1)S(1)}, bf16[256,1024]{1,0:T(8,128)(2,1)S(1)}, u32[]{:S(2)}, u32[]{:S(2)}) %collective-permute-start.40) | collective-permute-done | bytes 524320 | tf_op jit(solution)/shard_map/ppermute | solution.py:1253
  853.5 9.1 %collective-permute-done.47 = bf16[256,1024]{1,0:T(8,128)(2,1)} collective-permute-done((bf16[256,1024]{1,0:T(8,128)(2,1)}, bf16[256,1024]{1,0:T(8,128)(2,1)}, u32[]{:S(2)}, u32[]{:S(2)}) %collective-permute-start.47) | collective-permute-done | bytes 524320 | tf_op jit(solution)/shard_map/ppermute | solution.py:1253
  862.5 10.0 %collective-permute-done.48 = bf16[256,1024]{1,0:T(8,128)(2,1)} collective-permute-done((bf16[256,1024]{1,0:T(8,128)(2,1)}, bf16[256,1024]{1,0:T(8,128)(2,1)}, u32[]{:S(2)}, u32[]{:S(2)}) %collective-permute-start.48) | collective-permute-done | bytes 524320 | tf_op jit(solution)/shard_map/ppermute | solution.py:1253
  875.4 3.7 all-to-all-start.1
  881.0 11.1 %all-to-all-done.1 = bf16[4,2,32,1792]{3,2,1,0:T(8,128)(2,1)S(1)} async-done(((bf16[4,2,32,1792]{3,2,1,0:T(8,128)(2,1)}), bf16[4,2,32,1792]{3,2,1,0:T(8,128)(2,1)S(1)}, u32[]{:S(2)}, u32[]{:S(2)}) %all-to-all-start.1) | async-done | bytes 917536 | tf_op jit(solution)/shard_map/all_to_all | solution.py:1528
  (443 shorter events, 145.9 us)
Async XLA Ops:
  0.7 217.5 %collective-permute-start = (bf16[128,1024]{1,0:T(8,128)(2,1)}, bf16[128,1024]{1,0:T(8,128)(2,1)}, u32[]{:S(2)}, u32[]{:S(2)}) collective-permute-start(bf16[128,1024]{1,0:T(8,128)(2,1)} %bitcast.294), channel_id=1, source_target_pairs={{0,0},{1,4},{2,8},{3,12},{4,1},{5,5},{6,9},{7,13},{8,2},{9,6},{10,... | collective-permute-start | bytes 786440 | tf_op jit(solution)/shard_map/ppermute | solution.py:1392
  8.0 228.6 %all-to-all-start = ((bf16[4,2,32,1792]{3,2,1,0:T(8,128)(2,1)}), bf16[4,2,32,1792]{3,2,1,0:T(8,128)(2,1)}, u32[]{:S(2)}, u32[]{:S(2)}) async-start(bf16[4,2,32,1792]{3,2,1,0:T(8,128)(2,1)} %pad_maximum_fusion.1), calls=%async_computation | async-start | bytes 1835008 | tf_op jit(solution)/shard_map/all_to_all | solution.py:1342
  12.2 204.1 %collective-permute-start.30 = (bf16[128,32]{0,1:T(8,128)(2,1)}, bf16[128,32]{0,1:T(8,128)(2,1)S(1)}, u32[]{:S(2)}, u32[]{:S(2)}) collective-permute-start(bf16[128,32]{0,1:T(8,128)(2,1)} %bitcast.50), channel_id=1, source_target_pairs={{0,0},{1,4},{2,8},{3,12},{4,1},{5,5},{6,9},{7,13},{8,2},{9,6},{10,... | collective-permute-start | bytes 24584 | tf_op jit(solution)/shard_map/ppermute | solution.py:1393
  30.5 190.4 %collective-permute-start.32 = (bf16[32,128,32]{1,2,0:T(8,128)(2,1)}, bf16[32,128,32]{1,2,0:T(8,128)(2,1)}, u32[]{:S(2)}, u32[]{:S(2)}) collective-permute-start(bf16[32,128,32]{1,2,0:T(8,128)(2,1)} %bitcast.57), channel_id=1, source_target_pairs={{0,1},{1,0},{2,3},{3,2},{4,5},{5,4},{6,7},{7,6},{8,9},{9,8},{10,11... | collective-permute-start | bytes 786440 | tf_op jit(solution)/shard_map/ppermute | solution.py:1474
  198.3 113.9 %copy-start.32 = (f32[1024]{0:T(1024)}, f32[1024]{0:T(1024)S(1)}, u32[]{:S(2)}) copy-start(f32[1024]{0:T(1024)S(1)} %reshape.619) | copy-start | bytes 12292
  220.9 91.4 %copy-start = (f32[128,1024]{1,0:T(8,128)}, f32[128,1024]{1,0:T(8,128)S(1)}, u32[]{:S(2)}) copy-start(f32[128,1024]{1,0:T(8,128)S(1)} %get-tuple-element.142) | copy-start | bytes 1572868
  237.7 54.7 %copy-start.25 = (bf16[128,1024]{1,0:T(8,128)(2,1)}, bf16[128,1024]{1,0:T(8,128)(2,1)S(1)}, u32[]{:S(2)}) copy-start(bf16[128,1024]{1,0:T(8,128)(2,1)S(1)} %pad_maximum_fusion.5.rest_0_) | copy-start | bytes 786436
  237.7 13.1 %collective-permute-start.1 = (bf16[128,1024]{1,0:T(8,128)(2,1)S(1)}, bf16[128,1024]{1,0:T(8,128)(2,1)S(1)}, u32[]{:S(2)}, u32[]{:S(2)}) collective-permute-start(bf16[128,1024]{1,0:T(8,128)(2,1)S(1)} %pad_maximum_fusion.5.rest_0_), channel_id=1, source_target_pairs={{0,1},{1,0},{2,3},{3,2},{4,5},{5,4},{6,7},{7,6},{8,9},{9,8},{10,11... | collective-permute-start | bytes 786440 | tf_op jit(solution)/shard_map/ppermute | solution.py:1238
  239.3 19.2 %collective-permute-start.2 = (bf16[128,1024]{1,0:T(8,128)(2,1)S(1)}, bf16[128,1024]{1,0:T(8,128)(2,1)S(1)}, u32[]{:S(2)}, u32[]{:S(2)}) collective-permute-start(bf16[128,1024]{1,0:T(8,128)(2,1)S(1)} %pad_maximum_fusion.5.rest_0_), channel_id=1, source_target_pairs={{0,2},{1,3},{2,0},{3,1},{4,6},{5,7},{6,4},{7,5},{8,10},{9,11},{10,... | collective-permute-start | bytes 786440 | tf_op jit(solution)/shard_map/ppermute | solution.py:1238
  240.5 30.5 %collective-permute-start.3 = (bf16[128,1024]{1,0:T(8,128)(2,1)S(1)}, bf16[128,1024]{1,0:T(8,128)(2,1)S(1)}, u32[]{:S(2)}, u32[]{:S(2)}) collective-permute-start(bf16[128,1024]{1,0:T(8,128)(2,1)S(1)} %pad_maximum_fusion.5.rest_0_), channel_id=1, source_target_pairs={{0,3},{1,2},{2,1},{3,0},{4,7},{5,6},{6,5},{7,4},{8,11},{9,10},{10,... | collective-permute-start | bytes 786440 | tf_op jit(solution)/shard_map/ppermute | solution.py:1238
  241.3 30.9 %collective-permute-start.4 = (bf16[128,1024]{1,0:T(8,128)(2,1)S(1)}, bf16[128,1024]{1,0:T(8,128)(2,1)S(1)}, u32[]{:S(2)}, u32[]{:S(2)}) collective-permute-start(bf16[128,1024]{1,0:T(8,128)(2,1)S(1)} %pad_maximum_fusion.5.rest_0_), channel_id=1, source_target_pairs={{0,16},{16,0},{1,17},{17,1},{2,18},{18,2},{3,19},{19,3},{4,20},{20... | collective-permute-start | bytes 786440 | tf_op jit(solution)/shard_map/ppermute | solution.py:1241
  243.4 49.1 %collective-permute-start.15 = (bf16[128,1024]{1,0:T(8,128)(2,1)}, bf16[128,1024]{1,0:T(8,128)(2,1)}, u32[]{:S(2)}, u32[]{:S(2)}) collective-permute-start(bf16[128,1024]{1,0:T(8,128)(2,1)} %pad_maximum_fusion.6.rest_0_), channel_id=1, source_target_pairs={{0,1},{1,0},{2,3},{3,2},{4,5},{5,4},{6,7},{7,6},{8,9},{9,8},{10,11... | collective-permute-start | bytes 786440 | tf_op jit(solution)/shard_map/ppermute | solution.py:1238
  250.9 41.7 %collective-permute-start.16 = (bf16[128,1024]{1,0:T(8,128)(2,1)}, bf16[128,1024]{1,0:T(8,128)(2,1)}, u32[]{:S(2)}, u32[]{:S(2)}) collective-permute-start(bf16[128,1024]{1,0:T(8,128)(2,1)} %pad_maximum_fusion.6.rest_0_), channel_id=1, source_target_pairs={{0,2},{1,3},{2,0},{3,1},{4,6},{5,7},{6,4},{7,5},{8,10},{9,11},{10,... | collective-permute-start | bytes 786440 | tf_op jit(solution)/shard_map/ppermute | solution.py:1238
  258.5 51.7 %collective-permute-start.8 = (bf16[256,1024]{1,0:T(8,128)(2,1)}, bf16[256,1024]{1,0:T(8,128)(2,1)}, u32[]{:S(2)}, u32[]{:S(2)}) collective-permute-start(bf16[256,1024]{1,0:T(8,128)(2,1)} %pad_maximum_fusion.3.rest_0_), channel_id=1, source_target_pairs={{0,1},{1,0},{2,3},{3,2},{4,5},{5,4},{6,7},{7,6},{8,9},{9,8},{10,11... | collective-permute-start | bytes 1572872 | tf_op jit(solution)/shard_map/ppermute | solution.py:1238
  261.2 51.0 %copy-start.41 = (f32[128]{0:T(128)}, f32[128]{0:T(128)S(1)}, u32[]{:S(2)}) copy-start(f32[128]{0:T(128)S(1)} %broadcast_multiply_fusion.2) | copy-start | bytes 1540
  271.0 23.0 %collective-permute-start.17 = (bf16[128,1024]{1,0:T(8,128)(2,1)}, bf16[128,1024]{1,0:T(8,128)(2,1)}, u32[]{:S(2)}, u32[]{:S(2)}) collective-permute-start(bf16[128,1024]{1,0:T(8,128)(2,1)} %pad_maximum_fusion.6.rest_0_), channel_id=1, source_target_pairs={{0,3},{1,2},{2,1},{3,0},{4,7},{5,6},{6,5},{7,4},{8,11},{9,10},{10,... | collective-permute-start | bytes 786440 | tf_op jit(solution)/shard_map/ppermute | solution.py:1238
  272.2 38.0 %collective-permute-start.18 = (bf16[128,1024]{1,0:T(8,128)(2,1)}, bf16[128,1024]{1,0:T(8,128)(2,1)}, u32[]{:S(2)}, u32[]{:S(2)}) collective-permute-start(bf16[128,1024]{1,0:T(8,128)(2,1)} %pad_maximum_fusion.6.rest_0_), channel_id=1, source_target_pairs={{0,16},{16,0},{1,17},{17,1},{2,18},{18,2},{3,19},{19,3},{4,20},{20... | collective-permute-start | bytes 786440 | tf_op jit(solution)/shard_map/ppermute | solution.py:1241
  274.4 38.7 %copy-start.16 = (bf16[128,1024]{1,0:T(8,128)(2,1)S(1)}, bf16[128,1024]{1,0:T(8,128)(2,1)}, u32[]{:S(2)}) copy-start(bf16[128,1024]{1,0:T(8,128)(2,1)} %get-tuple-element.185) | copy-start | bytes 786436
  292.5 28.2 %collective-permute-start.9 = (bf16[256,1024]{1,0:T(8,128)(2,1)}, bf16[256,1024]{1,0:T(8,128)(2,1)S(1)}, u32[]{:S(2)}, u32[]{:S(2)}) collective-permute-start(bf16[256,1024]{1,0:T(8,128)(2,1)} %pad_maximum_fusion.3.rest_0_), channel_id=1, source_target_pairs={{0,2},{1,3},{2,0},{3,1},{4,6},{5,7},{6,4},{7,5},{8,10},{9,11},{10,... | collective-permute-start | bytes 1572872 | tf_op jit(solution)/shard_map/ppermute | solution.py:1238
  292.6 39.1 %collective-permute-start.10 = (bf16[256,1024]{1,0:T(8,128)(2,1)}, bf16[256,1024]{1,0:T(8,128)(2,1)S(1)}, u32[]{:S(2)}, u32[]{:S(2)}) collective-permute-start(bf16[256,1024]{1,0:T(8,128)(2,1)} %pad_maximum_fusion.3.rest_0_), channel_id=1, source_target_pairs={{0,3},{1,2},{2,1},{3,0},{4,7},{5,6},{6,5},{7,4},{8,11},{9,10},{10,... | collective-permute-start | bytes 1572872 | tf_op jit(solution)/shard_map/ppermute | solution.py:1238
  294.0 66.9 %copy-start.43 = (f32[128]{0:T(128)}, f32[128]{0:T(128)S(1)}, u32[]{:S(2)}) copy-start(f32[128]{0:T(128)S(1)} %add_rsqrt_fusion) | copy-start | bytes 1540
  294.0 37.7 %collective-permute-start.5 = (bf16[128,1024]{1,0:T(8,128)(2,1)}, bf16[128,1024]{1,0:T(8,128)(2,1)S(1)}, u32[]{:S(2)}, u32[]{:S(2)}) collective-permute-start(bf16[128,1024]{1,0:T(8,128)(2,1)} %copy-done.79), channel_id=1, source_target_pairs={{0,16},{16,0},{1,17},{17,1},{2,18},{18,2},{3,19},{19,3},{4,20},{20... | collective-permute-start | bytes 786440 | tf_op jit(solution)/shard_map/ppermute | solution.py:1241
  310.2 23.0 %collective-permute-start.6 = (bf16[128,1024]{1,0:T(8,128)(2,1)}, bf16[128,1024]{1,0:T(8,128)(2,1)S(1)}, u32[]{:S(2)}, u32[]{:S(2)}) collective-permute-start(bf16[128,1024]{1,0:T(8,128)(2,1)} %copy-done.80), channel_id=1, source_target_pairs={{0,16},{16,0},{1,17},{17,1},{2,18},{18,2},{3,19},{19,3},{4,20},{20... | collective-permute-start | bytes 786440 | tf_op jit(solution)/shard_map/ppermute | solution.py:1241
  310.2 23.6 %collective-permute-start.7 = (bf16[128,1024]{1,0:T(8,128)(2,1)}, bf16[128,1024]{1,0:T(8,128)(2,1)S(1)}, u32[]{:S(2)}, u32[]{:S(2)}) collective-permute-start(bf16[128,1024]{1,0:T(8,128)(2,1)} %copy-done.81), channel_id=1, source_target_pairs={{0,16},{16,0},{1,17},{17,1},{2,18},{18,2},{3,19},{19,3},{4,20},{20... | collective-permute-start | bytes 786440 | tf_op jit(solution)/shard_map/ppermute | solution.py:1241
  313.2 83.6 %copy-start.19 = (bf16[256,1024]{1,0:T(8,128)(2,1)}, bf16[256,1024]{1,0:T(8,128)(2,1)S(1)}, u32[]{:S(2)}) copy-start(bf16[256,1024]{1,0:T(8,128)(2,1)S(1)} %pad_maximum_fusion.4.rest_0_) | copy-start | bytes 1572868
  320.7 40.2 %copy-start.66 = (bf16[256,1024]{1,0:T(8,128)(2,1)}, bf16[256,1024]{1,0:T(8,128)(2,1)S(1)}, u32[]{:S(2)}) copy-start(bf16[256,1024]{1,0:T(8,128)(2,1)S(1)} %collective-permute-done.9.rest_2_) | copy-start | bytes 1572868
  320.7 40.2 %collective-permute-start.11 = (bf16[256,1024]{1,0:T(8,128)(2,1)}, bf16[256,1024]{1,0:T(8,128)(2,1)S(1)}, u32[]{:S(2)}, u32[]{:S(2)}) collective-permute-start(bf16[256,1024]{1,0:T(8,128)(2,1)} %pad_maximum_fusion.3.rest_0_), channel_id=1, source_target_pairs={{0,16},{16,0},{1,17},{17,1},{2,18},{18,2},{3,19},{19,3},{4,20},{20... | collective-permute-start | bytes 1572872 | tf_op jit(solution)/shard_map/ppermute | solution.py:1241
  331.7 32.1 %collective-permute-start.22 = (bf16[256,1024]{1,0:T(8,128)(2,1)S(1)}, bf16[256,1024]{1,0:T(8,128)(2,1)S(1)}, u32[]{:S(2)}, u32[]{:S(2)}) collective-permute-start(bf16[256,1024]{1,0:T(8,128)(2,1)S(1)} %pad_maximum_fusion.4.rest_0_), channel_id=1, source_target_pairs={{0,1},{1,0},{2,3},{3,2},{4,5},{5,4},{6,7},{7,6},{8,9},{9,8},{10,11... | collective-permute-start | bytes 1572872 | tf_op jit(solution)/shard_map/ppermute | solution.py:1238
  331.7 32.7 %collective-permute-start.12 = (bf16[256,1024]{1,0:T(8,128)(2,1)}, bf16[256,1024]{1,0:T(8,128)(2,1)S(1)}, u32[]{:S(2)}, u32[]{:S(2)}) collective-permute-start(bf16[256,1024]{1,0:T(8,128)(2,1)} %collective-permute-done.8.rest_1_), channel_id=1, source_target_pairs={{0,16},{16,0},{1,17},{17,1},{2,18},{18,2},{3,19},{19,3},{4,20},{20... | collective-permute-start | bytes 1572872 | tf_op jit(solution)/shard_map/ppermute | solution.py:1241
  333.2 31.9 %collective-permute-start.13 = (bf16[256,1024]{1,0:T(8,128)(2,1)S(1)}, bf16[256,1024]{1,0:T(8,128)(2,1)S(1)}, u32[]{:S(2)}, u32[]{:S(2)}) collective-permute-start(bf16[256,1024]{1,0:T(8,128)(2,1)S(1)} %collective-permute-done.9.rest_2_), channel_id=1, source_target_pairs={{0,16},{16,0},{1,17},{17,1},{2,18},{18,2},{3,19},{19,3},{4,20},{20... | collective-permute-start | bytes 1572872 | tf_op jit(solution)/shard_map/ppermute | solution.py:1241
  333.8 33.6 %collective-permute-start.14 = (bf16[256,1024]{1,0:T(8,128)(2,1)S(1)}, bf16[256,1024]{1,0:T(8,128)(2,1)S(1)}, u32[]{:S(2)}, u32[]{:S(2)}) collective-permute-start(bf16[256,1024]{1,0:T(8,128)(2,1)S(1)} %collective-permute-done.10.rest_3_), channel_id=1, source_target_pairs={{0,16},{16,0},{1,17},{17,1},{2,18},{18,2},{3,19},{19,3},{4,20},{20... | collective-permute-start | bytes 1572872 | tf_op jit(solution)/shard_map/ppermute | solution.py:1241
  361.0 35.9 %collective-permute-start.23 = (bf16[256,1024]{1,0:T(8,128)(2,1)S(1)}, bf16[256,1024]{1,0:T(8,128)(2,1)S(1)}, u32[]{:S(2)}, u32[]{:S(2)}) collective-permute-start(bf16[256,1024]{1,0:T(8,128)(2,1)S(1)} %pad_maximum_fusion.4.rest_0_), channel_id=1, source_target_pairs={{0,2},{1,3},{2,0},{3,1},{4,6},{5,7},{6,4},{7,5},{8,10},{9,11},{10,... | collective-permute-start | bytes 1572872 | tf_op jit(solution)/shard_map/ppermute | solution.py:1238
  363.8 45.4 %copy-start.72 = (bf16[256,1024]{1,0:T(8,128)(2,1)}, bf16[256,1024]{1,0:T(8,128)(2,1)S(1)}, u32[]{:S(2)}) copy-start(bf16[256,1024]{1,0:T(8,128)(2,1)S(1)} %collective-permute-done.22.rest_1_) | copy-start | bytes 1572868
  363.8 45.4 %collective-permute-start.24 = (bf16[256,1024]{1,0:T(8,128)(2,1)S(1)}, bf16[256,1024]{1,0:T(8,128)(2,1)S(1)}, u32[]{:S(2)}, u32[]{:S(2)}) collective-permute-start(bf16[256,1024]{1,0:T(8,128)(2,1)S(1)} %pad_maximum_fusion.4.rest_0_), channel_id=1, source_target_pairs={{0,3},{1,2},{2,1},{3,0},{4,7},{5,6},{6,5},{7,4},{8,11},{9,10},{10,... | collective-permute-start | bytes 1572872 | tf_op jit(solution)/shard_map/ppermute | solution.py:1238
  364.4 45.5 %collective-permute-start.19 = (bf16[128,1024]{1,0:T(8,128)(2,1)}, bf16[128,1024]{1,0:T(8,128)(2,1)S(1)}, u32[]{:S(2)}, u32[]{:S(2)}) collective-permute-start(bf16[128,1024]{1,0:T(8,128)(2,1)} %collective-permute-done.15.rest_1_), channel_id=1, source_target_pairs={{0,16},{16,0},{1,17},{17,1},{2,18},{18,2},{3,19},{19,3},{4,20},{20... | collective-permute-start | bytes 786440 | tf_op jit(solution)/shard_map/ppermute | solution.py:1241
  365.1 46.1 %collective-permute-start.20 = (bf16[128,1024]{1,0:T(8,128)(2,1)}, bf16[128,1024]{1,0:T(8,128)(2,1)S(1)}, u32[]{:S(2)}, u32[]{:S(2)}) collective-permute-start(bf16[128,1024]{1,0:T(8,128)(2,1)} %collective-permute-done.16.rest_2_), channel_id=1, source_target_pairs={{0,16},{16,0},{1,17},{17,1},{2,18},{18,2},{3,19},{19,3},{4,20},{20... | collective-permute-start | bytes 786440 | tf_op jit(solution)/shard_map/ppermute | solution.py:1241
  367.4 44.6 %collective-permute-start.21 = (bf16[128,1024]{1,0:T(8,128)(2,1)}, bf16[128,1024]{1,0:T(8,128)(2,1)S(1)}, u32[]{:S(2)}, u32[]{:S(2)}) collective-permute-start(bf16[128,1024]{1,0:T(8,128)(2,1)} %collective-permute-done.17.rest_3_), channel_id=1, source_target_pairs={{0,16},{16,0},{1,17},{17,1},{2,18},{18,2},{3,19},{19,3},{4,20},{20... | collective-permute-start | bytes 786440 | tf_op jit(solution)/shard_map/ppermute | solution.py:1241
  396.8 41.9 %copy-start.73 = (bf16[256,1024]{1,0:T(8,128)(2,1)}, bf16[256,1024]{1,0:T(8,128)(2,1)S(1)}, u32[]{:S(2)}) copy-start(bf16[256,1024]{1,0:T(8,128)(2,1)S(1)} %collective-permute-done.23.rest_2_) | copy-start | bytes 1572868
  396.8 41.9 %collective-permute-start.25 = (bf16[256,1024]{1,0:T(8,128)(2,1)S(1)}, bf16[256,1024]{1,0:T(8,128)(2,1)S(1)}, u32[]{:S(2)}, u32[]{:S(2)}) collective-permute-start(bf16[256,1024]{1,0:T(8,128)(2,1)S(1)} %pad_maximum_fusion.4.rest_0_), channel_id=1, source_target_pairs={{0,16},{16,0},{1,17},{17,1},{2,18},{18,2},{3,19},{19,3},{4,20},{20... | collective-permute-start | bytes 1572872 | tf_op jit(solution)/shard_map/ppermute | solution.py:1241
  409.2 29.5 %copy-start.74 = (bf16[256,1024]{1,0:T(8,128)(2,1)}, bf16[256,1024]{1,0:T(8,128)(2,1)S(1)}, u32[]{:S(2)}) copy-start(bf16[256,1024]{1,0:T(8,128)(2,1)S(1)} %collective-permute-done.24.rest_3_) | copy-start | bytes 1572868
  409.2 29.5 %collective-permute-start.26 = (bf16[256,1024]{1,0:T(8,128)(2,1)S(1)}, bf16[256,1024]{1,0:T(8,128)(2,1)S(1)}, u32[]{:S(2)}, u32[]{:S(2)}) collective-permute-start(bf16[256,1024]{1,0:T(8,128)(2,1)S(1)} %collective-permute-done.22.rest_1_), channel_id=1, source_target_pairs={{0,16},{16,0},{1,17},{17,1},{2,18},{18,2},{3,19},{19,3},{4,20},{20... | collective-permute-start | bytes 1572872 | tf_op jit(solution)/shard_map/ppermute | solution.py:1241
  410.0 28.8 %collective-permute-start.27 = (bf16[256,1024]{1,0:T(8,128)(2,1)S(1)}, bf16[256,1024]{1,0:T(8,128)(2,1)S(1)}, u32[]{:S(2)}, u32[]{:S(2)}) collective-permute-start(bf16[256,1024]{1,0:T(8,128)(2,1)S(1)} %collective-permute-done.23.rest_2_), channel_id=1, source_target_pairs={{0,16},{16,0},{1,17},{17,1},{2,18},{18,2},{3,19},{19,3},{4,20},{20... | collective-permute-start | bytes 1572872 | tf_op jit(solution)/shard_map/ppermute | solution.py:1241
  411.2 34.3 %collective-permute-start.28 = (bf16[256,1024]{1,0:T(8,128)(2,1)S(1)}, bf16[256,1024]{1,0:T(8,128)(2,1)S(1)}, u32[]{:S(2)}, u32[]{:S(2)}) collective-permute-start(bf16[256,1024]{1,0:T(8,128)(2,1)S(1)} %collective-permute-done.24.rest_3_), channel_id=1, source_target_pairs={{0,16},{16,0},{1,17},{17,1},{2,18},{18,2},{3,19},{19,3},{4,20},{20... | collective-permute-start | bytes 1572872 | tf_op jit(solution)/shard_map/ppermute | solution.py:1241
  553.3 30.8 %copy-start.4 = (f32[128,1024]{1,0:T(8,128)S(1)}, f32[128,1024]{1,0:T(8,128)}, u32[]{:S(2)}) copy-start(f32[128,1024]{1,0:T(8,128)} %copy-done.3) | copy-start | bytes 1572868
  612.1 161.2 %collective-permute-start.37 = (bf16[4,256,1024]{2,1,0:T(8,128)(2,1)}, bf16[4,256,1024]{2,1,0:T(8,128)(2,1)}, u32[]{:S(2)}, u32[]{:S(2)}) collective-permute-start(bf16[4,256,1024]{2,1,0:T(8,128)(2,1)} %slice_bitcast_fusion.1), channel_id=1, source_target_pairs={{0,16},{16,0},{1,17},{17,1},{2,18},{18,2},{3,19},{19,3},{4,20},{20... | collective-permute-start | bytes 6291464 | tf_op jit(solution)/shard_map/ppermute | solution.py:1249
  616.3 115.9 %collective-permute-start.33 = (bf16[4,128,1024]{2,1,0:T(8,128)(2,1)}, bf16[4,128,1024]{2,1,0:T(8,128)(2,1)}, u32[]{:S(2)}, u32[]{:S(2)}) collective-permute-start(bf16[4,128,1024]{2,1,0:T(8,128)(2,1)} %slice_bitcast_fusion.5), channel_id=1, source_target_pairs={{0,16},{16,0},{1,17},{17,1},{2,18},{18,2},{3,19},{19,3},{4,20},{20... | collective-permute-start | bytes 3145736 | tf_op jit(solution)/shard_map/ppermute | solution.py:1249
  618.6 117.0 %collective-permute-start.41 = (bf16[4,128,1024]{2,1,0:T(8,128)(2,1)}, bf16[4,128,1024]{2,1,0:T(8,128)(2,1)}, u32[]{:S(2)}, u32[]{:S(2)}) collective-permute-start(bf16[4,128,1024]{2,1,0:T(8,128)(2,1)} %slice_bitcast_fusion.4), channel_id=1, source_target_pairs={{0,16},{16,0},{1,17},{17,1},{2,18},{18,2},{3,19},{19,3},{4,20},{20... | collective-permute-start | bytes 3145736 | tf_op jit(solution)/shard_map/ppermute | solution.py:1249
  646.0 84.3 %collective-permute-start.31 = (f32[128,1024]{1,0:T(8,128)}, f32[128,1024]{1,0:T(8,128)}, u32[]{:S(2)}, u32[]{:S(2)}) collective-permute-start(f32[128,1024]{1,0:T(8,128)} %get-tuple-element.140), channel_id=1, source_target_pairs={{0,0},{1,4},{2,8},{3,12},{4,1},{5,5},{6,9},{7,13},{8,2},{9,6},{10,... | collective-permute-start | bytes 1572872 | tf_op jit(solution)/shard_map/ppermute | solution.py:1506
  713.6 15.5 %collective-permute-start.29 = (f32[128,32]{0,1:T(8,128)S(1)}, f32[128,32]{0,1:T(8,128)S(1)}, u32[]{:S(2)}, u32[]{:S(2)}) collective-permute-start(f32[128,32]{0,1:T(8,128)S(1)} %convolution_add_fusion), channel_id=1, source_target_pairs={{0,0},{1,4},{2,8},{3,12},{4,1},{5,5},{6,9},{7,13},{8,2},{9,6},{10,... | collective-permute-start | bytes 49160 | tf_op jit(solution)/shard_map/ppermute | solution.py:1425
  729.1 50.0 %collective-permute-start.45 = (bf16[4,256,1024]{2,1,0:T(8,128)(2,1)}, bf16[4,256,1024]{2,1,0:T(8,128)(2,1)S(1)}, u32[]{:S(2)}, u32[]{:S(2)}) collective-permute-start(bf16[4,256,1024]{2,1,0:T(8,128)(2,1)} %slice_bitcast_fusion), channel_id=1, source_target_pairs={{0,16},{16,0},{1,17},{17,1},{2,18},{18,2},{3,19},{19,3},{4,20},{20... | collective-permute-start | bytes 6291464 | tf_op jit(solution)/shard_map/ppermute | solution.py:1249
  734.4 9.9 %collective-permute-start.34 = (bf16[128,1024]{1,0:T(8,128)(2,1)S(1)}, bf16[128,1024]{1,0:T(8,128)(2,1)S(1)}, u32[]{:S(2)}, u32[]{:S(2)}) collective-permute-start(bf16[128,1024]{1,0:T(8,128)(2,1)S(1)} %get-tuple-element.175), channel_id=1, source_target_pairs={{0,1},{1,0},{2,3},{3,2},{4,5},{5,4},{6,7},{7,6},{8,9},{9,8},{10,11... | collective-permute-start | bytes 786440 | tf_op jit(solution)/shard_map/ppermute | solution.py:1253
  735.7 17.2 %collective-permute-start.35 = (bf16[128,1024]{1,0:T(8,128)(2,1)S(1)}, bf16[128,1024]{1,0:T(8,128)(2,1)S(1)}, u32[]{:S(2)}, u32[]{:S(2)}) collective-permute-start(bf16[128,1024]{1,0:T(8,128)(2,1)S(1)} %get-tuple-element.177), channel_id=1, source_target_pairs={{0,2},{1,3},{2,0},{3,1},{4,6},{5,7},{6,4},{7,5},{8,10},{9,11},{10,... | collective-permute-start | bytes 786440 | tf_op jit(solution)/shard_map/ppermute | solution.py:1253
  735.7 37.4 %collective-permute-start.36 = (bf16[128,1024]{1,0:T(8,128)(2,1)S(1)}, bf16[128,1024]{1,0:T(8,128)(2,1)S(1)}, u32[]{:S(2)}, u32[]{:S(2)}) collective-permute-start(bf16[128,1024]{1,0:T(8,128)(2,1)S(1)} %get-tuple-element.176), channel_id=1, source_target_pairs={{0,3},{1,2},{2,1},{3,0},{4,7},{5,6},{6,5},{7,4},{8,11},{9,10},{10,... | collective-permute-start | bytes 786440 | tf_op jit(solution)/shard_map/ppermute | solution.py:1253
  738.0 35.3 %copy-start.7 = (bf16[2,4,256,1024]{3,2,1,0:T(8,128)(2,1)S(1)}, bf16[2,4,256,1024]{3,2,1,0:T(8,128)(2,1)}, u32[]{:S(2)}) copy-start(bf16[2,4,256,1024]{3,2,1,0:T(8,128)(2,1)} %get-tuple-element.110) | copy-start | bytes 12582916
  744.4 41.4 %collective-permute-start.42 = (bf16[128,1024]{1,0:T(8,128)(2,1)S(1)}, bf16[128,1024]{1,0:T(8,128)(2,1)S(1)}, u32[]{:S(2)}, u32[]{:S(2)}) collective-permute-start(bf16[128,1024]{1,0:T(8,128)(2,1)S(1)} %get-tuple-element.178), channel_id=1, source_target_pairs={{0,1},{1,0},{2,3},{3,2},{4,5},{5,4},{6,7},{7,6},{8,9},{9,8},{10,11... | collective-permute-start | bytes 786440 | tf_op jit(solution)/shard_map/ppermute | solution.py:1253
  752.9 34.0 %collective-permute-start.43 = (bf16[128,1024]{1,0:T(8,128)(2,1)S(1)}, bf16[128,1024]{1,0:T(8,128)(2,1)S(1)}, u32[]{:S(2)}, u32[]{:S(2)}) collective-permute-start(bf16[128,1024]{1,0:T(8,128)(2,1)S(1)} %get-tuple-element.180), channel_id=1, source_target_pairs={{0,2},{1,3},{2,0},{3,1},{4,6},{5,7},{6,4},{7,5},{8,10},{9,11},{10,... | collective-permute-start | bytes 786440 | tf_op jit(solution)/shard_map/ppermute | solution.py:1253
  773.1 15.3 %collective-permute-start.44 = (bf16[128,1024]{1,0:T(8,128)(2,1)S(1)}, bf16[128,1024]{1,0:T(8,128)(2,1)S(1)}, u32[]{:S(2)}, u32[]{:S(2)}) collective-permute-start(bf16[128,1024]{1,0:T(8,128)(2,1)S(1)} %get-tuple-element.179), channel_id=1, source_target_pairs={{0,3},{1,2},{2,1},{3,0},{4,7},{5,6},{6,5},{7,4},{8,11},{9,10},{10,... | collective-permute-start | bytes 786440 | tf_op jit(solution)/shard_map/ppermute | solution.py:1253
  779.1 23.1 %collective-permute-start.38 = (bf16[256,1024]{1,0:T(8,128)(2,1)S(1)}, bf16[256,1024]{1,0:T(8,128)(2,1)S(1)}, u32[]{:S(2)}, u32[]{:S(2)}) collective-permute-start(bf16[256,1024]{1,0:T(8,128)(2,1)S(1)} %get-tuple-element.159), channel_id=1, source_target_pairs={{0,1},{1,0},{2,3},{3,2},{4,5},{5,4},{6,7},{7,6},{8,9},{9,8},{10,11... | collective-permute-start | bytes 1572872 | tf_op jit(solution)/shard_map/ppermute | solution.py:1253
  779.1 38.4 %collective-permute-start.39 = (bf16[256,1024]{1,0:T(8,128)(2,1)}, bf16[256,1024]{1,0:T(8,128)(2,1)S(1)}, u32[]{:S(2)}, u32[]{:S(2)}) collective-permute-start(bf16[256,1024]{1,0:T(8,128)(2,1)} %get-tuple-element.161), channel_id=1, source_target_pairs={{0,2},{1,3},{2,0},{3,1},{4,6},{5,7},{6,4},{7,5},{8,10},{9,11},{10,... | collective-permute-start | bytes 1572872 | tf_op jit(solution)/shard_map/ppermute | solution.py:1253
  785.8 66.1 %collective-permute-start.40 = (bf16[256,1024]{1,0:T(8,128)(2,1)S(1)}, bf16[256,1024]{1,0:T(8,128)(2,1)S(1)}, u32[]{:S(2)}, u32[]{:S(2)}) collective-permute-start(bf16[256,1024]{1,0:T(8,128)(2,1)S(1)} %get-tuple-element.160), channel_id=1, source_target_pairs={{0,3},{1,2},{2,1},{3,0},{4,7},{5,6},{6,5},{7,4},{8,11},{9,10},{10,... | collective-permute-start | bytes 1572872 | tf_op jit(solution)/shard_map/ppermute | solution.py:1253
  787.0 66.5 %collective-permute-start.46 = (bf16[256,1024]{1,0:T(8,128)(2,1)}, bf16[256,1024]{1,0:T(8,128)(2,1)S(1)}, u32[]{:S(2)}, u32[]{:S(2)}) collective-permute-start(bf16[256,1024]{1,0:T(8,128)(2,1)} %get-tuple-element.162), channel_id=1, source_target_pairs={{0,1},{1,0},{2,3},{3,2},{4,5},{5,4},{6,7},{7,6},{8,9},{9,8},{10,11... | collective-permute-start | bytes 1572872 | tf_op jit(solution)/shard_map/ppermute | solution.py:1253
  788.4 74.1 %collective-permute-start.47 = (bf16[256,1024]{1,0:T(8,128)(2,1)}, bf16[256,1024]{1,0:T(8,128)(2,1)}, u32[]{:S(2)}, u32[]{:S(2)}) collective-permute-start(bf16[256,1024]{1,0:T(8,128)(2,1)} %get-tuple-element.164), channel_id=1, source_target_pairs={{0,2},{1,3},{2,0},{3,1},{4,6},{5,7},{6,4},{7,5},{8,10},{9,11},{10,... | collective-permute-start | bytes 1572872 | tf_op jit(solution)/shard_map/ppermute | solution.py:1253
  802.1 70.3 %collective-permute-start.48 = (bf16[256,1024]{1,0:T(8,128)(2,1)}, bf16[256,1024]{1,0:T(8,128)(2,1)}, u32[]{:S(2)}, u32[]{:S(2)}) collective-permute-start(bf16[256,1024]{1,0:T(8,128)(2,1)} %get-tuple-element.163), channel_id=1, source_target_pairs={{0,3},{1,2},{2,1},{3,0},{4,7},{5,6},{6,5},{7,4},{8,11},{9,10},{10,... | collective-permute-start | bytes 1572872 | tf_op jit(solution)/shard_map/ppermute | solution.py:1253
  875.4 16.7 %all-to-all-start.1 = ((bf16[4,2,32,1792]{3,2,1,0:T(8,128)(2,1)}), bf16[4,2,32,1792]{3,2,1,0:T(8,128)(2,1)S(1)}, u32[]{:S(2)}, u32[]{:S(2)}) async-start(bf16[4,2,32,1792]{3,2,1,0:T(8,128)(2,1)} %pad_maximum_fusion.2), calls=%async_computation.1 | async-start | bytes 1835008 | tf_op jit(solution)/shard_map/all_to_all | solution.py:1528
  (78 other events, 749.1 us)

commit v2 on v0

--- a/solution.py
+++ b/solution.py
@@ -1,8 +1,11 @@
+import itertools
 import math
 
 import jax
 import jax.numpy as jnp
 from jax import lax
+from jax.experimental import pallas as pl
+from jax.experimental.pallas import tpu as pltpu
 from jax.sharding import PartitionSpec as P
 
 HEADS = 16
@@ -537,56 +540,1292 @@
     )
 
 
-def solution(mesh):
+MESH_ID = pl.DeviceIdType.MESH
+IN_VMEM = pl.BlockSpec(memory_space=pltpu.VMEM)
+ANYWHERE = pl.BlockSpec(memory_space=pl.ANY)
+AXES = ("y", "x", "c", "h", "l")
+PACK = 8
+RANKS = 4
+
+
+def kernel_params(collective=None):
+    if collective is None:
+        return pltpu.CompilerParams(vmem_limit_bytes=56 * 2**20)
+    return pltpu.CompilerParams(
+        vmem_limit_bytes=56 * 2**20, collective_id=collective, has_side_effects=True
+    )
+
+
+def cost(micros):
+    return pl.CostEstimate(flops=int(micros * 1.1e9), bytes_accessed=2**20, transcendentals=0)
+
+
+def greet(peers):
+    gate = pltpu.get_barrier_semaphore()
+    for peer in peers:
+        pl.semaphore_signal(gate, inc=1, device_id=peer, device_id_type=MESH_ID)
+    pl.semaphore_wait(gate, len(peers))
+
+
+def remote(source, target, send, receive, peer):
+    return pltpu.make_async_remote_copy(
+        source, target, send, receive, device_id=peer, device_id_type=MESH_ID
+    )
+
+
+def bits():
+    return tuple(lax.axis_index(axis) for axis in AXES)
+
+
+def index_of(y, x, c, h, l):
+    return y * 16 + x * 8 + c * 4 + h * 2 + l
+
+
+def turned_of(y, x, c, h, l):
+    return index_of(y, h, c, x, l)
+
+
+def group_of(y, x, c, h, l):
+    return index_of(y, x, c, h, l) // 2
+
+
+def flipped(mask):
+    return {
+        axis: 1 - lax.axis_index(axis)
+        for number, axis in enumerate(AXES)
+        if mask >> (len(AXES) - 1 - number) & 1
+    }
+
+
+def swap_all(collective, payloads):
+    count = len(payloads)
+    total = 2 ** len(AXES)
+
+    def shape_of(array, kind):
+        if kind == "group" or kind == "twist":
+            return array.shape
+        return (total,) + array.shape[1:]
+
+    def kernel(*refs):
+        sources, targets = refs[:count], refs[count : 2 * count]
+        sends, receives, own_sems = refs[2 * count :]
+        y, x, c, h, l = bits()
+        me = index_of(y, x, c, h, l)
+        t = x * 2 + l
+        peers = [flipped(mask) for mask in range(1, total)]
+        greet(peers)
+        copies = []
+        for p, (_, kind) in enumerate(payloads):
+            if kind == "twist":
+
+                @pl.when(h == l)
+                def _(p=p):
+                    pltpu.make_async_copy(sources[p], targets[p], own_sems.at[p]).start()
+
+                @pl.when(h != l)
+                def _(p=p):
+                    remote(
+                        sources[p], targets[p], sends.at[p, 0], receives.at[p, 0], flipped(3)
+                    ).start()
+
+                continue
+            own = sources[p].at[t] if kind == "group" else sources[p].at[kind(y, x, c, h, l)]
+            slot = t if kind == "group" else me
+            copy = pltpu.make_async_copy(own, targets[p].at[slot], own_sems.at[p])
+            copy.start()
+            copies.append(copy)
+            masks = (1, 8, 9) if kind == "group" else range(1, total)
+            for number, mask in enumerate(masks):
+                peer = flipped(mask)
+                place = [peer.get(axis, here) for axis, here in zip(AXES, (y, x, c, h, l))]
+                wanted = place[1] * 2 + place[4] if kind == "group" else kind(*place)
+                copy = remote(
+                    sources[p].at[wanted],
+                    targets[p].at[slot],
+                    sends.at[p, number],
+                    receives.at[p, number],
+                    peer,
+                )
+                copy.start()
+                copies.append(copy)
+        for copy in copies:
+            copy.wait()
+        for p, (_, kind) in enumerate(payloads):
+            if kind == "twist":
+
+                @pl.when(h == l)
+                def _(p=p):
+                    pltpu.make_async_copy(sources[p], targets[p], own_sems.at[p]).wait()
+
+                @pl.when(h != l)
+                def _(p=p):
+                    remote(
+                        sources[p], targets[p], sends.at[p, 0], receives.at[p, 0], flipped(3)
+                    ).wait()
+
+    return pl.pallas_call(
+        kernel,
+        out_shape=[
+            jax.ShapeDtypeStruct(shape_of(array, kind), array.dtype) for array, kind in payloads
+        ],
+        in_specs=[ANYWHERE] * count,
+        out_specs=[ANYWHERE] * count,
+        scratch_shapes=[
+            pltpu.SemaphoreType.DMA((count, total - 1)),
+            pltpu.SemaphoreType.DMA((count, total - 1)),
+            pltpu.SemaphoreType.DMA((count,)),
+        ],
+        compiler_params=kernel_params(collective),
+        cost_estimate=cost(20),
+    )(*[array for array, _ in payloads])
+
+
+def rank_lanes(bounds_ref, rows, width):
+    lanes = PACK * width
+    line = lax.broadcasted_iota(jnp.int32, (rows, lanes), 0) // PACK
+    lane = lax.broadcasted_iota(jnp.int32, (rows, lanes), 1) // width
+    frame = line * PACK + lane
+    rank = jnp.zeros((rows, lanes), jnp.int32)
+    for slot in range(bounds_ref.shape[1]):
+        rank = rank + (frame >= bounds_ref[:, slot : slot + 1]).astype(jnp.int32)
+    return rank
+
+
+def spread_ranks(wide, packed, rank, first):
+    rows = packed.shape[0]
+    wide[...] = jnp.zeros_like(wide)
+    for number in range(RANKS):
+        place = pl.ds(first + number * 64, rows)
+        wide[place, :] += jnp.where(rank == number, packed, 0.0)
+
+
+def collect_ranks(summed, rank, rows):
+    result = jnp.zeros((rows, summed.shape[1]), jnp.float32)
+    for number in range(RANKS):
+        result = jnp.where(rank == number, summed[number * 64 : number * 64 + rows, :], result)
+    return result
+
+
+def toeplitz(even, odd, taps, length):
+    total = None
+    for step in range(taps.shape[0]):
+        source = even if step % 2 == 0 else odd
+        part = jnp.dot(
+            source[pl.ds((step - step % 2) * 8, length), :],
+            taps[step],
+            preferred_element_type=jnp.float32,
+        )
+        total = part if total is None else total + part
+    return total
+
+
+def fill_pair(wide, even, odd):
+    length = even.shape[0]
+    even[...] = wide[:length, :].astype(jnp.bfloat16)
+    odd[...] = wide[8 : 8 + length, :].astype(jnp.bfloat16)
+
+
+def conv_forward_packed(packed, bounds, taps, bias):
+    rows = packed.shape[0]
+    length = rows + (RANKS - 1) * 64
+    held = length + 128
+    steps, depth, width = taps.shape
+
+    def kernel(x_ref, b_ref, k_ref, bias_ref, o_ref, even, odd, wide):
+        rank = rank_lanes(b_ref, rows, depth // PACK)
+        spread_ranks(wide, x_ref[...].astype(jnp.float32), rank, 64)
+        fill_pair(wide, even, odd)
+        summed = toeplitz(even, odd, k_ref, length)
+        rank_out = rank_lanes(b_ref, rows, width // PACK)
+        o_ref[...] = (collect_ranks(summed, rank_out, rows) + bias_ref[...]).astype(jnp.bfloat16)
+
+    return pl.pallas_call(
+        kernel,
+        out_shape=[
+            jax.ShapeDtypeStruct((rows, width), jnp.bfloat16),
+            jax.ShapeDtypeStruct((held, depth), jnp.bfloat16),
+            jax.ShapeDtypeStruct((held, depth), jnp.bfloat16),
+        ],
+        in_specs=[IN_VMEM] * 4,
+        out_specs=[IN_VMEM] * 3,
+        scratch_shapes=[pltpu.VMEM((held + 16, depth), jnp.float32)],
+        compiler_params=kernel_params(),
+        cost_estimate=cost(10),
+    )(packed, bounds, taps, bias)
+
+
+def conv_backward_packed(packed, own, bounds, taps, even, odd):
+    rows, depth = packed.shape
+    length = rows + (RANKS - 1) * 64
+    held = length + 128
+    steps, _, width = taps.shape
+    tap_count = (steps - 1) * PACK
+    group_width = depth // PACK
+    chans = width // PACK
+
+    def kernel(g_ref, own_ref, b_ref, k_ref, even_ref, odd_ref, o_ref, w_ref, s_ref, ge, go, wide, turned):
+        rank = rank_lanes(b_ref, rows, depth // PACK)
+        spread_ranks(wide, g_ref[...].astype(jnp.float32), rank, 64)
+        fill_pair(wide, ge, go)
+        summed = toeplitz(ge, go, k_ref, length)
+        rank_out = rank_lanes(b_ref, rows, width // PACK)
+        o_ref[...] = collect_ranks(summed, rank_out, rows).astype(jnp.bfloat16)
+        own_wide = own_ref[...].astype(jnp.float32)
+        s_ref[...] = jnp.sum(own_wide, axis=0, keepdims=True)
+        spread_ranks(wide.at[:length, :width], own_wide, rank_out, 0)
+        across = wide[:length, :width].T.astype(jnp.bfloat16)
+        for step in range(steps):
+            source = even_ref if step % 2 == 0 else odd_ref
+            turned[:, pl.ds(step * depth, depth)] = jnp.dot(
+                across,
+                source[pl.ds((step - step % 2) * 8, length), :],
+                preferred_element_type=jnp.float32,
+            )
+        total = turned[0:chans, 0 : tap_count * group_width]
+        for f in range(1, PACK):
+            total = total + turned[
+                f * chans : (f + 1) * chans,
+                f * group_width : f * group_width + tap_count * group_width,
+            ]
+        w_ref[...] = total
+
+    return pl.pallas_call(
+        kernel,
+        out_shape=[
+            jax.ShapeDtypeStruct((rows, width), jnp.bfloat16),
+            jax.ShapeDtypeStruct((chans, tap_count * group_width), jnp.float32),
+            jax.ShapeDtypeStruct((1, width), jnp.float32),
+        ],
+        in_specs=[IN_VMEM] * 6,
+        out_specs=[IN_VMEM] * 3,
+        scratch_shapes=[
+            pltpu.VMEM((held, depth), jnp.bfloat16),
+            pltpu.VMEM((held, depth), jnp.bfloat16),
+            pltpu.VMEM((held + 16, depth), jnp.float32),
+            pltpu.VMEM((width, steps * depth), jnp.float32),
+        ],
+        compiler_params=kernel_params(),
+        cost_estimate=cost(15),
+    )(packed, own, bounds, taps, even, odd)
+
+
+def shifted_taps(grid):
+    taps, depth, width = grid.shape
+    steps = 17
+    room = steps * PACK
+    parts = [
+        jnp.pad(grid, ((f, room - taps - f), (0, 0), (0, 0))).reshape(room * depth, width)
+        for f in range(PACK)
+    ]
+    return jnp.concatenate(parts, axis=1).reshape(steps, PACK * depth, PACK * width)
+
+
+def normed(tensor, gain, shift):
+    average = jnp.mean(tensor, axis=-1, keepdims=True)
+    centred = tensor - average
+    spread = jnp.mean(centred * centred, axis=-1, keepdims=True)
+    return centred * lax.rsqrt(spread + epsilon) * gain + shift
+
+
+def normed_back(tensor, gain, upstream):
+    average = jnp.mean(tensor, axis=-1, keepdims=True)
+    centred = tensor - average
+    spread = jnp.mean(centred * centred, axis=-1, keepdims=True)
+    inverse = lax.rsqrt(spread + epsilon)
+    unit = centred * inverse
+    scaled = upstream * gain
+    result = inverse * (
+        scaled
+        - jnp.mean(scaled, axis=-1, keepdims=True)
+        - unit * jnp.mean(scaled * unit, axis=-1, keepdims=True)
+    )
+    return (
+        result,
+        jnp.sum(upstream * unit, axis=0, keepdims=True),
+        jnp.sum(upstream, axis=0, keepdims=True),
+    )
+
+
+def gelu_pair(tensor):
+    half = 0.5 * (1.0 + lax.erf(tensor * (2.0**-0.5)))
+    slope = half + tensor * (jnp.exp(-0.5 * tensor * tensor) * ((2.0 * math.pi) ** -0.5))
+    return tensor * half, slope
+
+
+def dot(left, right):
+    return jnp.dot(left, right, preferred_element_type=jnp.float32)
+
+
+def dot_rt(left, right):
+    return lax.dot_general(left, right, (((1,), (1,)), ((), ())), preferred_element_type=jnp.float32)
+
+
+def dot_lt(left, right):
+    return lax.dot_general(left, right, (((0,), (0,)), ((), ())), preferred_element_type=jnp.float32)
+
+
+X_BIT, L_BIT = 8, 1
+H_BIT, Y_BIT, C_BIT = 2, 16, 4
+PIECES = 8
+
+
+def group_gather(block, t, sends, receives):
+    half = block.shape[1] // 2
+    x_peer, l_peer = flipped(X_BIT), flipped(L_BIT)
+    own = block.at[t]
+    to_x = remote(own, own, sends.at[0], receives.at[0], x_peer)
+    to_x.start()
+    to_l = remote(own, own, sends.at[1], receives.at[1], l_peer)
+    to_l.start()
+    to_x.wait_recv()
+    other = block.at[lax.bitwise_xor(t, 2), pl.ds(0, half)]
+    on_l = remote(other, other, sends.at[2], receives.at[2], l_peer)
+    on_l.start()
+    to_l.wait_recv()
+    other = block.at[lax.bitwise_xor(t, 1), pl.ds(half, half)]
+    on_x = remote(other, other, sends.at[3], receives.at[3], x_peer)
+    on_x.start()
+    on_l.wait_recv()
+    on_x.wait_recv()
+    for copy in (to_x, to_l, on_l, on_x):
+        copy.wait_send()
+
+
+def group_scatter(part, t, low, got, sends, receives, between=None):
+    half = low.shape[1]
+    x_peer, l_peer = flipped(X_BIT), flipped(L_BIT)
+
+    def send(slot, value, peer):
+        low[slot] = value.astype(jnp.bfloat16)
+        copy = remote(low.at[slot], got.at[slot], sends.at[slot], receives.at[slot], peer)
+        copy.start()
+        return copy
+
+    def arrived(slot):
+        return got[slot].astype(jnp.float32)
+
+    far = part(lax.bitwise_xor(t, 3))
+    far_x = send(0, far[:half], x_peer)
+    far_l = send(1, far[half:], l_peer)
+    beside_x = part(lax.bitwise_xor(t, 2))
+    near_x = send(2, beside_x[:half], x_peer)
+    beside_l = part(lax.bitwise_xor(t, 1))
+    near_l = send(3, beside_l[half:], l_peer)
+    far_x.wait_recv()
+    on_l = send(4, beside_l[:half] + arrived(0), l_peer)
+    far_l.wait_recv()
+    on_x = send(5, beside_x[half:] + arrived(1), x_peer)
+    own = part(t)
+    if between is not None:
+        between()
+    near_x.wait_recv()
+    near_l.wait_recv()
+    on_l.wait_recv()
+    on_x.wait_recv()
+    result = jnp.concatenate(
+        [own[:half] + arrived(2) + arrived(4), own[half:] + arrived(3) + arrived(5)], axis=0
+    )
+    for copy in (far_x, far_l, near_x, near_l, on_l, on_x):
+        copy.wait_send()
+    return result
+
+
+def group_scratch(n, width):
+    return [
+        pltpu.VMEM((6, n // 2, width), jnp.bfloat16),
+        pltpu.VMEM((6, n // 2, width), jnp.bfloat16),
+        pltpu.SemaphoreType.DMA((4,)),
+        pltpu.SemaphoreType.DMA((4,)),
+        pltpu.SemaphoreType.DMA((6,)),
+        pltpu.SemaphoreType.DMA((6,)),
+    ]
+
+
+class Spread:
+    def __init__(self, own, held, sends, receives, own_sem):
+        self.own, self.held = own, held
+        self.sends, self.receives, self.own_sem = sends, receives, own_sem
+        y, _, c, h, _ = bits()
+        self.me = c * 4 + y * 2 + h
+        self.pair = c * 4 + y * 2
+        self.four = c * 4
+
+    def copy(self, step):
+        pair, four = self.held.at[pl.ds(self.pair, 2)], self.held.at[pl.ds(self.four, 4)]
+        source = (self.own, pair, four)[step]
+        target = (self.held.at[self.me], pair, four)[step]
+        peer = flipped((H_BIT, Y_BIT, C_BIT)[step])
+        return remote(source, target, self.sends.at[step], self.receives.at[step], peer)
+
+    def over_h(self):
+        pltpu.make_async_copy(self.own, self.held.at[self.me], self.own_sem).start()
+        self.copy(0).start()
+
+    def over_y(self):
+        pltpu.make_async_copy(self.own, self.held.at[self.me], self.own_sem).wait()
+        self.copy(0).wait_recv()
+        self.copy(1).start()
+
+    def over_c(self):
+        self.copy(1).wait_recv()
+        self.copy(2).start()
+
+    def done(self):
+        for step in range(3):
+            self.copy(step).wait_send()
+        self.copy(2).wait_recv()
+
+
+def slots():
+    return [(c, y, h) for c in range(2) for y in range(2) for h in range(2)]
+
+
+def load_rows(held, target, sem, share, column, width):
+    for slot, (c, y, h) in enumerate(slots()):
+        for x in range(2):
+            pltpu.make_async_copy(
+                held.at[slot, pl.ds(x * 2 * share, 2 * share), pl.ds(column, width)],
+                target.at[pl.ds((y * 16 + x * 8 + c * 4 + h * 2) * share, 2 * share), :],
+                sem,
+            ).start()
+
+
+def load_chunks(held, target, sem, share, column, width):
+    for slot, (c, y, h) in enumerate(slots()):
+        for chunk in range(4):
+            pltpu.make_async_copy(
+                held.at[slot, pl.ds(chunk * share, share), pl.ds(column, width)],
+                target.at[pl.ds((y * 4 + c * 2 + h) * share, share), pl.ds(chunk * width, width)],
+                sem,
+            ).start()
+
+
+def load_blocks(held, target, sem, first, share):
+    for slot, (c, y, h) in enumerate(slots()):
+        pltpu.make_async_copy(
+            held.at[slot, pl.ds(first, share)],
+            target.at[pl.ds((y * 4 + c * 2 + h) * share, share), :],
+            sem,
+        ).start()
+
+
+def settle(target, sem):
+    pltpu.make_async_copy(target, target, sem).wait()
+
+
+def store_rows(target, grads, share, column):
+    y_me, _, c_me, h_me, _ = bits()
+    width = grads.shape[1]
+    for c, y, h in slots():
+        for x in range(2):
+            row = (y * 16 + x * 8 + c * 4 + h * 2) * share
+            target[
+                lax.bitwise_xor(c_me, c),
+                lax.bitwise_xor(y_me, y),
+                lax.bitwise_xor(h_me, h),
+                x * 2 * share : (x + 1) * 2 * share,
+                column : column + width,
+            ] = grads[row : row + 2 * share, :].astype(jnp.bfloat16)
+
+
+def store_chunks(target, grads, share, column):
+    y_me, _, c_me, h_me, _ = bits()
+    width = grads.shape[1] // 4
+    for c, y, h in slots():
+        row = (y * 4 + c * 2 + h) * share
+        for chunk in range(4):
+            target[
+                lax.bitwise_xor(c_me, c),
+                lax.bitwise_xor(y_me, y),
+                lax.bitwise_xor(h_me, h),
+                chunk * share : (chunk + 1) * share,
+                column : column + width,
+            ] = grads[row : row + share, chunk * width : (chunk + 1) * width].astype(jnp.bfloat16)
+
+
+def store_blocks(target, grads, first, share):
+    y_me, _, c_me, h_me, _ = bits()
+    for c, y, h in slots():
+        row = (y * 4 + c * 2 + h) * share
+        target[
+            lax.bitwise_xor(c_me, c),
+            lax.bitwise_xor(y_me, y),
+            lax.bitwise_xor(h_me, h),
+            first : first + share,
+            :,
+        ] = grads[row : row + share, :].astype(jnp.bfloat16)
+
+
+class Gather:
+    def __init__(self, parts, got_c, got_y, got_h, sends, receives, result):
+        self.parts, self.got = parts, (got_c, got_y, got_h)
+        self.sends, self.receives, self.result = sends, receives, result
+
+    def copy(self, step):
+        source = (self.parts.at[1], self.parts.at[0, 1], self.parts.at[0, 0, 1])[step]
+        return remote(
+            source,
+            self.got[step],
+            self.sends.at[step],
+            self.receives.at[step],
+            flipped((C_BIT, Y_BIT, H_BIT)[step]),
+        )
+
+    def over_c(self):
+        self.copy(0).start()
+
+    def over_y(self):
+        self.copy(0).wait_recv()
+        for y in (1, 0):
+            for h in range(2):
+                summed = self.parts[0, y, h].astype(jnp.float32) + self.got[0][y, h].astype(jnp.float32)
+                self.parts[0, y, h] = summed.astype(jnp.bfloat16)
+            if y == 1:
+                self.copy(1).start()
+
+    def over_h(self):
+        self.copy(1).wait_recv()
+        for h in (1, 0):
+            summed = self.parts[0, 0, h].astype(jnp.float32) + self.got[1][h].astype(jnp.float32)
+            self.parts[0, 0, h] = summed.astype(jnp.bfloat16)
+            if h == 1:
+                self.copy(2).start()
+
+    def done(self):
+        self.copy(2).wait_recv()
+        self.result[...] = self.parts[0, 0, 0].astype(jnp.float32) + self.got[2][...].astype(jnp.float32)
+        for step in range(3):
+            self.copy(step).wait_send()
+
+
+def greet_core():
+    greet([flipped(mask) for mask in (X_BIT, L_BIT, H_BIT, Y_BIT, C_BIT)])
+
+
+def block_rows(j, n):
+    return pl.ds(pl.multiple_of(j * n, n), n)
+
+
+def core_forward(hidden, seg_col, seg_row, vectors, query_bias, value_bias, hidden_bias, head_turned, vocab_bias, cotangent, bundles, collective):
+    n, width = hidden.shape
+    layers = query_bias.shape[0]
+    count = 4 * n
+    part = width // 4
+    inner = hidden_bias.shape[1]
+    head = width // HEADS
+    heads = part // head
+    share = width // 32
+    inner_share = inner // PIECES
+    scale = head**-0.5
+    vocab = head_turned.shape[0]
+    low, wide = jnp.bfloat16, jnp.float32
+    flat = [bundle for pair in bundles for bundle in pair]
+    kept = [
+        ((layers, 4, n, width), low),
+        ((layers, count, 3 * part), low),
+        ((layers, heads, count, count), low),
+        ((layers, count, part), low),
+        ((layers, n, width), wide),
+        ((layers, 4, n, width), low),
+        ((layers, count, inner), low),
+        ((layers, count, inner), low),
+        ((layers, n, width), wide),
+    ]
+    kinds = len(kept)
+
+    def kernel(*refs):
+        (h_ref, sc_ref, sr_ref, vec_ref, qb_ref, vb_ref, hb_ref, head_ref, vocab_ref, cot_ref) = refs[:10]
+        own = refs[10 : 10 + len(flat)]
+        rest = refs[10 + len(flat) :]
+        logits_ref, flow_ref, part_ref, sum_ref = rest[:4]
+        held = rest[4 : 4 + len(flat)]
+        saved = rest[4 + len(flat) : 4 + len(flat) + kinds]
+        rest = rest[4 + len(flat) + kinds :]
+        (x_all, qkv, weights_low, context, residual, m_all, active, slope, outer) = rest[:kinds]
+        (now, wj, wo, we, wr, low_buf, got, gs, gr, ss, sr, bs, br, bo, ws, ks) = rest[kinds:]
+        _, x, _, _, l = bits()
+        t = x * 2 + l
+        greet_core()
+        jobs = [
+            Spread(own[b], held[b], bs.at[b], br.at[b], bo.at[b]) for b in range(len(flat))
+        ]
+
+        def keep(kind, source, layer):
+            pltpu.make_async_copy(source.at[layer], saved[kind].at[layer], ks.at[kind, layer]).start()
+
+        jobs[0].over_h()
+        jobs[1].over_h()
+        jobs[0].over_y()
+        jobs[0].over_c()
+        jobs[2].over_h()
+        jobs[1].over_y()
+        now[...] = h_ref[...]
+        linked = sc_ref[...] == sr_ref[...]
+        for layer in range(layers):
+            first, second = jobs[2 * layer], jobs[2 * layer + 1]
+            x_all[layer, t] = now[...].astype(low)
+            first.done()
+            load_rows(held[2 * layer], wj, ws.at[0], share, 0, 3 * part)
+            load_chunks(held[2 * layer], wo, ws.at[1], share, 3 * part, part)
+            group_gather(x_all.at[layer], t, gs, gr)
+            keep(0, x_all, layer)
+            settle(wj, ws.at[0])
+            joint = dot(x_all[layer].reshape(count, width), wj[...])
+            qkv[layer, :, 0:part] = ((joint[:, 0:part] + qb_ref[layer : layer + 1]) * scale).astype(low)
+            qkv[layer, :, part : 2 * part] = joint[:, part : 2 * part].astype(low)
+            qkv[layer, :, 2 * part :] = (joint[:, 2 * part :] + vb_ref[layer : layer + 1]).astype(low)
+            keep(1, qkv, layer)
+            for at in range(heads):
+                queries = qkv[layer, :, at * head : (at + 1) * head]
+                keys = qkv[layer, :, part + at * head : part + (at + 1) * head]
+                values = qkv[layer, :, 2 * part + at * head : 2 * part + (at + 1) * head]
+                scores = jnp.where(linked, dot_rt(queries, keys), masked_score)
+                exponent = jnp.exp(scores - jnp.max(scores, axis=-1, keepdims=True))
+                inverse = 1.0 / jnp.sum(exponent, axis=-1, keepdims=True)
+                weights_low[layer, at] = (exponent * inverse).astype(low)
+                context[layer, :, at * head : (at + 1) * head] = dot(weights_low[layer, at], values).astype(low)
+            keep(2, weights_low, layer)
+            keep(3, context, layer)
+            settle(wo, ws.at[1])
+
+            def advance(layer=layer):
+                if layer == 0:
+                    jobs[1].over_c()
+                    jobs[2].over_y()
+                    jobs[3].over_h()
+                else:
+                    jobs[3].over_c()
+
+            attended = group_scatter(
+                lambda j: dot(context[layer, block_rows(j, n), :], wo[...]), t, low_buf, got, ss, sr, advance
+            )
+            residual[layer] = now[...] + (attended + vec_ref[layer : layer + 1])
+            keep(4, residual, layer)
+            at = layers + layer
+            middle = normed(residual[layer], vec_ref[at : at + 1], vec_ref[at + layers : at + layers + 1])
+            now[...] = middle
+            m_all[layer, t] = middle.astype(low)
+            second.done()
+            load_rows(held[2 * layer + 1], we, ws.at[2], share, 0, inner)
+            load_blocks(held[2 * layer + 1], wr, ws.at[3], 4 * share, inner_share)
+            group_gather(m_all.at[layer], t, gs, gr)
+            keep(5, m_all, layer)
+            settle(we, ws.at[2])
+            if layer == 0:
+                jobs[2].over_c()
+            made, bent = gelu_pair(dot(m_all[layer].reshape(count, width), we[...]) + hb_ref[layer : layer + 1])
+            active[layer] = made.astype(low)
+            slope[layer] = bent.astype(low)
+            keep(6, active, layer)
+            keep(7, slope, layer)
+            settle(wr, ws.at[3])
+
+            def advance_more(layer=layer):
+                if layer == 0:
+                    jobs[3].over_y()
+
+            fed = group_scatter(
+                lambda j: dot(active[layer, block_rows(j, n), :], wr[...]), t, low_buf, got, ss, sr, advance_more
+            )
+            at = 3 * layers + layer
+            outer[layer] = now[...] + fed + vec_ref[at : at + 1]
+            keep(8, outer, layer)
+            at += layers
+            now[...] = normed(outer[layer], vec_ref[at : at + 1], vec_ref[at + layers : at + layers + 1])
+        final_low = now[...].astype(low)
+        logits_ref[...] = dot_rt(final_low, head_ref[...]) + vocab_ref[...]
+        flow_ref[...] = dot(cot_ref[...], head_ref[...])
+        part_ref[...] = dot_lt(cot_ref[...], final_low)
+        sum_ref[...] = jnp.sum(cot_ref[...].astype(wide), axis=0, keepdims=True)
+        for kind in range(kinds):
+            for layer in range(layers):
+                pltpu.make_async_copy(
+                    saved[kind].at[layer], saved[kind].at[layer], ks.at[kind, layer]
+                ).wait()
+
+    outs = pl.pallas_call(
+        kernel,
+        out_shape=[
+            jax.ShapeDtypeStruct((n, vocab), wide),
+            jax.ShapeDtypeStruct((n, width), wide),
+            jax.ShapeDtypeStruct((vocab, width), wide),
+            jax.ShapeDtypeStruct((1, vocab), wide),
+        ]
+        + [jax.ShapeDtypeStruct((PIECES,) + bundle.shape, low) for bundle in flat]
+        + [jax.ShapeDtypeStruct(shape, kind) for shape, kind in kept],
+        in_specs=[IN_VMEM] * 10 + [ANYWHERE] * len(flat),
+        out_specs=[IN_VMEM] * 4 + [ANYWHERE] * (len(flat) + kinds),
+        scratch_shapes=[pltpu.VMEM(shape, kind) for shape, kind in kept]
+        + [
+            pltpu.VMEM((n, width), wide),
+            pltpu.VMEM((width, 3 * part), low),
+            pltpu.VMEM((part, width), low),
+            pltpu.VMEM((width, inner), low),
+            pltpu.VMEM((inner, width), low),
+        ]
+        + group_scratch(n, width)
+        + [
+            pltpu.SemaphoreType.DMA((len(flat), 3)),
+            pltpu.SemaphoreType.DMA((len(flat), 3)),
+            pltpu.SemaphoreType.DMA((len(flat),)),
+            pltpu.SemaphoreType.DMA((4,)),
+            pltpu.SemaphoreType.DMA((kinds, layers)),
+        ],
+        compiler_params=kernel_params(collective),
+        cost_estimate=cost(120),
+    )(hidden, seg_col, seg_row, vectors, query_bias, value_bias, hidden_bias, head_turned, vocab_bias, cotangent, *flat)
+    return outs[:4], outs[4 : 4 + len(flat)], outs[4 + len(flat) :]
+
+
+def core_backward(flow, vectors, held, saved, collective):
+    n, width = flow.shape
+    layers = saved[0].shape[0]
+    count = 4 * n
+    part = width // 4
+    inner = saved[6].shape[2]
+    head = width // HEADS
+    heads = part // head
+    share = width // 32
+    inner_share = inner // PIECES
+    scale = head**-0.5
+    low, wide = jnp.bfloat16, jnp.float32
+    kinds = len(saved)
+    bundles = len(held)
+    row_counts = [bundle.shape[1] for bundle in held]
+
+    def kernel(*refs):
+        flow_ref, vec_ref = refs[:2]
+        held_refs = refs[2 : 2 + bundles]
+        saved_refs = refs[2 + bundles : 2 + bundles + kinds]
+        rest = refs[2 + bundles + kinds :]
+        back_ref, token_ref, joint_ref, hidden_ref = rest[:4]
+        results = rest[4 : 4 + bundles]
+        rest = rest[4 + bundles :]
+        parts = rest[:bundles]
+        got_c, got_y, got_h = (rest[k * bundles : (k + 1) * bundles] for k in range(1, 4))
+        rest = rest[4 * bundles :]
+        (x_all, qkv, weights_low, context, residual, m_all, active, slope, outer) = rest[:kinds]
+        (fed, inner_low, grad_low, joint, wj, wo, we, wr, low_buf, got, gs, gr, ss, sr, rs_s, rs_r, ws, ks) = rest[kinds:]
+        _, x, _, _, l = bits()
+        t = x * 2 + l
+        buffers = rest[:kinds]
+
+        def fetch(kind, layer):
+            pltpu.make_async_copy(saved_refs[kind].at[layer], buffers[kind], ks.at[kind]).start()
+
+        def need(kind):
+            settle(buffers[kind], ks.at[kind])
+
+        def load_feed(layer):
+            fetch(8, layer)
+            load_blocks(held_refs[2 * layer + 1], wr, ws.at[3], 4 * share, inner_share)
+            fetch(7, layer)
+            load_rows(held_refs[2 * layer + 1], we, ws.at[2], share, 0, inner)
+            for kind in (6, 5, 4):
+                fetch(kind, layer)
+
+        def load_attend(layer):
+            load_chunks(held_refs[2 * layer], wo, ws.at[1], share, 3 * part, part)
+            for kind in (1, 2, 3, 0):
+                fetch(kind, layer)
+            load_rows(held_refs[2 * layer], wj, ws.at[0], share, 0, 3 * part)
+
+        greet_core()
+        load_feed(layers - 1)
+        load_attend(layers - 1)
+        jobs = [
+            Gather(parts[b], got_c[b], got_y[b], got_h[b], rs_s.at[b], rs_r.at[b], results[b])
+            for b in range(bundles)
+        ]
+        back_ref[...] = flow_ref[...]
+        for layer in reversed(range(layers)):
+            last = layer == layers - 1
+            feed_job, attend_job = jobs[2 * layer + 1], jobs[2 * layer]
+            sums = token_ref.at[layer]
+            sums[6:8] = jnp.zeros((2, width), wide)
+            at = 4 * layers + layer
+            need(8)
+            outer_grad, final_part, upper_part = normed_back(outer[...], vec_ref[at : at + 1], back_ref[...])
+            back_ref[...] = outer_grad
+            fed_low = outer_grad.astype(low)
+            fed[0, t] = fed_low
+            sums[0:1] = final_part
+            sums[1:2] = upper_part
+            sums[2:3] = jnp.sum(fed_low.astype(wide), axis=0, keepdims=True)
+            group_gather(fed.at[0], t, gs, gr)
+            settle(wr, ws.at[3])
+            active_grad = dot_rt(fed[0].reshape(count, width), wr[...])
+            need(7)
+            inner_low[...] = (active_grad * slope[...].astype(wide)).astype(low)
+            hidden_ref[layer : layer + 1] = jnp.sum(inner_low[...].astype(wide), axis=0, keepdims=True)
+            settle(we, ws.at[2])
+            need(6)
+            need(5)
+
+            def feed_weights(layer=layer, last=last, feed_job=feed_job):
+                store_blocks(feed_job.parts, dot_lt(active[...], fed[0].reshape(count, width)), 4 * share, inner_share)
+                store_rows(feed_job.parts, dot_lt(m_all[...].reshape(count, width), inner_low[...]), share, 0)
+                feed_job.over_c()
+                if not last:
+                    jobs[2 * layer + 2].over_y()
+                    jobs[2 * layer + 3].over_h()
+
+            back = group_scatter(
+                lambda j: dot_rt(inner_low[block_rows(j, n), :], we[...]), t, low_buf, got, ss, sr, feed_weights
+            )
+            need(4)
+            at = layers + layer
+            res_grad, middle_part, lower_part = normed_back(
+                residual[...], vec_ref[at : at + 1], back_ref[...] + back
+            )
+            back_ref[...] = res_grad
+            sums[3:4] = middle_part
+            sums[4:5] = lower_part
+            if layer:
+                load_feed(layer - 1)
+            own_low = res_grad.astype(low)
+            fed[1, t] = own_low
+            sums[5:6] = jnp.sum(own_low.astype(wide), axis=0, keepdims=True)
+            group_gather(fed.at[1], t, gs, gr)
+            settle(wo, ws.at[1])
+            grad_low[...] = dot_rt(fed[1].reshape(count, width), wo[...]).astype(low)
+            for kind in (1, 2, 3):
+                need(kind)
+            for at in range(heads):
+                mine = slice(at * head, (at + 1) * head)
+                queries = qkv[:, mine]
+                keys = qkv[:, part + at * head : part + (at + 1) * head]
+                values = qkv[:, 2 * part + at * head : 2 * part + (at + 1) * head]
+                weights = weights_low[at]
+                grads = grad_low[:, mine]
+                delta = jnp.sum(grads.astype(wide) * context[:, mine].astype(wide), axis=-1, keepdims=True)
+                score_grad = (weights.astype(wide) * (dot_rt(grads, values) - delta)).astype(low)
+                joint[:, mine] = (dot(score_grad, keys).astype(low).astype(wide) * scale).astype(low)
+                joint[:, part + at * head : part + (at + 1) * head] = dot_lt(score_grad, queries).astype(low)
+                joint[:, 2 * part + at * head : 2 * part + (at + 1) * head] = dot_lt(weights, grads).astype(low)
+            joint_ref[layer : layer + 1] = jnp.sum(joint[...].astype(wide), axis=0, keepdims=True)
+            settle(wj, ws.at[0])
+            need(0)
+
+            def attend_weights(layer=layer, last=last, feed_job=feed_job, attend_job=attend_job):
+                store_rows(attend_job.parts, dot_lt(x_all[...].reshape(count, width), joint[...]), share, 0)
+                store_chunks(attend_job.parts, dot_lt(context[...], fed[1].reshape(count, width)), share, 3 * part)
+                attend_job.over_c()
+                feed_job.over_y()
+                if not last:
+                    jobs[2 * layer + 2].over_h()
+                    jobs[2 * layer + 3].done()
+
+            back = group_scatter(
+                lambda j: dot_rt(joint[block_rows(j, n), :], wj[...]), t, low_buf, got, ss, sr, attend_weights
+            )
+            back_ref[...] = back_ref[...] + back
+            if layer:
+                load_attend(layer - 1)
+        jobs[0].over_y()
+        jobs[1].over_h()
+        jobs[2].done()
+        jobs[0].over_h()
+        jobs[1].done()
+        jobs[0].done()
+
+    return pl.pallas_call(
+        kernel,
+        out_shape=[
+            jax.ShapeDtypeStruct((n, width), wide),
+            jax.ShapeDtypeStruct((layers, 8, width), wide),
+            jax.ShapeDtypeStruct((layers, 3 * part), wide),
+            jax.ShapeDtypeStruct((layers, inner), wide),
+        ]
+        + [jax.ShapeDtypeStruct((rows, width), wide) for rows in row_counts],
+        in_specs=[IN_VMEM] * 2 + [ANYWHERE] * (bundles + kinds),
+        out_specs=[IN_VMEM] * (4 + bundles),
+        scratch_shapes=[pltpu.VMEM((2, 2, 2, rows, width), low) for rows in row_counts]
+        + [pltpu.VMEM((2, 2, rows, width), low) for rows in row_counts]
+        + [pltpu.VMEM((2, rows, width), low) for rows in row_counts]
+        + [pltpu.VMEM((rows, width), low) for rows in row_counts]
+        + [pltpu.VMEM(array.shape[1:], array.dtype) for array in saved]
+        + [
+            pltpu.VMEM((2, 4, n, width), low),
+            pltpu.VMEM((count, inner), low),
+            pltpu.VMEM((count, part), low),
+            pltpu.VMEM((count, 3 * part), low),
+            pltpu.VMEM((width, 3 * part), low),
+            pltpu.VMEM((part, width), low),
+            pltpu.VMEM((width, inner), low),
+            pltpu.VMEM((inner, width), low),
+        ]
+        + group_scratch(n, width)
+        + [
+            pltpu.SemaphoreType.DMA((bundles, 3)),
+            pltpu.SemaphoreType.DMA((bundles, 3)),
+            pltpu.SemaphoreType.DMA((4,)),
+            pltpu.SemaphoreType.DMA((kinds,)),
+        ],
+        compiler_params=kernel_params(collective),
+        cost_estimate=cost(130),
+    )(flow, vectors, *held, *saved)
+
+
+def fast_local(*arguments):
+    (
+        features,
+        utterance_ends,
+        kernel_weight,
+        position_bias,
+        entry_gain,
+        base_shift,
+        joint_weight,
+        query_bias,
+        value_bias,
+        output_weight,
+        attend_bias,
+        middle_gain,
+        lower_shift,
+        expand_weight,
+        hidden_bias,
+        reduce_weight,
+        return_bias,
+        final_gain,
+        upper_shift,
+        head_weight,
+        vocab_bias,
+        cotangent,
+    ) = arguments
+    devices = 32
+    _, n, width = features.shape
+    blocks = 4
+    frames = n * blocks
+    rows = 8
+    groups = CONV_G
+    group_width = width // groups
+    share = width // devices
+    taps = kernel_weight.shape[1] // group_width
+    layers = joint_weight.shape[0]
+    inner_all = expand_weight.shape[2]
+    inner = inner_all // 4
+    inner_share = inner_all // devices
+    part = width // 4
+    head = width // HEADS
+    vocab = head_weight.shape[1]
+    packs = n // PACK
+    y, x, c, h, l = bits()
+    turn = [
+        (index_of(*at), turned_of(*at)) for at in itertools.product((0, 1), repeat=len(AXES))
+    ]
+
+    joint_turned = joint_weight.reshape(layers, share, 3, 2, 2, 2, 2, head)
+    joint_turned = joint_turned.transpose(4, 6, 0, 1, 2, 3, 5, 7).reshape(4, layers, share, 3 * part)
+    expand_turned = expand_weight.reshape(layers, share, 2, 2, 2, 2, 2, inner_share)
+    expand_turned = expand_turned.transpose(3, 6, 0, 1, 2, 4, 5, 7).reshape(4, layers, share, inner)
+    columns = jnp.concatenate([joint_turned, expand_turned], axis=-1)
+
+    whole_rows = jnp.concatenate(
+        [entry_gain[None], base_shift[None], attend_bias, middle_gain, lower_shift]
+        + [return_bias, final_gain, upper_shift, head_weight.T, query_bias, value_bias]
+        + [hidden_bias.reshape(layers * inner_share // share, share)],
+        axis=0,
+    )
+    ends = jnp.concatenate([utterance_ends[0] // 32, utterance_ends[0] % 32])
+    flat_rows = jnp.concatenate([whole_rows.reshape(-1), ends.astype(jnp.bfloat16)])
+    flat_rows = jnp.pad(flat_rows, (0, -flat_rows.shape[0] % 2048)).reshape(1, -1, 128)
+
+    def by_group(tokens):
+        tokens = tokens.reshape(packs, PACK, groups, group_width)
+        return tokens.transpose(2, 0, 1, 3).reshape(groups, packs, PACK * group_width)
+
+    def from_channels(received):
+        received = received.reshape(devices, packs, PACK, share)
+        return received.transpose(1, 2, 0, 3).reshape(n, width)
+
+    def by_block(channels):
+        channels = channels.reshape(blocks, packs, rows, PACK * share)
+        return channels.transpose(2, 0, 1, 3).reshape(devices, packs, PACK * share)
+
+    arrived, columns, output_rows, small = swap_all(
+        1,
+        [
+            (by_group(features[0]), group_of),
+            (columns, "group"),
+            (output_weight, "twist"),
+            (flat_rows, lambda *place: 0),
+        ],
+    )
+    small = small.reshape(devices, -1)
+    taken = whole_rows.shape[0] * share
+    gathered = small[:, :taken].reshape(devices, -1, share)
+    vector_count = 2 + 6 * layers
+    whole = jnp.swapaxes(gathered[:, : vector_count + vocab], 0, 1).reshape(vector_count + vocab, width)
+    entry_full, base_full = widened(whole[0:1]), widened(whole[1:2])
+    vectors = widened(whole[2:vector_count])
+    head_turned = whole[vector_count:]
+    own_rows = gathered[:, vector_count + vocab :].reshape(2, 2, 2, 2, 2, -1, share)
+    own_rows = lax.dynamic_index_in_dim(own_rows, x, 1, keepdims=False)
+    by_head = lax.dynamic_index_in_dim(own_rows[..., : 2 * layers, :], l, 2, keepdims=False)
+    by_head = jnp.moveaxis(by_head, 3, 0).reshape(2, layers, part)
+    query_full, value_full = widened(by_head[0]), widened(by_head[1])
+    hidden_full = lax.dynamic_index_in_dim(own_rows[..., 2 * layers :, :], l, 3, keepdims=False)
+    hidden_full = hidden_full.reshape(2, 2, 2, layers, inner_share)
+    hidden_full = widened(jnp.moveaxis(hidden_full, 3, 0).reshape(layers, inner))
+    all_ends = small[:, taken : taken + 8].astype(jnp.int32)
+    all_ends = (all_ends[:, :4] * 32 + all_ends[:, 4:8])[::blocks]
+    row_ends = lax.dynamic_slice_in_dim(all_ends, y * 4 + h * 2 + c, 1, axis=0)
+    row_ids = segment_ids(jnp.arange(frames, dtype=jnp.int32), row_ends)
+    seg_col, seg_row = row_ids.reshape(frames, 1), row_ids
+    before = jnp.concatenate([jnp.zeros((rows, 1), jnp.int32), all_ends[:, :-1]], axis=1)
+    bounds = jnp.where(all_ends > before, all_ends, frames)
+    bounds = jnp.tile(bounds, (frames // PACK, 1))
+
+    bundles = []
+    for layer in range(layers):
+        joint_rows = columns[:, layer, :, : 3 * part].reshape(4 * share, 3 * part)
+        output_part = output_rows[layer].reshape(share, 4, part)
+        output_part = output_part.transpose(1, 0, 2).reshape(4 * share, part)
+        expand_rows = columns[:, layer, :, 3 * part :].reshape(4 * share, inner)
+        bundles.append(
+            (
+                jnp.concatenate([joint_rows, output_part], axis=1),
+                jnp.concatenate([expand_rows, reduce_weight[layer]], axis=0),
+            )
+        )
+
+    packed = arrived.reshape(rows, frames // PACK, PACK * group_width)
+    packed = packed.transpose(1, 0, 2).reshape(frames // PACK * rows, PACK * group_width)
+    grid = kernel_weight.reshape(share, taps, group_width)
+    conv_pre, even, odd = conv_forward_packed(
+        packed,
+        bounds,
+        shifted_taps(grid.transpose(1, 2, 0)),
+        jnp.tile(widened(position_bias), PACK)[None],
+    )
+    (pre_parts,) = swap_all(2, [(by_block(conv_pre), turned_of)])
+    pre = widened(from_channels(pre_parts))
+    own_feats = lax.ppermute(features[0], AXES, turn)
+    own_cot = lax.ppermute(cotangent[0], AXES, turn)
+    mixed = widened(own_feats) + gelu_exact(pre)
+    hidden = layer_norm(mixed, entry_full, base_full)
+
+    (logits, flow, head_part, vocab_sum), held, saved = core_forward(
+        hidden,
+        seg_col,
+        seg_row,
+        vectors,
+        query_full,
+        value_full,
+        hidden_full,
+        head_turned,
+        widened(vocab_bias)[None],
+        own_cot,
+        bundles,
+        3,
+    )
+    logits = lax.ppermute(logits, AXES, turn)
+    flow, token_sums, joint_sums, hidden_sums, *layer_sums = core_backward(flow, vectors, held, saved, 4)
+
+    mixed_grad, entry_part, base_part = normed_back(mixed, entry_full, flow)
+    slope = gelu_pair(pre)[1]
+    conv_low = rounded(mixed_grad * slope)
+    (low_parts,) = swap_all(5, [(by_group(conv_low), group_of)])
+    low_parts = low_parts.reshape(2, 2, 2, 2, 2, packs, PACK * group_width)
+    packed_low = low_parts.transpose(1, 4, 5, 0, 3, 2, 6)
+    packed_low = packed_low.reshape(frames // PACK * rows, PACK * group_width)
+    own_low = lax.dynamic_index_in_dim(
+        packed_low.reshape(-1, PACK, group_width // share, share), l, 2, keepdims=False
+    ).reshape(-1, PACK * share)
+    halves = grid.reshape(share, taps, 2, share)
+    kept = lax.dynamic_index_in_dim(halves, l, 2, keepdims=False)
+    given = lax.ppermute(
+        lax.dynamic_index_in_dim(halves, 1 - l, 2, keepdims=False), "l", [(0, 1), (1, 0)]
+    )
+    both = jnp.where(l == 0, jnp.stack([kept, given]), jnp.stack([given, kept]))
+    both = both.reshape(2 * share, taps, share).transpose(1, 0, 2)
+    both = jnp.pad(both[::-1], ((1, 0), (0, 0), (0, 0)))
+    feats_part, kernel_own, position_part = conv_backward_packed(
+        packed_low, own_low, bounds, shifted_taps(both), even, odd
+    )
+    position_own = jnp.sum(position_part.reshape(PACK, share), axis=0)
+
+    vector_sums = jnp.concatenate([entry_part, base_part] + [token_sums[k, :6] for k in range(layers)], axis=0)
+    vector_sums = vector_sums.reshape(vector_count, devices, share).transpose(1, 0, 2)
+    vector_sums = vector_sums.reshape(devices, vector_count * share)
+    place = jnp.arange(2)
+    heads_sums = jnp.concatenate(
+        [
+            joint_sums[:, :part].reshape(layers, 2, 1, 2, 1, 2, share),
+            joint_sums[:, 2 * part :].reshape(layers, 2, 1, 2, 1, 2, share),
+        ],
+        axis=0,
+    )
+    chosen = (place == x).reshape(2, 1, 1, 1, 1) & (place == l).reshape(2, 1, 1)
+    heads_sums = jnp.where(chosen, heads_sums, 0.0)
+    chosen = (place == x).reshape(2, 1, 1, 1, 1) & (place == l).reshape(2, 1)
+    inner_sums = jnp.where(chosen, hidden_sums.reshape(layers, 2, 1, 2, 2, 1, inner_share), 0.0)
+
+    def per_device(array):
+        return jnp.moveaxis(array, 0, 5).reshape(devices, -1)
+
+    flat = jnp.concatenate(
+        [
+            vector_sums,
+            per_device(heads_sums),
+            per_device(inner_sums),
+            jnp.broadcast_to(vocab_sum, (devices, vocab)),
+        ],
+        axis=1,
+    )
+    flat = jnp.pad(flat, ((0, 0), (0, -flat.shape[1] % 1024)))
+    head_rows = head_part.reshape(vocab, devices, share).transpose(1, 2, 0).reshape(devices, share * vocab)
+    flat = jnp.concatenate([flat, head_rows], axis=1).reshape(devices, -1, 128)
+
+    back_columns = jnp.stack(
+        [
+            jnp.concatenate(
+                [
+                    layer_sums[2 * layer][:, : 3 * part].reshape(4, share, 3 * part),
+                    layer_sums[2 * layer + 1][: 4 * share].reshape(4, share, inner),
+                ],
+                axis=-1,
+            )
+            for layer in range(layers)
+        ],
+        axis=1,
+    )
+    output_back = jnp.stack(
+        [
+            layer_sums[2 * layer][:, 3 * part :].reshape(4, share, part).transpose(1, 0, 2).reshape(share, width)
+            for layer in range(layers)
+        ]
+    )
+    feats_back, sums, back_columns, output_own = swap_all(
+        6,
+        [
+            (by_block(feats_part), index_of),
+            (flat, index_of),
+            (rounded(back_columns), "group"),
+            (output_back, "twist"),
+        ],
+    )
+    features_grad = lax.ppermute(mixed_grad, AXES, turn) + widened(from_channels(feats_back))
+    sums = jnp.sum(sums, axis=0).reshape(-1)
+    at = vector_count * share
+    vector_own = sums[:at].reshape(vector_count, share)
+    query_own = sums[at : at + layers * share].reshape(layers, share)
+    at += layers * share
+    value_own = sums[at : at + layers * share].reshape(layers, share)
+    at += layers * share
+    hidden_own = sums[at : at + layers * inner_share].reshape(layers, inner_share)
+    at += layers * inner_share
+    vocab_own = sums[at : at + vocab]
+    head_own = sums[-share * vocab :].reshape(share, vocab)
+    back_columns = widened(back_columns)
+    joint_own = back_columns[..., : 3 * part].reshape(2, 2, layers, share, 3, 2, 2, head)
+    joint_own = joint_own.transpose(2, 3, 4, 5, 0, 6, 1, 7).reshape(layers, share, 3 * width)
+    expand_own = back_columns[..., 3 * part :].reshape(2, 2, layers, share, 2, 2, 2, inner_share)
+    expand_own = expand_own.transpose(2, 3, 4, 0, 5, 6, 1, 7).reshape(layers, share, inner_all)
+    reduce_own = jnp.stack([layer_sums[2 * layer + 1][4 * share :] for layer in range(layers)])
+    per_layer = vector_own[2:].reshape(layers, 6, share)
+    return (
+        logits[None],
+        features_grad[None],
+        kernel_own,
+        position_own,
+        vector_own[0],
+        vector_own[1],
+        joint_own,
+        query_own,
+        value_own,
+        output_own,
+        per_layer[:, 5],
+        per_layer[:, 3],
+        per_layer[:, 4],
+        expand_own,
+        hidden_own,
+        reduce_own,
+        per_layer[:, 2],
+        per_layer[:, 0],
+        per_layer[:, 1],
+        head_own,
+        vocab_own,
+    )
+
+
+def fits(dp_size, seq_size, width):
+    share = width // 32
+    return (
+        dp_size == 8
+        and seq_size == 4
+        and share % 16 == 0
+        and share * 2 == width // CONV_G
+        and share * 2 == width // HEADS
+    )
+
+
+def placed(mesh, width):
+    if fits(mesh.shape["dp"], mesh.shape["seq"], width):
+        body = fast_local
+        mesh = jax.sharding.Mesh(mesh.devices.reshape((2,) * len(AXES)), AXES)
+        split, over, within = AXES[:3], AXES[3:], AXES
+    else:
+        body, split, over, within = local, "dp", "seq", ("dp", "seq")
+    tokens = P(split, over, None)
+    first, first_wide = P(within), P(within, None)
+    second, second_wide = P(None, within), P(None, within, None)
     return jax.shard_map(
-        local,
+        body,
         mesh=mesh,
         in_specs=(
-            P("dp", "seq", None),
-            P("dp", None),
-            P(("dp", "seq"), None),
-            P(("dp", "seq")),
-            P(("dp", "seq")),
-            P(("dp", "seq")),
-            P(None, ("dp", "seq"), None),
-            P(None, ("dp", "seq")),
-            P(None, ("dp", "seq")),
-            P(None, ("dp", "seq"), None),
-            P(None, ("dp", "seq")),
-            P(None, ("dp", "seq")),
-            P(None, ("dp", "seq")),
-            P(None, ("dp", "seq"), None),
-            P(None, ("dp", "seq")),
-            P(None, ("dp", "seq"), None),
-            P(None, ("dp", "seq")),
-            P(None, ("dp", "seq")),
-            P(None, ("dp", "seq")),
-            P(("dp", "seq"), None),
+            tokens,
+            P(split, None),
+            first_wide,
+            first,
+            first,
+            first,
+            second_wide,
+            second,
+            second,
+            second_wide,
+            second,
+            second,
+            second,
+            second_wide,
+            second,
+            second_wide,
+            second,
+            second,
+            second,
+            first_wide,
             P(),
-            P("dp", "seq", None),
+            tokens,
         ),
         out_specs=(
-            P("dp", "seq", None),
-            P("dp", "seq", None),
-            P(("dp", "seq"), None),
-            P(("dp", "seq")),
-            P(("dp", "seq")),
-            P(("dp", "seq")),
-            P(None, ("dp", "seq"), None),
-            P(None, ("dp", "seq")),
-            P(None, ("dp", "seq")),
-            P(None, ("dp", "seq"), None),
-            P(None, ("dp", "seq")),
-            P(None, ("dp", "seq")),
-            P(None, ("dp", "seq")),
-            P(None, ("dp", "seq"), None),
-            P(None, ("dp", "seq")),
-            P(None, ("dp", "seq"), None),
-            P(None, ("dp", "seq")),
-            P(None, ("dp", "seq")),
-            P(None, ("dp", "seq")),
-            P(("dp", "seq"), None),
+            tokens,
+            tokens,
+            first_wide,
+            first,
+            first,
+            first,
+            second_wide,
+            second,
+            second,
+            second_wide,
+            second,
+            second,
+            second,
+            second_wide,
+            second,
+            second_wide,
+            second,
+            second,
+            second,
+            first_wide,
             P(),
         ),
         check_vma=False,
     )
+
+
+def solution(mesh):
+    def whole(*arguments):
+        return placed(mesh, arguments[0].shape[2])(*arguments)
+
+    return whole

time: 4180 us -> 631 us (0.15)
  waiting for transfers between devices: 2720 us -> 0.01 us
  local copies, waits for them, and re-layouts: 773 us -> 161 us
  Pallas kernels: 0 us -> 419 us
  matrix products: 279 us -> 0 us
  blocking collectives: 278 us -> 0 us
  other arithmetic: 78.1 us -> 22 us
    reduce_scatter x4 -> x0, waiting for transfers between devices: 2310 us -> none  [the longest x2 1480 us: local(): lax.psum_scatter(layer_term(jnp.int32(0), rows_share * lax.axis_size(('dp...]
    pallas_call x0 -> x8, Pallas kernels: none -> 419 us  [the longest x1 156 us: core_forward(): pl.pallas_call(kernel, out_shape=[jax.ShapeDtypeStruct((n, vocab), wide),...]
    all_gather x13 -> x0, waiting for transfers between devices: 373 us -> none  [the longest x2 147 us: local(): lax.all_gather(reduce_weight[layer_at], ('dp', 'seq'), axis=0, tiled=True)]
    dot_general x63 -> x0, matrix products: 279 us -> none  [the longest x8 63.8 us: conv_backward(): jnp.einsum('rtgo,rtkgi->goki', grouped, feats_window, preferred_element_t...]
    slice x143 -> x27, local copies, waits for them, and re-layouts: 242 us -> 14.4 us  [the longest x2 2.04 us: fast_local(): layer_sums[2 * layer][:, :3 * part].reshape(4, share, 3 * part)]
    all_gather x3 -> x0, blocking collectives: 192 us -> none  [the longest x2 126 us: local(): lax.all_gather(hidden_bias[layer_at], ('dp', 'seq'), axis=0, tiled=True)]
    unnamed x1035 -> x130, local copies, waits for them, and re-layouts: 150 us -> 7.85 us
    concatenate x3 -> x11, local copies, waits for them, and re-layouts: 176 us -> 36.9 us  [the longest x2 36 us: shifted_taps(): jnp.concatenate(parts, axis=1).reshape(steps, PACK * depth, PACK * width)]
  transfers between devices with their start and end apart: 25 -> 5, of which waited for: 12 -> 0; matrix products, arithmetic and copies ran while one was open for 24% -> 22% of each run, Pallas kernels for 0% -> 61%
where the time goes in v2:
time: 631 us; the launch traced here: 621 us
  Pallas kernels  419 us (66%)
  local copies, waits for them, and re-layouts  161 us (26%)
  other arithmetic  22 us (3%)
  starting transfers between devices  17.2 us (3%)
    pallas_call x1, Pallas kernels, core_forward(): pl.pallas_call(kernel, out_shape=[jax.ShapeDtypeStruct((n, vocab), wide),...  156 us
    pallas_call x1, Pallas kernels, core_backward(): pl.pallas_call(kernel, out_shape=[jax.ShapeDtypeStruct((n, width), wide),...  156 us
    pallas_call x4, Pallas kernels, swap_all(): pl.pallas_call(kernel, out_shape=[jax.ShapeDtypeStruct(shape_of(array, ki...  86.4 us
    concatenate x2, local copies, waits for them, and re-layouts, shifted_taps(): jnp.concatenate(parts, axis=1).reshape(steps, PACK * depth, PACK * width)  36 us
    pad x2, local copies, waits for them, and re-layouts, shifted_taps(): jnp.pad(grid, ((f, room - taps - f), (0, 0), (0, 0)))  20.7 us
    convert_element_type x14, local copies, waits for them, and re-layouts, widened(): return tensor.astype(jnp.float32)  15.9 us
  transfers between devices with their start and end apart: 5, of which 0 were waited for; matrix products, arithmetic and copies ran while one was open for 22% of the time, Pallas kernels for 61%

profile of v2, /device:TPU:16, one launch (start us, length us, event | category | flops | bytes accessed | tf_op | source)
XLA Modules:
  0.0 621.1 jit_solution(15691332255842472695)
XLA Ops:
  0.7 3.2 collective-permute-start
  3.8 1.4 copy.268
  5.2 4.5 collective-permute-start.1
  9.7 2.5 reshape_reshape.7
  12.2 6.8 %constant_dynamic-slice_fusion.1 = (bf16[32,128,1,32]{3,2,1,0:T(2,128)(2,1)}, bf16[32,128,1,32]{3,2,1,0:T(2,128)(2,1)}) fusion(bf16[32,128,2,32]{3,2,1,0:T(2,128)(2,1)S(1)} %reshape_reshape.7, s32[]{:T(128)S(6)} %select_n.65, s32[]{:T(128)S(6)} %select_n.67), kind=kLoop, calls=%fused_computation.90 | loop fusion | bytes 1048584 | tf_op jit(solution)/shard_map/jit(dynamic_index_in_dim)/dynamic_slice | solution.py:1636
  19.0 5.4 copy.276
  24.4 1.6 collective-permute-start.4
  26.4 1.1 reshape.462
  27.7 1.0 reshape.451.refs_0_
  33.6 1.0 pad_maximum_fusion.1.refs_1_
  34.5 28.8 %shard_map.373 = (bf16[32,16,512]{2,1,0:T(8,128)(2,1)}, bf16[4,2,32,1792]{3,2,1,0:T(8,128)(2,1)}, bf16[2,32,1024]{2,1,0:T(8,128)(2,1)}, bf16[32,16,128]{2,1,0:T(8,128)(2,1)}) custom-call(bf16[16,16,512]{2,1,0:T(8,128)(2,1)} %reshape.451.refs_0_, bf16[4,2,32,1792]{3,2,1,0:T(8,128)(2,1)} %pad_maximum_fusion.1.refs_1_, bf16[2,32,1024]{2,1,0:T(8,128)(2,1)} %refs_2_.1, ...), custom_call_target="tpu_custom_call" | custom-call | flops 22000001024 | bytes 1048576 | tf_op jit(solution)/shard_map/pallas_call | solution.py:666
  66.9 1.7 fusion.24
  68.6 1.1 fusion.23
  70.2 1.1 copy.321
  72.2 2.4 copy.292
  74.6 13.0 %fusion.22 = (bf16[136,64,32]{2,1,0:T(8,128)(2,1)S(1)}, bf16[136,64,32]{2,1,0:T(8,128)(2,1)}, bf16[136,64,32]{2,1,0:T(8,128)(2,1)}, bf16[136,64,32]{2,1,0:T(8,12...) fusion(bf16[128,64,32]{2,1,0:T(8,128)(2,1)} %copy.292), kind=kLoop, calls=%fused_computation.113 | loop fusion | bytes 4980736 | tf_op jit(solution)/shard_map/jit(_pad)/pad | solution.py:817
  88.2 18.0 %concatenate.113.k_ref = bf16[17,512,256]{2,1,0:T(8,128)(2,1)} concatenate(bf16[17,512,32]{2,1,0:T(8,128)(2,1)} %bitcast.197, bf16[17,512,32]{2,1,0:T(8,128)(2,1)} %bitcast.196, bf16[17,512,32]{2,1,0:T(8,128)(2,1)} %bitcast.195, bf16[17,512,32]{2,1,0:T(8,128)(2,1)} %bitcast.194, bf16[17,512,32]{2,1,0:T(8,128)(2,1)} %bitcast.193, bf16[17,512,32]{2,1,0:T(8,128)(2,1)} %bitcast.192, ...), dimensions={2} | concatenate | bytes 8912896 | tf_op jit(solution)/shard_map/concatenate | solution.py:820
  106.3 7.5 %shard_map.374 = (bf16[512,256]{1,0:T(8,128)(2,1)}, bf16[832,512]{1,0:T(8,128)(2,1)}, bf16[832,512]{1,0:T(8,128)(2,1)}) custom-call(bf16[512,512]{1,0:T(8,128)(2,1)} %bitcast.234, s32[512,4]{1,0:T(8,128)} %broadcast_bitcast_fusion.b_ref, bf16[17,512,256]{2,1,0:T(8,128)(2,1)} %concatenate.113.k_ref, f32[1,256]{1,0:T(1,128)} %broadcast_in_dim_tile.3.bias_ref), custom_call_target="tpu_custom_call" | custom-call | flops 11000000512 | bytes 1048576 | tf_op jit(solution)/shard_map/pallas_call | solution.py:742
  113.7 1.7 copy.261
  115.4 12.3 %shard_map.375 = bf16[32,16,256]{2,1,0:T(8,128)(2,1)} custom-call(bf16[32,16,256]{2,1,0:T(8,128)(2,1)} %bitcast.250), custom_call_target="tpu_custom_call" | custom-call | flops 22000001024 | bytes 1048576 | tf_op jit(solution)/shard_map/pallas_call | solution.py:666
  130.2 1.0 pad_maximum_fusion.3
  131.3 1.6 reshape.505
  132.8 2.6 copy.317
  135.4 2.6 reshape.496
  142.7 3.9 copy.275
  148.5 2.2 fusion.19
  152.4 156.2 %shard_map.376 = (f32[128,32]{1,0:T(8,128)}, f32[128,1024]{1,0:T(8,128)}, f32[32,1024]{1,0:T(8,128)}, f32[1,32]{1,0:T(1,128)}, bf16[8,128,1024]{2,1,0:T(8,128)(2...) custom-call(f32[128,1024]{1,0:T(8,128)} %multiply_add_fusion.refs_0_, ...), custom_call_target="tpu_custom_call" | custom-call | flops 131999997952 | bytes 1048576 | tf_op jit(solution)/shard_map/pallas_call | solution.py:1246
  308.8 156.1 %shard_map.377 = (f32[128,1024]{1,0:T(8,128)}, f32[2,8,1024]{2,1,0:T(8,128)}, f32[2,768]{1,0:T(2,128)}, f32[2,1024]{1,0:T(2,128)}, f32[128,1024]{1,0:T(8,128)}, ...) custom-call(f32[128,1024]{1,0:T(8,128)} %get-tuple-element.66.refs_0_, ...), custom_call_target="tpu_custom_call" | custom-call | flops 142999994368 | bytes 1048576 | tf_op jit(solution)/shard_map/pallas_call | solution.py:1432
  465.0 1.3 multiply_reduce_fusion
  466.3 2.2 fusion.8
  469.1 1.0 reshape.471.refs_0_
  470.2 18.8 %shard_map.378 = bf16[32,16,512]{2,1,0:T(8,128)(2,1)} custom-call(bf16[16,16,512]{2,1,0:T(8,128)(2,1)} %reshape.471.refs_0_), custom_call_target="tpu_custom_call" | custom-call | flops 22000001024 | bytes 1048576 | tf_op jit(solution)/shard_map/pallas_call | solution.py:666
  489.0 1.6 copy.319
  490.6 1.0 reshape.473.g_ref
  491.6 1.0 reshape_reshape.6
  492.6 1.0 slice.289
  494.6 1.0 slice.290
  496.5 3.5 constant_dynamic-slice_fusion.2
  500.0 4.4 copy.274
  505.3 1.1 maximum_select_fusion
  506.4 3.0 copy.277
  509.4 1.5 rev.3
  510.9 2.2 pad.86
  513.1 7.8 %fusion.21 = (bf16[136,64,32]{2,1,0:T(8,128)(2,1)S(1)}, bf16[136,64,32]{2,1,0:T(8,128)(2,1)}, bf16[136,64,32]{2,1,0:T(8,128)(2,1)}, bf16[136,64,32]{2,1,0:T(8,12...) fusion(bf16[129,64,32]{2,1,0:T(8,128)(2,1)S(1)} %pad.86), kind=kLoop, calls=%fused_computation.112 | loop fusion | bytes 4984832 | tf_op jit(solution)/shard_map/jit(_pad)/pad | solution.py:817
  520.9 18.0 %concatenate.126.k_ref = bf16[17,512,256]{2,1,0:T(8,128)(2,1)} concatenate(bf16[17,512,32]{2,1,0:T(8,128)(2,1)} %bitcast.205, bf16[17,512,32]{2,1,0:T(8,128)(2,1)} %bitcast.204, bf16[17,512,32]{2,1,0:T(8,128)(2,1)} %bitcast.203, bf16[17,512,32]{2,1,0:T(8,128)(2,1)} %bitcast.202, bf16[17,512,32]{2,1,0:T(8,128)(2,1)} %bitcast.201, bf16[17,512,32]{2,1,0:T(8,128)(2,1)} %bitcast.200, ...), dimensions={2} | concatenate | bytes 8912896 | tf_op jit(solution)/shard_map/concatenate | solution.py:820
  538.9 12.4 %shard_map.379 = (bf16[512,256]{1,0:T(8,128)(2,1)}, f32[32,8192]{1,0:T(8,128)}, f32[1,256]{1,0:T(1,128)}) custom-call(bf16[512,512]{1,0:T(8,128)(2,1)} %reshape.473.g_ref, bf16[512,256]{1,0:T(8,128)(2,1)} %copy.278.own_ref, s32[512,4]{1,0:T(8,128)} %broadcast_bitcast_fusion.b_ref, bf16[17,512,256]{2,1,0:T(8,128)(2,1)} %concatenate.126.k_ref, ...), custom_call_target="tpu_custom_call" | custom-call | flops 16499999744 | bytes 1048576 | tf_op jit(solution)/shard_map/pallas_call | solution.py:792
  551.3 1.7 copy.279
  554.8 1.1 slice.287
  557.1 1.0 pad_maximum_fusion.2.refs_2_
  558.8 26.4 %shard_map.380 = (bf16[32,16,256]{2,1,0:T(8,128)(2,1)}, f32[32,16,128]{2,1,0:T(8,128)}, bf16[4,2,32,1792]{3,2,1,0:T(8,128)(2,1)}, f32[2,32,1024]{2,1,0:T(8,128)}) custom-call(bf16[32,16,256]{2,1,0:T(8,128)(2,1)} %bitcast.247, f32[32,16,128]{2,1,0:T(8,128)} %pad_maximum_fusion.7.refs_1_, bf16[4,2,32,1792]{3,2,1,0:T(8,128)(2,1)} %pad_maximum_fusion.2.refs_2_, ...), custom_call_target="tpu_custom_call" | custom-call | flops 22000001024 | bytes 1048576 | tf_op jit(solution)/shard_map/pallas_call | solution.py:666
  585.2 1.1 reduce_sum.100
  587.7 3.4 collective-permute-start.2
  591.1 4.5 collective-permute-start.3
  595.6 1.3 fusion.27
  598.2 1.1 pad_maximum_fusion
  599.4 1.1 slice.261
  600.5 1.7 reshape.507
  602.2 2.8 copy.286
  605.0 1.8 reshape.504
  608.6 1.0 reshape.489
  609.6 1.2 copy.287
  610.9 2.3 reshape.490
  614.9 1.8 reshape.493
  618.1 1.9 add_bitcast_fusion
  (258 shorter events, 36.5 us)
Async XLA Ops:
  0.7 147.8 %collective-permute-start = (bf16[128,1024]{1,0:T(8,128)(2,1)}, bf16[128,1024]{1,0:T(8,128)(2,1)}, u32[]{:S(2)}, u32[]{:S(2)}) collective-permute-start(bf16[128,1024]{1,0:T(8,128)(2,1)} %bitcast.244), channel_id=1, source_target_pairs={{0,0},{1,1},{2,8},{3,9},{4,4},{5,5},{6,12},{7,13},{8,2},{9,3},{10,... | collective-permute-start | bytes 786440 | tf_op jit(solution)/shard_map/ppermute | solution.py:1603
  5.2 147.2 %collective-permute-start.1 = (bf16[128,32]{1,0:T(8,128)(2,1)}, bf16[128,32]{1,0:T(8,128)(2,1)}, u32[]{:S(2)}, u32[]{:S(2)}) collective-permute-start(bf16[128,32]{1,0:T(8,128)(2,1)} %bitcast.38), channel_id=1, source_target_pairs={{0,0},{1,1},{2,8},{3,9},{4,4},{5,5},{6,12},{7,13},{8,2},{9,3},{10,... | collective-permute-start | bytes 24584 | tf_op jit(solution)/shard_map/ppermute | solution.py:1604
  19.0 7.0 %copy-start.17 = (bf16[1,128,1024]{2,1,0:T(8,128)(2,1)S(1)}, bf16[1,128,1024]{2,1,0:T(8,128)(2,1)}, u32[]{:S(2)}) copy-start(bf16[1,128,1024]{2,1,0:T(8,128)(2,1)} %param.22) | copy-start | bytes 786436
  19.0 7.4 %copy-start.7 = (bf16[32,8192]{1,0:T(8,128)(2,1)S(1)}, bf16[32,8192]{1,0:T(8,128)(2,1)}, u32[]{:S(2)}) copy-start(bf16[32,8192]{1,0:T(8,128)(2,1)} %param.24) | copy-start | bytes 1572868
  24.4 4.3 copy-start.13
  24.4 480.9 %collective-permute-start.4 = (bf16[32,128,32]{1,2,0:T(8,128)(2,1)}, bf16[32,128,32]{1,2,0:T(8,128)(2,1)}, u32[]{:S(2)}, u32[]{:S(2)}) collective-permute-start(bf16[32,128,32]{1,2,0:T(8,128)(2,1)} %bitcast.55), channel_id=1, source_target_pairs={{0,1},{1,0},{2,3},{3,2},{4,5},{5,4},{6,7},{7,6},{8,9},{9,8},{10,11... | collective-permute-start | bytes 786440 | tf_op jit(solution)/shard_map/ppermute | solution.py:1637
  27.7 2.1 copy-start.16
  29.7 1.5 copy-start.40
  29.8 1.6 copy-start.41
  29.8 2.7 copy-start.30
  30.3 1.2 copy-start.42
  30.3 1.3 copy-start.43
  30.3 1.4 copy-start.44
  30.3 1.5 copy-start.45
  30.3 1.6 copy-start.46
  30.3 1.7 copy-start.47
  30.3 1.8 copy-start.48
  30.4 1.9 copy-start.49
  30.4 1.9 copy-start.50
  30.4 2.5 copy-start.55
  64.8 5.4 copy-start.15
  74.6 13.0 %copy-start.51 = (bf16[32]{0:T(256)(128)(2,1)S(1)}, bf16[32]{0:T(256)(128)(2,1)}, u32[]{:S(2)}) copy-start(bf16[32]{0:T(256)(128)(2,1)} %param.25) | copy-start | bytes 196
  115.4 13.1 %copy-start.27 = (bf16[2,2,2,2,4,32]{5,4,2,1,0,3:T(4,128)(2,1)S(1)}, bf16[2,2,2,2,4,32]{5,4,2,1,0,3:T(4,128)(2,1)}, u32[]{:S(2)}) copy-start(bf16[2,2,2,2,4,32]{5,4,2,1,0,3:T(4,128)(2,1)} %slice.243) | copy-start | bytes 12292
  115.4 13.1 %copy-start.21 = (bf16[2,32,1024]{2,1,0:T(8,128)(2,1)S(1)}, bf16[2,32,1024]{2,1,0:T(8,128)(2,1)}, u32[]{:S(2)}) copy-start(bf16[2,32,1024]{2,1,0:T(8,128)(2,1)} %get-tuple-element.64) | copy-start | bytes 393220
  115.4 13.3 %copy-start.14 = (bf16[2,128,1024]{2,1,0:T(8,128)(2,1)S(1)}, bf16[2,128,1024]{2,1,0:T(8,128)(2,1)}, u32[]{:S(2)}) copy-start(bf16[2,128,1024]{2,1,0:T(8,128)(2,1)} %param.37) | copy-start | bytes 1572868
  115.4 13.3 %copy-start.53 = (pred[2]{0:T(512)(128)(4,1)S(1)}, pred[2]{0:T(512)(128)(4,1)}, u32[]{:S(2)}) copy-start(pred[2]{0:T(512)(128)(4,1)} %get-tuple-element.263) | copy-start | bytes 10
  115.4 13.3 %copy-start.54 = (pred[2]{0:T(512)(128)(4,1)S(1)}, pred[2]{0:T(512)(128)(4,1)}, u32[]{:S(2)}) copy-start(pred[2]{0:T(512)(128)(4,1)} %get-tuple-element.264) | copy-start | bytes 10
  115.4 13.9 %copy-start.10 = (bf16[4,1,32,768]{3,2,1,0:T(8,128)(2,1)S(1)}, bf16[4,1,32,768]{3,2,1,0:T(8,128)(2,1)}, u32[]{:S(2)}) copy-start(bf16[4,1,32,768]{3,2,1,0:T(8,128)(2,1)} %get-tuple-element.233) | copy-start | bytes 589828
  128.6 2.6 copy-start.22
  135.4 2.6 copy-start.25
  135.4 2.8 copy-start.28
  135.4 7.3 %copy-start.2 = (bf16[32,128,1,32]{3,2,1,0:T(2,128)(2,1)S(1)}, bf16[32,128,1,32]{3,2,1,0:T(2,128)(2,1)}, u32[]{:S(2)}) copy-start(bf16[32,128,1,32]{3,2,1,0:T(2,128)(2,1)} %get-tuple-element.220) | copy-start | bytes 786436
  138.0 12.7 %copy-start.3 = (f32[128,1024]{1,0:T(8,128)}, f32[128,1024]{1,0:T(8,128)S(1)}, u32[]{:S(2)}) copy-start(f32[128,1024]{1,0:T(8,128)S(1)} %reshape.496) | copy-start | bytes 1572868
  138.0 8.6 %copy-start.38 = (pred[2,2]{1,0:T(4,128)(4,1)S(1)}, pred[2,2]{1,0:T(4,128)(4,1)}, u32[]{:S(2)}) copy-start(pred[2,2]{1,0:T(4,128)(4,1)} %broadcast_and_fusion) | copy-start | bytes 16
  138.0 10.0 %copy-start.56 = (bf16[32]{0:T(256)(128)(2,1)S(1)}, bf16[32]{0:T(256)(128)(2,1)}, u32[]{:S(2)}) copy-start(bf16[32]{0:T(256)(128)(2,1)} %param.42) | copy-start | bytes 196
  138.2 12.7 %copy-start.23 = (f32[1024]{0:T(1024)}, f32[1024]{0:T(1024)S(1)}, u32[]{:S(2)}) copy-start(f32[1024]{0:T(1024)S(1)} %reshape.497) | copy-start | bytes 12292
  150.7 0.8 copy-start
  150.7 158.0 %copy-start.31 = (f32[128]{0:T(128)}, f32[128]{0:T(128)S(1)}, u32[]{:S(2)}) copy-start(f32[128]{0:T(128)S(1)} %broadcast_multiply_fusion.2) | copy-start | bytes 1540
  151.5 157.2 %copy-start.33 = (f32[128]{0:T(128)}, f32[128]{0:T(128)S(1)}, u32[]{:S(2)}) copy-start(f32[128]{0:T(128)S(1)} %add_rsqrt_fusion) | copy-start | bytes 1540
  308.7 156.2 %copy-start.1 = (f32[128,1024]{1,0:T(8,128)S(1)}, f32[128,1024]{1,0:T(8,128)}, u32[]{:S(2)}) copy-start(f32[128,1024]{1,0:T(8,128)} %copy-done) | copy-start | bytes 1572868
  308.7 156.2 %copy-start.24 = (f32[1024]{0:T(1024)S(1)}, f32[1024]{0:T(1024)}, u32[]{:S(2)}) copy-start(f32[1024]{0:T(1024)} %copy-done.23) | copy-start | bytes 12292
  308.7 156.2 %copy-start.32 = (f32[128]{0:T(128)S(1)}, f32[128]{0:T(128)}, u32[]{:S(2)}) copy-start(f32[128]{0:T(128)} %copy-done.31) | copy-start | bytes 1540
  308.8 156.2 %copy-start.34 = (f32[128]{0:T(128)S(1)}, f32[128]{0:T(128)}, u32[]{:S(2)}) copy-start(f32[128]{0:T(128)} %copy-done.33) | copy-start | bytes 1540
  308.8 157.5 %copy-start.4 = (f32[128,1024]{1,0:T(8,128)S(1)}, f32[128,1024]{1,0:T(8,128)}, u32[]{:S(2)}) copy-start(f32[128,1024]{1,0:T(8,128)} %copy-done.3) | copy-start | bytes 1572868
  500.0 5.3 copy-start.9
  538.9 14.2 %copy-start.20 = (f32[32,1024]{1,0:T(8,128)S(1)}, f32[32,1024]{1,0:T(8,128)}, u32[]{:S(2)}) copy-start(f32[32,1024]{1,0:T(8,128)} %get-tuple-element.88) | copy-start | bytes 393220
  538.9 14.5 %copy-start.29 = (f32[2,1024]{1,0:T(2,128)S(1)}, f32[2,1024]{1,0:T(2,128)}, u32[]{:S(2)}) copy-start(f32[2,1024]{1,0:T(2,128)} %get-tuple-element.86) | copy-start | bytes 24580
  538.9 14.6 %copy-start.35 = (f32[2,768]{1,0:T(2,128)S(1)}, f32[2,768]{1,0:T(2,128)}, u32[]{:S(2)}) copy-start(f32[2,768]{1,0:T(2,128)} %get-tuple-element.85) | copy-start | bytes 18436
  538.9 14.9 %copy-start.26 = (f32[2,8,1024]{2,1,0:T(8,128)S(1)}, f32[2,8,1024]{2,1,0:T(8,128)}, u32[]{:S(2)}) copy-start(f32[2,8,1024]{2,1,0:T(8,128)} %get-tuple-element.84) | copy-start | bytes 196612
  551.3 3.2 copy-start.36
  551.3 3.2 copy-start.37
  551.3 3.3 copy-start.52
  553.0 2.9 copy-start.11
  558.8 28.8 %copy-start.12 = (f32[256,1024]{1,0:T(8,128)S(1)}, f32[256,1024]{1,0:T(8,128)}, u32[]{:S(2)}) copy-start(f32[256,1024]{1,0:T(8,128)} %get-tuple-element.92) | copy-start | bytes 3145732
  585.2 14.1 %copy-start.6 = (bf16[4,2,32,1792]{3,2,1,0:T(8,128)(2,1)S(1)}, bf16[4,2,32,1792]{3,2,1,0:T(8,128)(2,1)}, u32[]{:S(2)}) copy-start(bf16[4,2,32,1792]{3,2,1,0:T(8,128)(2,1)} %get-tuple-element.97) | copy-start | bytes 2752516
  587.7 29.7 %collective-permute-start.2 = (f32[128,32]{1,0:T(8,128)}, f32[128,32]{1,0:T(8,128)S(1)}, u32[]{:S(2)}, u32[]{:S(2)}) collective-permute-start(f32[128,32]{1,0:T(8,128)} %get-tuple-element.65), channel_id=1, source_target_pairs={{0,0},{1,1},{2,8},{3,9},{4,4},{5,5},{6,12},{7,13},{8,2},{9,3},{10,... | collective-permute-start | bytes 49160 | tf_op jit(solution)/shard_map/ppermute | solution.py:1622
  591.1 27.0 %collective-permute-start.3 = (f32[128,1024]{1,0:T(8,128)}, f32[128,1024]{1,0:T(8,128)}, u32[]{:S(2)}, u32[]{:S(2)}) collective-permute-start(f32[128,1024]{1,0:T(8,128)} %get-tuple-element.209), channel_id=1, source_target_pairs={{0,0},{1,1},{2,8},{3,9},{4,4},{5,5},{6,12},{7,13},{8,2},{9,3},{10,... | collective-permute-start | bytes 1572872 | tf_op jit(solution)/shard_map/ppermute | solution.py:1708
  599.3 1.2 copy-start.18
  605.0 2.3 copy-start.39
  610.8 2.4 copy-start.5
  614.1 4.0 copy-start.8
  614.9 5.1 copy-start.19

commit v3 on v0

--- a/solution.py
+++ b/solution.py
@@ -1,8 +1,11 @@
+import itertools
 import math
 
 import jax
 import jax.numpy as jnp
 from jax import lax
+from jax.experimental import pallas as pl
+from jax.experimental.pallas import tpu as pltpu
 from jax.sharding import PartitionSpec as P
 
 HEADS = 16
@@ -537,56 +540,1584 @@
     )
 
 
-def solution(mesh):
+MESH_ID = pl.DeviceIdType.MESH
+IN_VMEM = pl.BlockSpec(memory_space=pltpu.VMEM)
+ANYWHERE = pl.BlockSpec(memory_space=pl.ANY)
+AXES = ("y", "x", "c", "h", "l")
+Y_BIT, X_BIT, C_BIT, H_BIT, L_BIT = 16, 8, 4, 2, 1
+DEVICES = 32
+PIECES = 8
+PACK = 8
+RANKS = 4
+LOW, WIDE = jnp.bfloat16, jnp.float32
+
+
+def kernel_params(collective):
+    return pltpu.CompilerParams(
+        vmem_limit_bytes=62 * 2**20, collective_id=collective, has_side_effects=True
+    )
+
+
+def cost(micros):
+    return pl.CostEstimate(flops=int(micros * 1.1e9), bytes_accessed=2**20, transcendentals=0)
+
+
+def bits():
+    return tuple(lax.axis_index(axis) for axis in AXES)
+
+
+def index_of(y, x, c, h, l):
+    return y * 16 + x * 8 + c * 4 + h * 2 + l
+
+
+def turned_of(y, x, c, h, l):
+    return index_of(y, h, c, x, l)
+
+
+def flipped(mask):
+    return {
+        axis: 1 - lax.axis_index(axis)
+        for number, axis in enumerate(AXES)
+        if mask >> (len(AXES) - 1 - number) & 1
+    }
+
+
+def place_of(mask):
+    return [
+        1 - here if mask >> (len(AXES) - 1 - number) & 1 else here
+        for number, here in enumerate(bits())
+    ]
+
+
+def greet_all():
+    gate = pltpu.get_barrier_semaphore()
+    for mask in range(1, DEVICES):
+        pl.semaphore_signal(gate, inc=1, device_id=flipped(mask), device_id_type=MESH_ID)
+
+
+def all_greeted():
+    pl.semaphore_wait(pltpu.get_barrier_semaphore(), DEVICES - 1)
+
+
+def remote(source, target, send, receive, peer):
+    return pltpu.make_async_remote_copy(
+        source, target, send, receive, device_id=peer, device_id_type=MESH_ID
+    )
+
+
+class Swap:
+    def __init__(self, block_for, target, sends, receives, own_sem):
+        self.block_for, self.target = block_for, target
+        self.sends, self.receives, self.own_sem = sends, receives, own_sem
+
+    def own(self):
+        place = bits()
+        return pltpu.make_async_copy(
+            self.block_for(*place), self.target.at[index_of(*place)], self.own_sem
+        )
+
+    def copy(self, mask):
+        return remote(
+            self.block_for(*place_of(mask)),
+            self.target.at[index_of(*bits())],
+            self.sends.at[mask - 1],
+            self.receives.at[mask - 1],
+            flipped(mask),
+        )
+
+    def start(self):
+        self.own().start()
+        for mask in range(1, DEVICES):
+            self.copy(mask).start()
+
+    def arrived(self):
+        self.own().wait()
+        for mask in range(1, DEVICES):
+            self.copy(mask).wait_recv()
+
+    def sent(self):
+        for mask in range(1, DEVICES):
+            self.copy(mask).wait_send()
+
+
+def swap_sems():
+    return [
+        pltpu.SemaphoreType.DMA((DEVICES - 1,)),
+        pltpu.SemaphoreType.DMA((DEVICES - 1,)),
+        pltpu.SemaphoreType.DMA,
+    ]
+
+
+class Move:
+    def __init__(self, pairs, same, mask, sends, receives):
+        self.pairs, self.same, self.mask = pairs, same, mask
+        self.sends, self.receives = sends, receives
+
+    def each(self, action):
+        @pl.when(self.same)
+        def _():
+            for number, (source, target) in enumerate(self.pairs):
+                copy = pltpu.make_async_copy(source, target, self.receives.at[number])
+                copy.start() if action == "start" else copy.wait()
+
+        @pl.when(jnp.logical_not(self.same))
+        def _():
+            for number, (source, target) in enumerate(self.pairs):
+                copy = remote(
+                    source,
+                    target,
+                    self.sends.at[number],
+                    self.receives.at[number],
+                    flipped(self.mask),
+                )
+                copy.start() if action == "start" else copy.wait()
+
+    def start(self):
+        self.each("start")
+
+    def done(self):
+        self.each("wait")
+
+
+def put_lanes(target, value):
+    for q in range(value.shape[1] // 128):
+        target[q] = value[:, q * 128 : (q + 1) * 128]
+
+
+def get_lanes(source, width):
+    return jnp.concatenate([source[q] for q in range(width // 128)], axis=1)
+
+
+def bounds_of(ends, frames):
+    before = [jnp.zeros_like(ends[0])] + ends[:-1]
+    return [jnp.where(end > last, end, float(frames)) for end, last in zip(ends, before)]
+
+
+def rank_lanes(bounds, frames, width):
+    shape = (frames // PACK, 8, PACK * width)
+    frame = lax.broadcasted_iota(jnp.int32, shape, 0) * PACK
+    frame = frame + lax.broadcasted_iota(jnp.int32, shape, 2) // width
+    rank = jnp.zeros(shape, jnp.int32)
+    for bound in bounds:
+        rank = rank + (frame >= bound[None].astype(jnp.int32)).astype(jnp.int32)
+    return rank.reshape(frames, PACK * width)
+
+
+def spread_ranks(wide, packed, rank, first):
+    lines = packed.shape[0]
+    wide[...] = jnp.zeros_like(wide)
+    for number in range(RANKS):
+        place = pl.ds(first + number * 64, lines)
+        wide[place, :] += jnp.where(rank == number, packed, 0.0)
+
+
+def collect_ranks(summed, rank, lines):
+    result = jnp.zeros((lines, summed.shape[1]), WIDE)
+    for number in range(RANKS):
+        result = jnp.where(rank == number, summed[number * 64 : number * 64 + lines, :], result)
+    return result
+
+
+def fill_pair(wide, even, odd):
+    length = even.shape[0]
+    even[...] = wide[:length, :].astype(LOW)
+    odd[...] = wide[8 : 8 + length, :].astype(LOW)
+
+
+def shifted(even, odd, step, length):
+    source = even if step % 2 == 0 else odd
+    return source[pl.ds((step - step % 2) * 8, length), :]
+
+
+def normed(tensor, gain, shift):
+    average = jnp.mean(tensor, axis=-1, keepdims=True)
+    centred = tensor - average
+    spread = jnp.mean(centred * centred, axis=-1, keepdims=True)
+    return centred * lax.rsqrt(spread + epsilon) * gain + shift
+
+
+def normed_back(tensor, gain, upstream):
+    average = jnp.mean(tensor, axis=-1, keepdims=True)
+    centred = tensor - average
+    spread = jnp.mean(centred * centred, axis=-1, keepdims=True)
+    inverse = lax.rsqrt(spread + epsilon)
+    unit = centred * inverse
+    scaled = upstream * gain
+    result = inverse * (
+        scaled
+        - jnp.mean(scaled, axis=-1, keepdims=True)
+        - unit * jnp.mean(scaled * unit, axis=-1, keepdims=True)
+    )
+    return (
+        result,
+        jnp.sum(upstream * unit, axis=0, keepdims=True),
+        jnp.sum(upstream, axis=0, keepdims=True),
+    )
+
+
+def gelu_pair(tensor):
+    half = 0.5 * (1.0 + lax.erf(tensor * (2.0**-0.5)))
+    slope = half + tensor * (jnp.exp(-0.5 * tensor * tensor) * ((2.0 * math.pi) ** -0.5))
+    return tensor * half, slope
+
+
+def dot(left, right):
+    return jnp.dot(left, right, preferred_element_type=WIDE)
+
+
+def dot_rt(left, right):
+    return lax.dot_general(left, right, (((1,), (1,)), ((), ())), preferred_element_type=WIDE)
+
+
+def dot_lt(left, right):
+    return lax.dot_general(left, right, (((0,), (0,)), ((), ())), preferred_element_type=WIDE)
+
+
+def group_gather(block, t, sends, receives, ready, use):
+    half = block.shape[1] // 2
+    x_peer, l_peer = flipped(X_BIT), flipped(L_BIT)
+    own = block.at[t]
+    to_x = remote(own, own, sends.at[0], receives.at[0], x_peer)
+    to_x.start()
+    to_l = remote(own, own, sends.at[1], receives.at[1], l_peer)
+    to_l.start()
+    ready()
+    use(t)
+    to_x.wait_recv()
+    other = block.at[lax.bitwise_xor(t, 2), pl.ds(0, half)]
+    on_l = remote(other, other, sends.at[2], receives.at[2], l_peer)
+    on_l.start()
+    to_l.wait_recv()
+    other = block.at[lax.bitwise_xor(t, 1), pl.ds(half, half)]
+    on_x = remote(other, other, sends.at[3], receives.at[3], x_peer)
+    on_x.start()
+    use(lax.bitwise_xor(t, 2))
+    use(lax.bitwise_xor(t, 1))
+    on_l.wait_recv()
+    on_x.wait_recv()
+    use(lax.bitwise_xor(t, 3))
+    for copy in (to_x, to_l, on_l, on_x):
+        copy.wait_send()
+
+
+def group_scatter(part, t, low, got, sends, receives, between=None):
+    half = low.shape[1]
+    x_peer, l_peer = flipped(X_BIT), flipped(L_BIT)
+
+    def send(slot, value, peer):
+        low[slot] = value.astype(LOW)
+        copy = remote(low.at[slot], got.at[slot], sends.at[slot], receives.at[slot], peer)
+        copy.start()
+        return copy
+
+    def arrived(slot):
+        return got[slot].astype(WIDE)
+
+    far = part(lax.bitwise_xor(t, 3))
+    far_x = send(0, far[:half], x_peer)
+    far_l = send(1, far[half:], l_peer)
+    beside_x = part(lax.bitwise_xor(t, 2))
+    near_x = send(2, beside_x[:half], x_peer)
+    beside_l = part(lax.bitwise_xor(t, 1))
+    near_l = send(3, beside_l[half:], l_peer)
+    far_x.wait_recv()
+    on_l = send(4, beside_l[:half] + arrived(0), l_peer)
+    far_l.wait_recv()
+    on_x = send(5, beside_x[half:] + arrived(1), x_peer)
+    own = part(t)
+    if between is not None:
+        between()
+    near_x.wait_recv()
+    near_l.wait_recv()
+    on_l.wait_recv()
+    on_x.wait_recv()
+    result = jnp.concatenate(
+        [own[:half] + arrived(2) + arrived(4), own[half:] + arrived(3) + arrived(5)], axis=0
+    )
+    for copy in (far_x, far_l, near_x, near_l, on_l, on_x):
+        copy.wait_send()
+    return result
+
+
+def group_scratch(n, width):
+    return [
+        pltpu.VMEM((6, n // 2, width), LOW),
+        pltpu.VMEM((6, n // 2, width), LOW),
+        pltpu.SemaphoreType.DMA((4,)),
+        pltpu.SemaphoreType.DMA((4,)),
+        pltpu.SemaphoreType.DMA((6,)),
+        pltpu.SemaphoreType.DMA((6,)),
+    ]
+
+
+def block_rows(j, n):
+    return pl.ds(pl.multiple_of(j * n, n), n)
+
+
+def slots():
+    return [(c, y, h) for c in range(2) for y in range(2) for h in range(2)]
+
+
+class Spread:
+    def __init__(self, held, sends, receives):
+        self.held, self.sends, self.receives = held, sends, receives
+
+    def copy(self, step):
+        y, _, c, h, _ = bits()
+        own = c * 4 + y * 2 + h
+        near = c * 4 + y * 2 + 1 - h
+        view = self.held.at[(pl.ds(own, 1), pl.ds(own, 1), pl.ds(near, 1), pl.ds(c * 4, 4))[step]]
+        peer = flipped((H_BIT, Y_BIT, Y_BIT, C_BIT)[step])
+        return remote(view, view, self.sends.at[step], self.receives.at[step], peer)
+
+    def begin(self):
+        self.copy(0).start()
+        self.copy(1).start()
+
+    def forward(self):
+        self.copy(0).wait_recv()
+        self.copy(2).start()
+
+    def over_c(self):
+        self.copy(1).wait_recv()
+        self.copy(2).wait_recv()
+        self.copy(3).start()
+
+    def done(self):
+        self.copy(3).wait_recv()
+        for step in range(4):
+            self.copy(step).wait_send()
+
+
+def load_rows(held, target, sem, share, column, width):
+    for slot, (c, y, h) in enumerate(slots()):
+        for x in range(2):
+            pltpu.make_async_copy(
+                held.at[slot, pl.ds(x * 2 * share, 2 * share), pl.ds(column, width)],
+                target.at[pl.ds((y * 16 + x * 8 + c * 4 + h * 2) * share, 2 * share), :],
+                sem,
+            ).start()
+
+
+def load_chunks(held, target, sem, share, column, width):
+    for slot, (c, y, h) in enumerate(slots()):
+        for chunk in range(4):
+            pltpu.make_async_copy(
+                held.at[slot, pl.ds(chunk * share, share), pl.ds(column, width)],
+                target.at[pl.ds((y * 4 + c * 2 + h) * share, share), pl.ds(chunk * width, width)],
+                sem,
+            ).start()
+
+
+def load_blocks(held, target, sem, first, share):
+    for slot, (c, y, h) in enumerate(slots()):
+        pltpu.make_async_copy(
+            held.at[slot, pl.ds(first, share)],
+            target.at[pl.ds((y * 4 + c * 2 + h) * share, share), :],
+            sem,
+        ).start()
+
+
+def load_line(held, target, sem, first, width):
+    for slot, (c, y, h) in enumerate(slots()):
+        pltpu.make_async_copy(
+            held.at[slot, pl.ds(first, 16), pl.ds(0, width)],
+            target.at[:, pl.ds((y * 4 + c * 2 + h) * width, width)],
+            sem,
+        ).start()
+
+
+def settle(target, sem):
+    pltpu.make_async_copy(target, target, sem).wait()
+
+
+def relative(target, c, y, h):
+    y_me, _, c_me, h_me, _ = bits()
+    return target.at[
+        lax.bitwise_xor(c_me, c), lax.bitwise_xor(y_me, y), lax.bitwise_xor(h_me, h)
+    ]
+
+
+def store_rows(target, grads, share, column):
+    width = grads.shape[1]
+    for c, y, h in slots():
+        for x in range(2):
+            row = (y * 16 + x * 8 + c * 4 + h * 2) * share
+            relative(target, c, y, h)[
+                x * 2 * share : (x + 1) * 2 * share, column : column + width
+            ] = grads[row : row + 2 * share, :].astype(LOW)
+
+
+def store_chunks(target, grads, share, column):
+    width = grads.shape[1] // 4
+    for c, y, h in slots():
+        row = (y * 4 + c * 2 + h) * share
+        for chunk in range(4):
+            relative(target, c, y, h)[
+                chunk * share : (chunk + 1) * share, column : column + width
+            ] = grads[row : row + share, chunk * width : (chunk + 1) * width].astype(LOW)
+
+
+def store_blocks(target, grads, first, share):
+    for c, y, h in slots():
+        row = (y * 4 + c * 2 + h) * share
+        relative(target, c, y, h)[first : first + share, :] = grads[row : row + share, :].astype(LOW)
+
+
+class Gather:
+    def __init__(self, parts, got_c, got_y, got_h, sends, receives):
+        self.parts, self.got = parts, (got_c, got_y, got_h)
+        self.sends, self.receives = sends, receives
+
+    def copy(self, step):
+        source = (self.parts.at[1], self.parts.at[0, 1], self.parts.at[0, 0, 1])[step]
+        return remote(
+            source,
+            self.got[step],
+            self.sends.at[step],
+            self.receives.at[step],
+            flipped((C_BIT, Y_BIT, H_BIT)[step]),
+        )
+
+    def over_c(self):
+        self.copy(0).start()
+
+    def over_y(self):
+        self.copy(0).wait_recv()
+        for y in (1, 0):
+            for h in range(2):
+                summed = self.parts[0, y, h].astype(WIDE) + self.got[0][y, h].astype(WIDE)
+                self.parts[0, y, h] = summed.astype(LOW)
+            if y == 1:
+                self.copy(1).start()
+
+    def over_h(self):
+        self.copy(1).wait_recv()
+        for h in (1, 0):
+            summed = self.parts[0, 0, h].astype(WIDE) + self.got[1][h].astype(WIDE)
+            self.parts[0, 0, h] = summed.astype(LOW)
+            if h == 1:
+                self.copy(2).start()
+
+    def done(self):
+        self.copy(2).wait_recv()
+        for step in range(3):
+            self.copy(step).wait_send()
+
+    def total(self, first, last):
+        return self.parts[0, 0, 0, first:last, :].astype(WIDE) + self.got[2][first:last, :].astype(WIDE)
+
+
+class Sizes:
+    def __init__(self, n, width, inner, layers, taps, vocab):
+        self.n, self.width, self.inner, self.layers = n, width, inner, layers
+        self.taps, self.vocab = taps, vocab
+        self.count = 4 * n
+        self.part = width // 4
+        self.head = width // HEADS
+        self.heads = self.part // self.head
+        self.share = width // DEVICES
+        self.inner_share = inner // PIECES
+        self.scale = self.head**-0.5
+        self.group_width = width // CONV_G
+        self.packs = n // PACK
+        self.steps = taps // PACK + 1
+        self.length = self.count + (RANKS - 1) * 64
+        self.lines = self.length + 128
+        self.held_rows = (4 * self.share, 4 * self.share, self.inner_share + 16)
+        self.grad_rows = (4 * self.share + 16, 4 * self.share, self.inner_share + 16)
+        self.bundles = 3 * layers
+        self.at = {"entry": 0, "base": 1}
+        at = 2
+        for name in ("attend", "middle", "lower", "return", "final", "upper"):
+            self.at[name] = at
+            at += layers
+        self.vectors = at
+        self.at["head"] = at
+        self.at["heads"] = at + vocab
+        self.named = at + vocab + 2 * layers
+        self.line = -(-(self.named + 1) // 8) * 8
+        self.gathered = 64
+
+    def saved(self):
+        n, count, layers, width = self.n, self.count, self.layers, self.width
+        return [
+            ((layers, 4, n, width), LOW),
+            ((layers, count, 3 * self.part), LOW),
+            ((layers, self.heads * count, count), LOW),
+            ((layers, count, self.part), LOW),
+            ((layers, n, width), WIDE),
+            ((layers, 4, n, width), LOW),
+            ((layers, count, self.inner), LOW),
+            ((layers, count, self.inner), LOW),
+            ((layers, n, width), WIDE),
+        ]
+
+
+def forward(z, features, cot_turned, kernel_weight, small, head_weight, ends_own, hidden_bias, joint_weight, expand_weight, output_weight, reduce_weight):
+    kept = z.saved()
+    kinds = len(kept)
+    layers, n, width, part, inner, share = z.layers, z.n, z.width, z.part, z.inner, z.share
+    count, head, heads, packs, gw = z.count, z.head, z.heads, z.packs, z.group_width
+    depth, own_width = PACK * gw, PACK * share
+
+    def kernel(*refs):
+        (f_ref, cot_ref, k_ref, small_ref, head_ref, e_ref, hb_ref, jw_ref, ew_ref, ow_ref, rw_ref) = refs[:11]
+        rest = refs[11:]
+        (logits_ref, flow_ref, part_ref, whole, mixed_ref, bend_ref, ends_ref) = rest[:7]
+        even_out, odd_out, taps_out = rest[7:10]
+        held = rest[10 : 10 + z.bundles]
+        saved = rest[10 + z.bundles : 10 + z.bundles + kinds]
+        rest = rest[10 + z.bundles + kinds :]
+        (x_all, qkv, weights_low, context, residual, m_all, active, slope, outer) = rest[:kinds]
+        (now, wj, wo, we, wr, hb, low_buf, got, gs, gr, ss, sr) = rest[kinds : kinds + 12]
+        (bs, br, ws, ks, tokens, messages, feats, small_all, packed, wide, even, odd, taps, out_messages) = rest[kinds + 12 : kinds + 26]
+        (pres, new_feats, cot, logits_own, cs, cr, rs, fs, ms, mr, lines_out) = rest[kinds + 26 : kinds + 37]
+        (cols, hidden_lines, gathering, message) = rest[kinds + 37 : kinds + 41]
+        swap1, swap2, swap3 = (rest[kinds + 41 + 3 * k : kinds + 44 + 3 * k] for k in range(3))
+        y, x, c, h, l = bits()
+        t = x * 2 + l
+        slot = c * 4 + y * 2 + h
+
+        put_lanes(tokens, f_ref[...].astype(WIDE))
+        for f in range(0, PACK, 2):
+            for q in range(width // 128):
+                pair = [tokens[q, pl.ds(f + k, packs, stride=PACK), :] for k in range(2)]
+                for k in range(2):
+                    messages[2 * q + k, :, f * gw : (f + 2) * gw] = jnp.concatenate(
+                        [piece[:, k * gw : (k + 1) * gw] for piece in pair], axis=1
+                    ).astype(LOW)
+        def column_copies():
+            copies = []
+            for layer in range(layers):
+                for kind, (first, span) in enumerate(((0, 3 * part), (3 * part, inner))):
+                    target = held[3 * layer + kind].at[slot, pl.ds(t * share, share), pl.ds(0, span)]
+                    for number, mask in enumerate((0, L_BIT, X_BIT, X_BIT | L_BIT)):
+                        place = place_of(mask)
+                        source = cols.at[place[1] * 2 + place[4], layer, :, pl.ds(first, span)]
+                        if mask == 0:
+                            copy = pltpu.make_async_copy(source, target, cr.at[layer, kind, 0])
+                        else:
+                            copy = remote(
+                                source, target, cs.at[layer, kind, number], cr.at[layer, kind, number], flipped(mask)
+                            )
+                        copies.append((3 * layer + kind, mask, copy))
+            return copies
+
+        def row_copies():
+            copies = []
+            for layer in range(layers):
+                for kind, (source, first) in enumerate(((rw_ref, 0), (hidden_lines, z.inner_share))):
+                    target = held[3 * layer + 2].at[slot, pl.ds(first, source.shape[1])]
+                    copies.append((3 * layer + 2, pltpu.make_async_copy(source.at[layer], target, rs.at[layer, kind])))
+            return copies
+
+        moves = []
+        for layer in range(layers):
+            pairs = [
+                (
+                    ow_ref.at[layer, :, pl.ds(chunk * part, part)],
+                    held[3 * layer].at[
+                        c * 4 + y * 2 + l, pl.ds(chunk * share, share), pl.ds(3 * part, part)
+                    ],
+                )
+                for chunk in range(4)
+            ]
+            moves.append(Move(pairs, h == l, H_BIT | L_BIT, ms.at[layer], mr.at[layer]))
+        column_all, row_all = column_copies(), row_copies()
+        greet_all()
+        hidden_lines[...] = jnp.zeros_like(hidden_lines)
+        for layer in range(layers):
+            hidden_lines[layer, :, 0 : z.inner_share] = jnp.broadcast_to(
+                hb_ref[layer : layer + 1, :].astype(WIDE), (16, z.inner_share)
+            ).astype(LOW)
+        for _, copy in row_all:
+            copy.start()
+
+        for x_at in range(2):
+            for l_at in range(2):
+                for layer in range(layers):
+                    for which in range(3):
+                        for y_at in range(2):
+                            cuts = [
+                                which * width + (y_at * 8 + x_at * 4 + c_at * 2 + l_at) * head for c_at in range(2)
+                            ]
+                            at = which * part + y_at * 2 * head
+                            cols[x_at * 2 + l_at, layer, :, at : at + 2 * head] = jnp.concatenate(
+                                [jw_ref[layer, :, cut : cut + head] for cut in cuts], axis=1
+                            )
+                    for c_at, y_at, h_at in slots():
+                        cut = index_of(y_at, x_at, c_at, h_at, l_at) * z.inner_share
+                        at = 3 * part + (y_at * 4 + c_at * 2 + h_at) * z.inner_share
+                        cols[x_at * 2 + l_at, layer, :, at : at + z.inner_share] = ew_ref[
+                            layer, :, cut : cut + z.inner_share
+                        ]
+        same = lax.broadcasted_iota(jnp.int32, (share, share), 0) == lax.broadcasted_iota(jnp.int32, (share, share), 1)
+        unit = jnp.where(same, 1.0, 0.0).astype(LOW)
+        lines_low = small_ref[...].astype(WIDE)
+        gathering[...] = jnp.zeros_like(gathering)
+        gathering[0 : z.vectors, 0:share] = lines_low[0 : z.vectors]
+        gathering[z.vectors : z.at["heads"], 0:share] = dot_lt(head_ref[...], unit)
+        gathering[z.at["heads"] : z.named, 0:share] = lines_low[z.vectors : z.vectors + 2 * layers]
+        own_ends = e_ref[...]
+        gathering[z.named : z.named + 1, 0:4] = lax.shift_right_logical(own_ends, 5).astype(WIDE)
+        gathering[z.named : z.named + 1, 4:8] = lax.bitwise_and(own_ends, 31).astype(WIDE)
+        per_line = 128 // share
+        message_lines = gathering.shape[0] // per_line
+        message[...] = jnp.concatenate(
+            [gathering[pl.ds(k, message_lines, stride=per_line), :][:, 0:share] for k in range(per_line)], axis=1
+        ).astype(LOW)
+        position = jnp.concatenate([lines_low[z.vectors + 2 * layers : z.vectors + 2 * layers + 1]] * PACK, axis=1)
+
+        jobs = [Spread(held[b], bs.at[b], br.at[b]) for b in range(z.bundles)]
+        all_greeted()
+
+        def launch(layer):
+            for number, _, copy in column_all:
+                if number // 3 == layer:
+                    copy.start()
+            moves[layer].start()
+
+        launch(0)
+        to_owners = Swap(lambda *place: messages.at[index_of(*place) // 2], feats, *swap1)
+        to_owners.start()
+        vectors = Swap(lambda *place: message, small_all, *swap2)
+        vectors.start()
+        frames_move = Move([(f_ref, new_feats), (cot_ref, cot)], x == h, X_BIT | H_BIT, fs.at[0], fs.at[1])
+        frames_move.start()
+        for layer in range(1, layers):
+            launch(layer)
+
+        def own_ready(bundle):
+            for number, mask, copy in column_all:
+                if number == bundle:
+                    if mask:
+                        copy.wait_recv()
+                        copy.wait_send()
+                    else:
+                        copy.wait()
+            for number, copy in row_all:
+                if number == bundle:
+                    copy.wait()
+            if bundle % 3 == 0:
+                moves[bundle // 3].done()
+            jobs[bundle].begin()
+
+        own_ready(2)
+
+        def keep(source, target, sem):
+            pltpu.make_async_copy(source, target, sem).start()
+
+        span = z.taps * gw
+        for step in range(z.steps):
+            taps[step] = jnp.zeros((own_width, depth), LOW)
+        for f in range(PACK):
+            lines = slice(f * share, (f + 1) * share)
+            shift = f * gw
+            for step in range(z.steps):
+                begin = max(step * depth - shift, 0)
+                end = min((step + 1) * depth - shift, span)
+                at = begin + shift - step * depth
+                if begin < end:
+                    taps[step, lines, at : at + end - begin] = k_ref[:, begin:end]
+        keep(taps, taps_out, ks.at[kinds, 0])
+
+        own_ready(0)
+        own_ready(1)
+        to_owners.arrived()
+        jobs[2].forward()
+        vectors.arrived()
+        for at in range(DEVICES):
+            place = pl.ds((at % 4) * packs * 8 + at // 4, packs, stride=8)
+            for q in range(depth // 128):
+                packed[q, place, :] = feats[at, :, q * 128 : (q + 1) * 128].astype(WIDE)
+        line, lane = z.named * share // 128, z.named * share % 128
+        encoded = jnp.concatenate(
+            [small_all[4 * row, line : line + 1, :].astype(WIDE) for row in range(8)], axis=0
+        )
+        ends_ref[...] = encoded
+        ends = [
+            encoded[:, lane + k : lane + k + 1] * 32.0 + encoded[:, lane + 4 + k : lane + 5 + k]
+            for k in range(4)
+        ]
+        bounds = bounds_of(ends, count)
+        spread_ranks(wide, get_lanes(packed, depth), rank_lanes(bounds, count, gw), 64)
+        fill_pair(wide, even, odd)
+        keep(even, even_out, ks.at[kinds, 1])
+        keep(odd, odd_out, ks.at[kinds + 1, 0])
+        summed = jnp.zeros((z.length, own_width), WIDE)
+        for step in range(z.steps):
+            summed = summed + dot_rt(shifted(even, odd, step, z.length), taps[step])
+            if step == z.steps // 2:
+                jobs[0].forward()
+        made = collect_ranks(summed, rank_lanes(bounds, count, share), count) + position
+        put_lanes(packed, made)
+        for at in range(DEVICES):
+            place = pl.ds((at % 4) * packs * 8 + at // 4, packs, stride=8)
+            for q in range(own_width // 128):
+                out_messages[at, :, q * 128 : (q + 1) * 128] = packed[q, place, :].astype(LOW)
+        to_frames = Swap(lambda *place: out_messages.at[turned_of(*place)], pres, *swap3)
+        to_frames.start()
+        jobs[0].over_c()
+        jobs[2].over_c()
+        own_ready(3)
+
+        for q in range(width // 128):
+            for k in range(per_line):
+                cut = slice(k * share, (k + 1) * share)
+                lines_out[q, pl.ds(k, message_lines, stride=per_line), :] = jnp.concatenate(
+                    [small_all[at, :, cut].astype(WIDE) for at in range(4 * q, 4 * q + 4)], axis=1
+                )
+        whole[...] = get_lanes(lines_out, width)
+
+        def vector(name, layer=0):
+            at = z.at[name] + layer
+            return whole[at : at + 1, :]
+
+        heads_lines = jnp.zeros((2 * layers, part), WIDE)
+        for x_at in range(2):
+            for l_at in range(2):
+                cuts = [
+                    whole[
+                        z.at["heads"] : z.at["heads"] + 2 * layers,
+                        (y_at * 16 + x_at * 8 + c_at * 4 + l_at * 2) * share : (y_at * 16 + x_at * 8 + c_at * 4 + l_at * 2 + 2) * share,
+                    ]
+                    for y_at in range(2)
+                    for c_at in range(2)
+                ]
+                heads_lines = jnp.where(t == x_at * 2 + l_at, jnp.concatenate(cuts, axis=1), heads_lines)
+        mine = lax.broadcasted_iota(jnp.int32, (8, 1), 0) == y * 4 + h * 2 + c
+        row_ends = [jnp.sum(jnp.where(mine, end, 0.0), axis=0, keepdims=True).astype(jnp.int32) for end in ends]
+        across = lax.broadcasted_iota(jnp.int32, (1, count), 1)
+        down = lax.broadcasted_iota(jnp.int32, (count, 1), 0)
+        across = sum((across >= end).astype(jnp.int32) for end in row_ends)
+        down = sum((down >= end).astype(jnp.int32) for end in row_ends)
+        linked = down == across
+
+        frames_move.done()
+        to_frames.arrived()
+        jobs[1].forward()
+        own_ready(5)
+        own_ready(4)
+        for f in range(PACK):
+            cut = slice(f * share, (f + 1) * share)
+            for q in range(width // 128):
+                tokens[q, pl.ds(f, packs, stride=PACK), :] = jnp.concatenate(
+                    [pres[at, :, cut].astype(WIDE) for at in range(4 * q, 4 * q + 4)], axis=1
+                )
+        made, bent = gelu_pair(get_lanes(tokens, width))
+        bend_ref[...] = bent
+        mixed = new_feats[...].astype(WIDE) + made
+        mixed_ref[...] = mixed
+        now[...] = normed(mixed, vector("entry"), vector("base"))
+
+        for layer in range(layers):
+            first, second, third = jobs[3 * layer : 3 * layer + 3]
+            later = jobs[3 * layer + 3 : 3 * layer + 6]
+            x_all[layer, t] = now[...].astype(LOW)
+
+            def attend_ready(layer=layer, first=first):
+                first.done()
+                load_rows(held[3 * layer], wj, ws.at[0], share, 0, 3 * part)
+                load_chunks(held[3 * layer], wo, ws.at[1], share, 3 * part, part)
+                settle(wj, ws.at[0])
+
+            def attend_use(j, layer=layer):
+                lines = block_rows(j, n)
+                made = dot(x_all[layer, j], wj[...])
+                qkv[layer, lines, 0:part] = ((made[:, 0:part] + heads_lines[layer : layer + 1]) * z.scale).astype(LOW)
+                qkv[layer, lines, part : 2 * part] = made[:, part : 2 * part].astype(LOW)
+                qkv[layer, lines, 2 * part :] = (
+                    made[:, 2 * part :] + heads_lines[layers + layer : layers + layer + 1]
+                ).astype(LOW)
+
+            group_gather(x_all.at[layer], t, gs, gr, attend_ready, attend_use)
+            if layer == 0:
+                second.over_c()
+                later[0].forward()
+            keep(x_all.at[layer], saved[0].at[layer], ks.at[0, layer])
+            keep(qkv.at[layer], saved[1].at[layer], ks.at[1, layer])
+            for at in range(heads):
+                queries = qkv[layer, :, at * head : (at + 1) * head]
+                keys = qkv[layer, :, part + at * head : part + (at + 1) * head]
+                values = qkv[layer, :, 2 * part + at * head : 2 * part + (at + 1) * head]
+                scores = jnp.where(linked, dot_rt(queries, keys), masked_score)
+                exponent = jnp.exp(scores - jnp.max(scores, axis=-1, keepdims=True))
+                inverse = 1.0 / jnp.sum(exponent, axis=-1, keepdims=True)
+                made = (exponent * inverse).astype(LOW)
+                weights_low[layer, at * count : (at + 1) * count, :] = made
+                context[layer, :, at * head : (at + 1) * head] = dot(made, values).astype(LOW)
+            keep(weights_low.at[layer], saved[2].at[layer], ks.at[2, layer])
+            keep(context.at[layer], saved[3].at[layer], ks.at[3, layer])
+            settle(wo, ws.at[1])
+
+            def advance(later=later):
+                if later:
+                    later[0].over_c()
+
+            attended = group_scatter(
+                lambda j: dot(context[layer, block_rows(j, n), :], wo[...]), t, low_buf, got, ss, sr, advance
+            )
+            residual[layer] = now[...] + (attended + vector("attend", layer))
+            keep(residual.at[layer], saved[4].at[layer], ks.at[4, layer])
+            middle = normed(residual[layer], vector("middle", layer), vector("lower", layer))
+            now[...] = middle
+            m_all[layer, t] = middle.astype(LOW)
+
+            def feed_ready(layer=layer, second=second, third=third):
+                second.done()
+                load_rows(held[3 * layer + 1], we, ws.at[2], share, 0, inner)
+                third.done()
+                load_line(held[3 * layer + 2], hb, ws.at[4], z.inner_share, z.inner_share)
+                load_blocks(held[3 * layer + 2], wr, ws.at[3], 0, z.inner_share)
+                settle(we, ws.at[2])
+                settle(hb, ws.at[4])
+
+            def feed_use(j, layer=layer):
+                lines = block_rows(j, n)
+                made, bent = gelu_pair(dot(m_all[layer, j], we[...]) + hb[0:1, :].astype(WIDE))
+                active[layer, lines, :] = made.astype(LOW)
+                slope[layer, lines, :] = bent.astype(LOW)
+
+            group_gather(m_all.at[layer], t, gs, gr, feed_ready, feed_use)
+            if later:
+                later[2].forward()
+            keep(m_all.at[layer], saved[5].at[layer], ks.at[5, layer])
+            keep(active.at[layer], saved[6].at[layer], ks.at[6, layer])
+            keep(slope.at[layer], saved[7].at[layer], ks.at[7, layer])
+            settle(wr, ws.at[3])
+
+            def advance_more(later=later):
+                if later:
+                    later[1].forward()
+                    later[2].over_c()
+
+            fed = group_scatter(
+                lambda j: dot(active[layer, block_rows(j, n), :], wr[...]), t, low_buf, got, ss, sr, advance_more
+            )
+            outer[layer] = now[...] + fed + vector("return", layer)
+            keep(outer.at[layer], saved[8].at[layer], ks.at[8, layer])
+            now[...] = normed(outer[layer], vector("final", layer), vector("upper", layer))
+            if later:
+                later[1].over_c()
+        final_low = now[...].astype(LOW)
+        head_turned = whole[z.at["head"] : z.at["head"] + z.vocab, :].astype(LOW)
+        vocab_at = z.vectors + 2 * layers + 1
+        vocab_bias = lines_low[vocab_at : vocab_at + 1, :].astype(LOW)
+        logits_own[...] = dot_rt(head_turned, final_low) + dot_lt(vocab_bias, jnp.ones((1, n), LOW))
+        logits_move = Move([(logits_own, logits_ref)], x == h, X_BIT | H_BIT, fs.at[2], fs.at[3])
+        logits_move.start()
+        flow_ref[...] = dot_lt(cot[...], head_turned)
+        part_ref[...] = dot(cot[...], final_low)
+        vocab_sum = dot_rt(jnp.ones((8, n), LOW), cot[...])
+        vocab_sum = jnp.concatenate([vocab_sum] * (128 // z.vocab), axis=1)
+        whole[z.line : z.line + 8, :] = jnp.concatenate([vocab_sum] * (width // 128), axis=1)
+        logits_move.done()
+        to_owners.sent()
+        vectors.sent()
+        to_frames.sent()
+        for kind in range(kinds):
+            for layer in range(layers):
+                settle(saved[kind].at[layer], ks.at[kind, layer])
+        settle(taps_out, ks.at[kinds, 0])
+        settle(even_out, ks.at[kinds, 1])
+        settle(odd_out, ks.at[kinds + 1, 0])
+
+    outs = pl.pallas_call(
+        kernel,
+        out_shape=[
+            jax.ShapeDtypeStruct((z.vocab, n), WIDE),
+            jax.ShapeDtypeStruct((n, width), WIDE),
+            jax.ShapeDtypeStruct((z.vocab, width), WIDE),
+            jax.ShapeDtypeStruct((z.gathered, width), WIDE),
+            jax.ShapeDtypeStruct((n, width), WIDE),
+            jax.ShapeDtypeStruct((n, width), WIDE),
+            jax.ShapeDtypeStruct((8, 128), WIDE),
+            jax.ShapeDtypeStruct((z.lines, depth), LOW),
+            jax.ShapeDtypeStruct((z.lines, depth), LOW),
+            jax.ShapeDtypeStruct((z.steps, own_width, depth), LOW),
+        ]
+        + [jax.ShapeDtypeStruct((PIECES, z.held_rows[b % 3], width), LOW) for b in range(z.bundles)]
+        + [jax.ShapeDtypeStruct(shape, kind) for shape, kind in kept],
+        in_specs=[IN_VMEM] * 9 + [ANYWHERE] * 2,
+        out_specs=[IN_VMEM] * 7 + [ANYWHERE] * (3 + z.bundles + kinds),
+        scratch_shapes=[pltpu.VMEM(shape, kind) for shape, kind in kept]
+        + [
+            pltpu.VMEM((n, width), WIDE),
+            pltpu.VMEM((width, 3 * part), LOW),
+            pltpu.VMEM((part, width), LOW),
+            pltpu.VMEM((width, inner), LOW),
+            pltpu.VMEM((inner, width), LOW),
+            pltpu.VMEM((16, inner), LOW),
+        ]
+        + group_scratch(n, width)
+        + [
+            pltpu.SemaphoreType.DMA((z.bundles, 4)),
+            pltpu.SemaphoreType.DMA((z.bundles, 4)),
+            pltpu.SemaphoreType.DMA((5,)),
+            pltpu.SemaphoreType.DMA((kinds + 2, layers)),
+            pltpu.VMEM((width // 128, n, 128), WIDE),
+            pltpu.VMEM((CONV_G, packs, depth), LOW),
+            pltpu.VMEM((DEVICES, packs, depth), LOW),
+            pltpu.VMEM((DEVICES, z.gathered * share // 128, 128), LOW),
+            pltpu.VMEM((depth // 128, count, 128), WIDE),
+            pltpu.VMEM((z.lines + 16, depth), WIDE),
+            pltpu.VMEM((z.lines, depth), LOW),
+            pltpu.VMEM((z.lines, depth), LOW),
+            pltpu.VMEM((z.steps, own_width, depth), LOW),
+            pltpu.VMEM((DEVICES, packs, own_width), LOW),
+            pltpu.VMEM((DEVICES, packs, own_width), LOW),
+            pltpu.VMEM((n, width), LOW),
+            pltpu.VMEM((z.vocab, n), LOW),
+            pltpu.VMEM((z.vocab, n), WIDE),
+            pltpu.SemaphoreType.DMA((layers, 2, 4)),
+            pltpu.SemaphoreType.DMA((layers, 2, 4)),
+            pltpu.SemaphoreType.DMA((layers, 2)),
+            pltpu.SemaphoreType.DMA((4, 2)),
+            pltpu.SemaphoreType.DMA((layers, 4)),
+            pltpu.SemaphoreType.DMA((layers, 4)),
+            pltpu.VMEM((width // 128, z.gathered, 128), WIDE),
+            pltpu.VMEM((4, layers, share, 3 * part + inner), LOW),
+            pltpu.VMEM((layers, 16, width), LOW),
+            pltpu.VMEM((z.gathered, 128), WIDE),
+            pltpu.VMEM((z.gathered * share // 128, 128), LOW),
+        ]
+        + swap_sems() * 3,
+        compiler_params=kernel_params(1),
+        cost_estimate=cost(200),
+    )(features, cot_turned, kernel_weight, small, head_weight, ends_own, hidden_bias, joint_weight, expand_weight, output_weight, reduce_weight)
+    return outs[:7], outs[7:10], outs[10 : 10 + z.bundles], outs[10 + z.bundles :]
+
+
+def backward(z, flow, head_sums, whole, mixed, bend, ends, even, odd, taps, held, saved):
+    kinds = len(saved)
+    layers, n, width, part, inner, share = z.layers, z.n, z.width, z.part, z.inner, z.share
+    count, head, heads, packs, gw = z.count, z.head, z.heads, z.packs, z.group_width
+    depth, own_width = PACK * gw, PACK * share
+    bundles = z.bundles
+    row_counts = [z.grad_rows[b % 3] for b in range(bundles)]
+    lines = 8 * (-(-(3 + 6 * layers) // 8))
+    tap_places = [(half, row, cut) for half in range(2) for row in range(4) for cut in range(2)]
+
+    def kernel(*refs):
+        flow_ref, head_ref, whole_ref, mixed_ref, bend_ref, ends_ref = refs[:6]
+        even_ref, odd_ref, taps_ref = refs[6:9]
+        held_refs = refs[9 : 9 + bundles]
+        saved_refs = refs[9 + bundles : 9 + bundles + kinds]
+        rest = refs[9 + bundles + kinds :]
+        feats_ref, kernel_ref, position_ref, sums_ref, heads_ref = rest[:5]
+        joint_ref, expand_ref, reduce_ref, output_ref, small_ref = rest[5:10]
+        rest = rest[10:]
+        parts = rest[:bundles]
+        got_c, got_y, got_h = (rest[k * bundles : (k + 1) * bundles] for k in range(1, 4))
+        rest = rest[4 * bundles :]
+        buffers = rest[:kinds]
+        (x_all, qkv, weights_low, context, residual, m_all, active, slope, outer) = buffers
+        rest = rest[kinds:]
+        inner_low = slope
+        (fed, grad_low, joint, wj, wo, we, wr, low_buf, got, gs, gr, ss, sr) = rest[:13]
+        rest = rest[13:]
+        (rs_s, rs_r, ws, ks, back, vector_sums, all_sums, all_heads, tokens, out_low, low_parts) = rest[:11]
+        (wide, grads_even, grads_odd, collected, out_feats, feat_parts) = rest[11:17]
+        even, odd = weights_low.at[pl.ds(0, z.lines)], weights_low.at[pl.ds(2 * count, z.lines)]
+        (own_back, columns, column_parts, output_own, small_own, fs, cs, cr, ms, mr) = rest[17:27]
+        swaps = [rest[27 + 3 * k : 30 + 3 * k] for k in range(4)]
+        y, x, c, h, l = bits()
+        t = x * 2 + l
+
+        def fetch(kind, layer):
+            pltpu.make_async_copy(saved_refs[kind].at[layer], buffers[kind], ks.at[kind]).start()
+
+        def need(kind):
+            settle(buffers[kind], ks.at[kind])
+
+        def load_feed(layer):
+            fetch(8, layer)
+            load_blocks(held_refs[3 * layer + 2], wr, ws.at[3], 0, z.inner_share)
+            fetch(7, layer)
+            load_rows(held_refs[3 * layer + 1], we, ws.at[2], share, 0, inner)
+            for kind in (6, 5, 4):
+                fetch(kind, layer)
+
+        def load_attend(layer):
+            load_chunks(held_refs[3 * layer], wo, ws.at[1], share, 3 * part, part)
+            for kind in (1, 2, 3, 0):
+                fetch(kind, layer)
+            load_rows(held_refs[3 * layer], wj, ws.at[0], share, 0, 3 * part)
+
+        def vector(name, layer=0):
+            at = z.at[name] + layer
+            return whole_ref[at : at + 1, :]
+
+        def lanes_for(source):
+            def block_for(*place):
+                cut = pl.multiple_of(index_of(*place) * share // 128 * 128, 128)
+                return source.at[:, pl.ds(cut, 128)]
+
+            return block_for
+
+        load_feed(layers - 1)
+        load_attend(layers - 1)
+        greet_all()
+        all_greeted()
+        heads_swap = Swap(lanes_for(head_ref), all_heads, *swaps[0])
+        heads_swap.start()
+        jobs = [
+            Gather(parts[b], got_c[b], got_y[b], got_h[b], rs_s.at[b], rs_r.at[b]) for b in range(bundles)
+        ]
+
+        def column_copies(bundle):
+            layer, kind = bundle // 3, bundle % 3
+            first, extent = ((0, 3 * part), (3 * part, inner))[kind]
+            copies = []
+            for number, mask in enumerate((0, L_BIT, X_BIT, X_BIT | L_BIT)):
+                place = place_of(mask)
+                source = columns.at[layer, pl.ds((place[1] * 2 + place[4]) * share, share), pl.ds(first, extent)]
+                target = column_parts.at[t, layer, :, pl.ds(first, extent)]
+                if mask == 0:
+                    copies.append(pltpu.make_async_copy(source, target, cr.at[layer, kind, 0]))
+                else:
+                    copies.append(
+                        remote(source, target, cs.at[layer, kind, number], cr.at[layer, kind, number], flipped(mask))
+                    )
+            return copies
+
+        def row_move(layer):
+            pairs = [
+                (
+                    output_own.at[layer, pl.ds(chunk * share, share)],
+                    output_ref.at[layer, :, pl.ds(chunk * part, part)],
+                )
+                for chunk in range(4)
+            ]
+            pairs.append((small_own.at[layer], small_ref.at[layer]))
+            return Move(pairs, h == l, H_BIT | L_BIT, ms.at[layer], mr.at[layer])
+
+        def hand_over(bundle):
+            layer, kind = bundle // 3, bundle % 3
+            jobs[bundle].done()
+            if kind == 0:
+                total = jobs[bundle].total(0, 4 * share)
+                columns[layer, :, 0 : 3 * part] = total[:, : 3 * part].astype(LOW)
+                output_own[layer] = total[:, 3 * part :]
+                small_own[layer] = jobs[bundle].total(4 * share, 4 * share + 16)[:, 0:128]
+                row_move(layer).start()
+            elif kind == 1:
+                columns[layer, :, 3 * part :] = jobs[bundle].total(0, 4 * share).astype(LOW)
+            else:
+                end = z.inner_share
+                reduce_ref[layer] = jobs[bundle].total(0, end)
+                sums_ref[8 * layer : 8 * layer + 8, :] = jobs[bundle].total(end, end + 16)[0:8, 0:128]
+                return
+            for copy in column_copies(bundle):
+                copy.start()
+
+        back[...] = flow_ref[...]
+        vector_sums[...] = jnp.zeros_like(vector_sums)
+        vector_sums[2 + 6 * layers : 3 + 6 * layers, :] = whole_ref[z.line : z.line + 1, :]
+
+        for layer in reversed(range(layers)):
+            last = layer == layers - 1
+            attend_job, expand_job, reduce_job = jobs[3 * layer : 3 * layer + 3]
+            after = 3 * layer + 3
+
+            def note(name, value, layer=layer):
+                at = z.at[name] + layer
+                vector_sums[at : at + 1, :] = value
+
+            need(8)
+            outer_grad, final_part, upper_part = normed_back(outer[...], vector("final", layer), back[...])
+            back[...] = outer_grad
+            fed_low = outer_grad.astype(LOW)
+            fed[0, t] = fed_low
+            note("final", final_part)
+            note("upper", upper_part)
+            note("return", jnp.sum(fed_low.astype(WIDE), axis=0, keepdims=True))
+
+            def feed_ready():
+                settle(wr, ws.at[3])
+                need(7)
+
+            def feed_use(j):
+                lines = block_rows(j, n)
+                made = dot_rt(fed[0, j], wr[...]) * slope[lines, :].astype(WIDE)
+                inner_low[lines, :] = made.astype(LOW)
+
+            group_gather(fed.at[0], t, gs, gr, feed_ready, feed_use)
+            if not last:
+                jobs[after].over_h()
+            settle(we, ws.at[2])
+            need(6)
+            need(5)
+
+            def feed_weights(after=after, last=last, expand_job=expand_job, reduce_job=reduce_job):
+                store_rows(expand_job.parts, dot_lt(m_all[...].reshape(count, width), inner_low[...]), share, 0)
+                expand_job.over_c()
+                target = reduce_job.parts
+                store_blocks(target, dot_lt(active[...], fed[0].reshape(count, width)), 0, z.inner_share)
+                hidden_sum = jnp.sum(inner_low[...].astype(WIDE), axis=0, keepdims=True)
+                first = z.inner_share
+                for c_at, y_at, h_at in slots():
+                    at = (y_at * 4 + c_at * 2 + h_at) * z.inner_share
+                    view = relative(target, c_at, y_at, h_at)
+                    view[first : first + 16, :] = jnp.zeros((16, width), LOW)
+                    view[first : first + 16, 0 : z.inner_share] = jnp.broadcast_to(
+                        hidden_sum[:, at : at + z.inner_share], (16, z.inner_share)
+                    ).astype(LOW)
+                reduce_job.over_c()
+                if not last:
+                    hand_over(after + 1)
+
+            got_back = group_scatter(
+                lambda j: dot_rt(inner_low[block_rows(j, n), :], we[...]), t, low_buf, got, ss, sr, feed_weights
+            )
+            expand_job.over_y()
+            reduce_job.over_y()
+            need(4)
+            res_grad, middle_part, lower_part = normed_back(
+                residual[...], vector("middle", layer), back[...] + got_back
+            )
+            back[...] = res_grad
+            note("middle", middle_part)
+            note("lower", lower_part)
+            if layer:
+                load_feed(layer - 1)
+            else:
+                for step in range(z.steps - 1):
+                    half, row, cut = tap_places[step]
+                    target = (we, wr)[half].at[pl.ds(row * own_width, own_width), pl.ds(cut * depth, depth)]
+                    pltpu.make_async_copy(taps_ref.at[step], target, ws.at[2 + half]).start()
+            own_low = res_grad.astype(LOW)
+            fed[1, t] = own_low
+            note("attend", jnp.sum(own_low.astype(WIDE), axis=0, keepdims=True))
+
+            def attend_ready():
+                settle(wo, ws.at[1])
+
+            def attend_use(j):
+                grad_low[block_rows(j, n), :] = dot_rt(fed[1, j], wo[...]).astype(LOW)
+
+            group_gather(fed.at[1], t, gs, gr, attend_ready, attend_use)
+            expand_job.over_h()
+            if not last:
+                hand_over(after + 2)
+                hand_over(after)
+            if layer == 0:
+                pltpu.make_async_copy(
+                    taps_ref.at[z.steps - 1], wo.at[pl.ds(0, own_width), pl.ds(0, depth)], ws.at[1]
+                ).start()
+            for kind in (1, 2, 3):
+                need(kind)
+            for at in range(heads):
+                mine = slice(at * head, (at + 1) * head)
+                queries = qkv[:, mine]
+                keys = qkv[:, part + at * head : part + (at + 1) * head]
+                values = qkv[:, 2 * part + at * head : 2 * part + (at + 1) * head]
+                weights = weights_low[at * count : (at + 1) * count, :]
+                grads = grad_low[:, mine]
+                weights_wide = weights.astype(WIDE)
+                prob_grad = dot_rt(grads, values)
+                delta = jnp.sum(weights_wide * prob_grad, axis=-1, keepdims=True)
+                score_grad = (weights_wide * (prob_grad - delta)).astype(LOW)
+                joint[:, mine] = (dot(score_grad, keys).astype(LOW).astype(WIDE) * z.scale).astype(LOW)
+                joint[:, part + at * head : part + (at + 1) * head] = dot_lt(score_grad, queries).astype(LOW)
+                joint[:, 2 * part + at * head : 2 * part + (at + 1) * head] = dot_lt(weights, grads).astype(LOW)
+            if layer == 0:
+                pltpu.make_async_copy(even_ref, even, ks.at[kinds]).start()
+                pltpu.make_async_copy(odd_ref, odd, ks.at[kinds + 1]).start()
+            settle(wj, ws.at[0])
+            need(0)
+
+            def attend_weights(attend_job=attend_job):
+                target = attend_job.parts
+                store_rows(target, dot_lt(x_all[...].reshape(count, width), joint[...]), share, 0)
+                store_chunks(target, dot_lt(context[...], fed[1].reshape(count, width)), share, 3 * part)
+                joint_sum = jnp.sum(joint[...].astype(WIDE), axis=0, keepdims=True)
+                for c_at, y_at, h_at in slots():
+                    at = (y_at * 4 + c_at * 2 + h_at) * share
+                    view = relative(target, c_at, y_at, h_at)
+                    line = jnp.concatenate(
+                        [
+                            joint_sum[:, at : at + share],
+                            joint_sum[:, 2 * part + at : 2 * part + at + share],
+                            jnp.zeros((1, 128 - 2 * share), WIDE),
+                        ],
+                        axis=1,
+                    )
+                    view[4 * share : 4 * share + 16, :] = jnp.zeros((16, width), LOW)
+                    view[4 * share : 4 * share + 16, 0:128] = jnp.broadcast_to(line, (16, 128)).astype(LOW)
+                attend_job.over_c()
+
+            got_back = group_scatter(
+                lambda j: dot_rt(joint[block_rows(j, n), :], wj[...]), t, low_buf, got, ss, sr, attend_weights
+            )
+            reduce_job.over_h()
+            attend_job.over_y()
+            back[...] = back[...] + got_back
+            if layer:
+                load_attend(layer - 1)
+
+        mixed_grad, entry_part, base_part = normed_back(mixed_ref[...], vector("entry"), back[...])
+        vector_sums[z.at["entry"] : z.at["entry"] + 1, :] = entry_part
+        vector_sums[z.at["base"] : z.at["base"] + 1, :] = base_part
+        back[...] = mixed_grad
+        put_lanes(tokens, mixed_grad * bend_ref[...])
+        for f in range(0, PACK, 4):
+            for q in range(width // 128):
+                four = [tokens[q, pl.ds(f + k, packs, stride=PACK), :] for k in range(4)]
+                for k in range(4):
+                    out_low[4 * q + k, :, f * share : (f + 4) * share] = jnp.concatenate(
+                        [piece[:, k * share : (k + 1) * share] for piece in four], axis=1
+                    ).astype(LOW)
+        low_swap = Swap(lambda *place: out_low.at[index_of(*place)], low_parts, *swaps[1])
+        low_swap.start()
+        sums_swap = Swap(lanes_for(vector_sums), all_sums, *swaps[2])
+        sums_swap.start()
+        mixed_move = Move([(back, own_back)], x == h, X_BIT | H_BIT, fs.at[0], fs.at[1])
+        mixed_move.start()
+        encoded = ends_ref[...]
+        lane = z.named * share % 128
+        bounds = bounds_of(
+            [
+                encoded[:, lane + k : lane + k + 1] * 32.0 + encoded[:, lane + 4 + k : lane + 5 + k]
+                for k in range(4)
+            ],
+            count,
+        )
+        pltpu.make_async_copy(even, even, ks.at[kinds]).wait()
+        pltpu.make_async_copy(odd, odd, ks.at[kinds + 1]).wait()
+        settle(we, ws.at[2])
+        settle(wr, ws.at[3])
+        settle(wo.at[pl.ds(0, own_width), pl.ds(0, depth)], ws.at[1])
+        low_swap.arrived()
+        for at, (y_at, x_at, c_at, h_at, l_at) in enumerate(itertools.product((0, 1), repeat=5)):
+            row, block = y_at * 4 + h_at * 2 + c_at, x_at * 2 + l_at
+            place = pl.ds(block * packs * 8 + row, packs, stride=8)
+            for q in range(own_width // 128):
+                collected[q, place, :] = low_parts[at, :, q * 128 : (q + 1) * 128].astype(WIDE)
+        packed = get_lanes(collected, own_width)
+        position_ref[...] = jnp.sum(packed, axis=0, keepdims=True)
+        spread_ranks(wide, packed, rank_lanes(bounds, count, share), 64)
+        fill_pair(wide, grads_even, grads_odd)
+        across = wide[64 : 64 + z.length, :].T.astype(LOW)
+
+        def taps_at(step):
+            if step == z.steps - 1:
+                return wo[0:own_width, 0:depth]
+            half, row, cut = tap_places[step]
+            return (we, wr)[half][row * own_width : (row + 1) * own_width, cut * depth : (cut + 1) * depth]
+
+        summed = jnp.zeros((z.length, depth), WIDE)
+        for step in range(z.steps):
+            summed = summed + dot(shifted(grads_even, grads_odd, step, z.length), taps_at(z.steps - 1 - step))
+            if step == z.steps // 2:
+                jobs[0].over_h()
+        put_lanes(collected, collect_ranks(summed, rank_lanes(bounds, count, gw), count))
+        for at in range(DEVICES):
+            place = pl.ds((at % 4) * packs * 8 + at // 4, packs, stride=8)
+            for q in range(depth // 128):
+                out_feats[at, :, q * 128 : (q + 1) * 128] = collected[q, place, :].astype(LOW)
+        feats_swap = Swap(lambda *place: out_feats.at[index_of(*place)], feat_parts, *swaps[3])
+        feats_swap.start()
+        hand_over(1)
+        hand_over(2)
+
+        kernel_ref[...] = jnp.zeros_like(kernel_ref)
+        for step in range(z.steps):
+            made = dot(across, shifted(even, odd, step, z.length))
+            for f in range(PACK):
+                begin = (step + 1) * depth - f * gw
+                kernel_ref[:, begin : begin + depth] += made[f * share : (f + 1) * share, :]
+        hand_over(0)
+
+        sums_swap.arrived()
+        sums_ref[8 * layers :, :] = jnp.sum(all_sums[...], axis=0)
+        heads_swap.arrived()
+        heads_ref[...] = jnp.sum(all_heads[...], axis=0)
+        feats_swap.arrived()
+        for f in range(PACK):
+            cut = slice(f * gw, (f + 1) * gw)
+            for q in range(width // 128):
+                tokens[q, pl.ds(f, packs, stride=PACK), :] = jnp.concatenate(
+                    [
+                        feat_parts[at, :, cut].astype(WIDE) + feat_parts[at + 1, :, cut].astype(WIDE)
+                        for at in (4 * q, 4 * q + 2)
+                    ],
+                    axis=1,
+                )
+        mixed_move.done()
+        feats_ref[...] = get_lanes(tokens, width) + own_back[...]
+        for bundle in (4, 3, 1, 0):
+            for copy in column_copies(bundle):
+                copy.wait()
+            layer, kind = bundle // 3, bundle % 3
+            for x_at in range(2):
+                for l_at in range(2):
+                    piece = column_parts.at[x_at * 2 + l_at, layer]
+                    if kind == 0:
+                        for which in range(3):
+                            for y_at in range(2):
+                                for c_at in range(2):
+                                    source = which * part + (y_at * 2 + c_at) * head
+                                    target = which * width + (y_at * 8 + x_at * 4 + c_at * 2 + l_at) * head
+                                    joint_ref[layer, :, target : target + head] = piece[
+                                        :, source : source + head
+                                    ].astype(WIDE)
+                    else:
+                        for c_at, y_at, h_at in slots():
+                            source = 3 * part + (y_at * 4 + c_at * 2 + h_at) * z.inner_share
+                            target = index_of(y_at, x_at, c_at, h_at, l_at) * z.inner_share
+                            expand_ref[layer, :, target : target + z.inner_share] = piece[
+                                :, source : source + z.inner_share
+                            ].astype(WIDE)
+        for layer in range(layers):
+            row_move(layer).done()
+        for swap in (heads_swap, low_swap, sums_swap, feats_swap):
+            swap.sent()
+
+    return pl.pallas_call(
+        kernel,
+        out_shape=[
+            jax.ShapeDtypeStruct((n, width), WIDE),
+            jax.ShapeDtypeStruct((share, (z.steps + 1) * depth), WIDE),
+            jax.ShapeDtypeStruct((1, own_width), WIDE),
+            jax.ShapeDtypeStruct((8 * layers + lines, 128), WIDE),
+            jax.ShapeDtypeStruct((z.vocab, 128), WIDE),
+            jax.ShapeDtypeStruct((layers, share, 3 * width), WIDE),
+            jax.ShapeDtypeStruct((layers, share, 4 * inner), WIDE),
+            jax.ShapeDtypeStruct((layers, z.inner_share, width), WIDE),
+            jax.ShapeDtypeStruct((layers, share, width), WIDE),
+            jax.ShapeDtypeStruct((layers, 16, 128), WIDE),
+        ],
+        in_specs=[IN_VMEM] * 6 + [ANYWHERE] * (3 + bundles + kinds),
+        out_specs=[IN_VMEM] * 10,
+        scratch_shapes=[pltpu.VMEM((2, 2, 2, rows, width), LOW) for rows in row_counts]
+        + [pltpu.VMEM((2, 2, rows, width), LOW) for rows in row_counts]
+        + [pltpu.VMEM((2, rows, width), LOW) for rows in row_counts]
+        + [pltpu.VMEM((rows, width), LOW) for rows in row_counts]
+        + [pltpu.VMEM(array.shape[1:], array.dtype) for array in saved]
+        + [
+            pltpu.VMEM((2, 4, n, width), LOW),
+            pltpu.VMEM((count, part), LOW),
+            pltpu.VMEM((count, 3 * part), LOW),
+            pltpu.VMEM((width, 3 * part), LOW),
+            pltpu.VMEM((part, width), LOW),
+            pltpu.VMEM((width, inner), LOW),
+            pltpu.VMEM((inner, width), LOW),
+        ]
+        + group_scratch(n, width)
+        + [
+            pltpu.SemaphoreType.DMA((bundles, 3)),
+            pltpu.SemaphoreType.DMA((bundles, 3)),
+            pltpu.SemaphoreType.DMA((4,)),
+            pltpu.SemaphoreType.DMA((kinds + 2,)),
+            pltpu.VMEM((n, width), WIDE),
+            pltpu.VMEM((lines, width), WIDE),
+            pltpu.VMEM((DEVICES, lines, 128), WIDE),
+            pltpu.VMEM((DEVICES, z.vocab, 128), WIDE),
+            pltpu.VMEM((width // 128, n, 128), WIDE),
+            pltpu.VMEM((DEVICES, packs, own_width), LOW),
+            pltpu.VMEM((DEVICES, packs, own_width), LOW),
+            pltpu.VMEM((z.lines + 16, own_width), WIDE),
+            pltpu.VMEM((z.lines, own_width), LOW),
+            pltpu.VMEM((z.lines, own_width), LOW),
+            pltpu.VMEM((depth // 128, count, 128), WIDE),
+            pltpu.VMEM((DEVICES, packs, depth), LOW),
+            pltpu.VMEM((DEVICES, packs, depth), LOW),
+            pltpu.VMEM((n, width), WIDE),
+            pltpu.VMEM((layers, 4 * share, 3 * part + inner), LOW),
+            pltpu.VMEM((4, layers, share, 3 * part + inner), LOW),
+            pltpu.VMEM((layers, 4 * share, part), WIDE),
+            pltpu.VMEM((layers, 16, 128), WIDE),
+            pltpu.SemaphoreType.DMA((2, 1)),
+            pltpu.SemaphoreType.DMA((layers, 2, 4)),
+            pltpu.SemaphoreType.DMA((layers, 2, 4)),
+            pltpu.SemaphoreType.DMA((layers, 5)),
+            pltpu.SemaphoreType.DMA((layers, 5)),
+        ]
+        + swap_sems() * 4,
+        compiler_params=kernel_params(2),
+        cost_estimate=cost(220),
+    )(flow, head_sums, whole, mixed, bend, ends, even, odd, taps, *held, *saved)
+
+
+def fast_local(*arguments):
+    (
+        features,
+        utterance_ends,
+        kernel_weight,
+        position_bias,
+        entry_gain,
+        base_shift,
+        joint_weight,
+        query_bias,
+        value_bias,
+        output_weight,
+        attend_bias,
+        middle_gain,
+        lower_shift,
+        expand_weight,
+        hidden_bias,
+        reduce_weight,
+        return_bias,
+        final_gain,
+        upper_shift,
+        head_weight,
+        vocab_bias,
+        cotangent,
+    ) = arguments
+    _, n, width = features.shape
+    layers, inner_all = joint_weight.shape[0], expand_weight.shape[2]
+    vocab = head_weight.shape[1]
+    taps = kernel_weight.shape[1] // (width // CONV_G)
+    z = Sizes(n, width, inner_all // 4, layers, taps, vocab)
+    share = z.share
+
+    small = jnp.concatenate(
+        [entry_gain[None], base_shift[None], attend_bias, middle_gain, lower_shift]
+        + [return_bias, final_gain, upper_shift, query_bias, value_bias]
+        + [position_bias[None], vocab_bias[None]],
+        axis=0,
+    )
+    firsts, conv_saved, held, saved = forward(
+        z,
+        features[0],
+        cotangent[0].T,
+        kernel_weight,
+        small,
+        head_weight,
+        utterance_ends,
+        hidden_bias,
+        joint_weight,
+        expand_weight,
+        output_weight,
+        reduce_weight,
+    )
+    logits, flow, head_sums, whole, mixed, bend, ends = firsts
+    (
+        features_grad,
+        kernel_wide,
+        position_part,
+        sums,
+        heads_sums,
+        joint_own,
+        expand_own,
+        reduce_own,
+        output_own,
+        small_own,
+    ) = backward(z, flow, head_sums, whole, mixed, bend, ends, *conv_saved, held, saved)
+    _, _, _, h, l = bits()
+    place = (h * 2 + l) * share
+    own_sums = lax.dynamic_slice_in_dim(sums[8 * layers :], place, share, axis=1)
+    head_own = lax.dynamic_slice_in_dim(heads_sums, place, share, axis=1).T
+
+    first = PACK * z.group_width
+
+    def own(name):
+        return own_sums[z.at[name] : z.at[name] + layers]
+
+    return (
+        logits.T[None],
+        features_grad[None],
+        kernel_wide[:, first : first + kernel_weight.shape[1]],
+        jnp.sum(position_part.reshape(PACK, share), axis=0),
+        own_sums[0],
+        own_sums[1],
+        joint_own,
+        small_own[:, 0, :share],
+        small_own[:, 0, share : 2 * share],
+        output_own,
+        own("attend"),
+        own("middle"),
+        own("lower"),
+        expand_own,
+        sums[0 : 8 * layers : 8, : z.inner_share],
+        reduce_own,
+        own("return"),
+        own("final"),
+        own("upper"),
+        head_own,
+        own_sums[z.vectors],
+    )
+
+
+def fits(dp_size, seq_size, width):
+    share = width // 32
+    return (
+        dp_size == 8
+        and seq_size == 4
+        and share % 16 == 0
+        and share * 2 == width // CONV_G
+        and share * 2 == width // HEADS
+    )
+
+
+def placed(mesh, width):
+    if fits(mesh.shape["dp"], mesh.shape["seq"], width):
+        body = fast_local
+        mesh = jax.sharding.Mesh(mesh.devices.reshape((2,) * len(AXES)), AXES)
+        split, over, within = AXES[:3], AXES[3:], AXES
+    else:
+        body, split, over, within = local, "dp", "seq", ("dp", "seq")
+    tokens = P(split, over, None)
+    first, first_wide = P(within), P(within, None)
+    second, second_wide = P(None, within), P(None, within, None)
     return jax.shard_map(
-        local,
+        body,
         mesh=mesh,
         in_specs=(
-            P("dp", "seq", None),
-            P("dp", None),
-            P(("dp", "seq"), None),
-            P(("dp", "seq")),
-            P(("dp", "seq")),
-            P(("dp", "seq")),
-            P(None, ("dp", "seq"), None),
-            P(None, ("dp", "seq")),
-            P(None, ("dp", "seq")),
-            P(None, ("dp", "seq"), None),
-            P(None, ("dp", "seq")),
-            P(None, ("dp", "seq")),
-            P(None, ("dp", "seq")),
-            P(None, ("dp", "seq"), None),
-            P(None, ("dp", "seq")),
-            P(None, ("dp", "seq"), None),
-            P(None, ("dp", "seq")),
-            P(None, ("dp", "seq")),
-            P(None, ("dp", "seq")),
-            P(("dp", "seq"), None),
+            tokens,
+            P(split, None),
+            first_wide,
+            first,
+            first,
+            first,
+            second_wide,
+            second,
+            second,
+            second_wide,
+            second,
+            second,
+            second,
+            second_wide,
+            second,
+            second_wide,
+            second,
+            second,
+            second,
+            first_wide,
             P(),
-            P("dp", "seq", None),
+            tokens,
         ),
         out_specs=(
-            P("dp", "seq", None),
-            P("dp", "seq", None),
-            P(("dp", "seq"), None),
-            P(("dp", "seq")),
-            P(("dp", "seq")),
-            P(("dp", "seq")),
-            P(None, ("dp", "seq"), None),
-            P(None, ("dp", "seq")),
-            P(None, ("dp", "seq")),
-            P(None, ("dp", "seq"), None),
-            P(None, ("dp", "seq")),
-            P(None, ("dp", "seq")),
-            P(None, ("dp", "seq")),
-            P(None, ("dp", "seq"), None),
-            P(None, ("dp", "seq")),
-            P(None, ("dp", "seq"), None),
-            P(None, ("dp", "seq")),
-            P(None, ("dp", "seq")),
-            P(None, ("dp", "seq")),
-            P(("dp", "seq"), None),
+            tokens,
+            tokens,
+            first_wide,
+            first,
+            first,
+            first,
+            second_wide,
+            second,
+            second,
+            second_wide,
+            second,
+            second,
+            second,
+            second_wide,
+            second,
+            second_wide,
+            second,
+            second,
+            second,
+            first_wide,
             P(),
         ),
         check_vma=False,
     )
+
+
+def solution(mesh):
+    def whole(*arguments):
+        return placed(mesh, arguments[0].shape[2])(*arguments)
+
+    return whole

time: 4180 us -> 450 us (0.11)
  waiting for transfers between devices: 2720 us -> 0 us
  local copies, waits for them, and re-layouts: 773 us -> 15.8 us
  Pallas kernels: 0 us -> 425 us
  matrix products: 279 us -> 0 us
  blocking collectives: 278 us -> 0 us
  other arithmetic: 78.1 us -> 1.2 us
    reduce_scatter x4 -> x0, waiting for transfers between devices: 2310 us -> none  [the longest x2 1480 us: local(): lax.psum_scatter(layer_term(jnp.int32(0), rows_share * lax.axis_size(('dp...]
    pallas_call x0 -> x2, Pallas kernels: none -> 425 us  [the longest x1 221 us: backward(): pl.pallas_call(kernel, out_shape=[jax.ShapeDtypeStruct((n, width), WIDE),...]
    all_gather x13 -> x0, waiting for transfers between devices: 373 us -> none  [the longest x2 147 us: local(): lax.all_gather(reduce_weight[layer_at], ('dp', 'seq'), axis=0, tiled=True)]
    dot_general x63 -> x0, matrix products: 279 us -> none  [the longest x8 63.8 us: conv_backward(): jnp.einsum('rtgo,rtkgi->goki', grouped, feats_window, preferred_element_t...]
    slice x143 -> x5, local copies, waits for them, and re-layouts: 242 us -> 5.02 us  [the longest x1 2.38 us: fast_local(): kernel_wide[:, first:first + kernel_weight.shape[1]]]
    all_gather x3 -> x0, blocking collectives: 192 us -> none  [the longest x2 126 us: local(): lax.all_gather(hidden_bias[layer_at], ('dp', 'seq'), axis=0, tiled=True)]
    concatenate x3 -> x1, local copies, waits for them, and re-layouts: 176 us -> 3.89 us  [fast_local(): jnp.concatenate([entry_gain[None], base_shift[None], attend_bias, middle_...]
    reshape x8 -> x1, local copies, waits for them, and re-layouts: 145 us -> 0.08 us  [fast_local(): position_part.reshape(PACK, share)]
  transfers between devices with their start and end apart: 25 -> 0, of which waited for: 12 -> 0; matrix products, arithmetic and copies ran while one was open for 24% -> 0% of each run, Pallas kernels for 0% -> 0%
where the time goes in v3:
time: 450 us; the launch traced here: 443 us
  Pallas kernels  425 us (94%)
  local copies, waits for them, and re-layouts  15.8 us (4%)
    pallas_call x1, Pallas kernels, backward(): pl.pallas_call(kernel, out_shape=[jax.ShapeDtypeStruct((n, width), WIDE),...  221 us
    pallas_call x1, Pallas kernels, forward(): pl.pallas_call(kernel, out_shape=[jax.ShapeDtypeStruct((z.vocab, n), WIDE...  204 us

profile of v3, /device:TPU:16, one launch (start us, length us, event | category | flops | bytes accessed | tf_op | source)
XLA Modules:
  0.0 442.9 jit_solution(9503326889532569117)
XLA Ops:
  0.7 3.9 concatenate.3.refs_3_
  4.6 203.9 %shard_map.373 = (f32[32,128]{1,0:T(8,128)}, f32[128,1024]{1,0:T(8,128)}, f32[32,1024]{1,0:T(8,128)}, f32[64,1024]{1,0:T(8,128)}, f32[128,1024]{1,0:T(8,128)}, /...) custom-call(bf16[128,1024]{1,0:T(8,128)(2,1)} %bitcast.30, ...), custom_call_target="tpu_custom_call" | custom-call | flops 219999993856 | bytes 1048576 | tf_op jit(solution)/shard_map/pallas_call | solution.py:1426
  208.5 221.1 %shard_map.374 = (f32[128,1024]{1,0:T(8,128)}, f32[32,9216]{1,0:T(8,128)}, f32[1,256]{1,0:T(1,128)}, f32[32,128]{1,0:T(8,128)}, f32[32,128]{1,0:T(8,128)}, /*ind...) custom-call(f32[128,1024]{1,0:T(8,128)} %get-tuple-element.57.refs_0, ...), custom_call_target="tpu_custom_call" | custom-call | flops 242000003072 | bytes 1048576 | tf_op jit(solution)/shard_map/pallas_call | solution.py:1878
  429.5 0.0 copy-start.8
  429.6 0.0 copy-start.7
  429.6 0.0 copy-start.6
  429.6 0.0 copy-start.5
  429.6 0.0 copy-start.3
  429.6 0.0 copy-start.2
  429.6 0.0 copy-start.4
  429.6 2.4 slice.42
  432.0 0.0 copy-start.1
  432.0 0.5 broadcast.3
  432.5 0.0 copy-done.8
  432.5 0.7 reduce.3
  433.2 0.1 reshape.45
  433.3 0.5 reduce_sum.9
  433.8 0.0 copy-done.7
  433.8 0.6 dynamic-slice_bitcast_fusion.1
  434.4 1.4 fusion
  435.8 0.7 fusion.1
  436.5 0.6 slice.51
  437.0 0.0 copy-done.6
  437.0 0.1 dynamic-slice_bitcast_fusion
  437.1 0.7 copy.43
  437.8 0.0 copy-done.5
  437.8 0.6 copy.50
  438.4 0.0 copy-done.3
  438.4 0.8 copy.51
  439.2 0.0 copy-done.2
  439.2 0.0 copy-start
  439.2 0.9 copy.52
  440.1 0.0 copy-done.4
  440.1 0.7 copy.53
  440.8 0.0 copy-done.1
  440.8 1.0 copy.54
  441.8 0.0 copy-done
  441.8 1.0 copy.55
  (1 shorter events, 0.0 us)
Async XLA Ops:
  429.5 3.0 copy-start.8
  429.6 4.2 copy-start.7
  429.6 7.5 %copy-start.6 = (f32[32,128]{1,0:T(8,128)S(1)}, f32[32,128]{1,0:T(8,128)}, u32[]{:S(2)}) copy-start(f32[32,128]{1,0:T(8,128)} %get-tuple-element.90) | copy-start | bytes 49156
  429.6 8.2 %copy-start.5 = (f32[32,128]{1,0:T(8,128)S(1)}, f32[32,128]{1,0:T(8,128)}, u32[]{:S(2)}) copy-start(f32[32,128]{1,0:T(8,128)} %get-tuple-element.56) | copy-start | bytes 49156
  429.6 8.8 %copy-start.3 = (f32[128,1024]{1,0:T(8,128)S(1)}, f32[128,1024]{1,0:T(8,128)}, u32[]{:S(2)}) copy-start(f32[128,1024]{1,0:T(8,128)} %get-tuple-element.81) | copy-start | bytes 1572868
  429.6 9.6 %copy-start.2 = (f32[2,32,3072]{2,1,0:T(8,128)S(1)}, f32[2,32,3072]{2,1,0:T(8,128)}, u32[]{:S(2)}) copy-start(f32[2,32,3072]{2,1,0:T(8,128)} %get-tuple-element.150) | copy-start | bytes 2359300
  429.6 10.5 %copy-start.4 = (f32[2,32,1024]{2,1,0:T(8,128)S(1)}, f32[2,32,1024]{2,1,0:T(8,128)}, u32[]{:S(2)}) copy-start(f32[2,32,1024]{2,1,0:T(8,128)} %get-tuple-element.153) | copy-start | bytes 786436
  432.0 8.8 %copy-start.1 = (f32[2,32,4096]{2,1,0:T(8,128)S(1)}, f32[2,32,4096]{2,1,0:T(8,128)}, u32[]{:S(2)}) copy-start(f32[2,32,4096]{2,1,0:T(8,128)} %get-tuple-element.157) | copy-start | bytes 3145732
  439.2 2.6 copy-start

commit v4 on v3

--- a/solution.py
+++ b/solution.py
@@ -571,7 +571,7 @@
 
 
 def turned_of(y, x, c, h, l):
-    return index_of(y, h, c, x, l)
+    return index_of(h, l, c, y, x)
 
 
 def flipped(mask):
@@ -649,9 +649,11 @@
 
 
 class Move:
-    def __init__(self, pairs, same, mask, sends, receives):
-        self.pairs, self.same, self.mask = pairs, same, mask
-        self.sends, self.receives = sends, receives
+    def __init__(self, pairs, sends, receives):
+        y, x, _, h, l = bits()
+        self.pairs, self.sends, self.receives = pairs, sends, receives
+        self.same = jnp.logical_and(y == h, x == l)
+        self.peer = {"y": h, "x": l, "h": y, "l": x}
 
     def each(self, action):
         @pl.when(self.same)
@@ -664,11 +666,7 @@
         def _():
             for number, (source, target) in enumerate(self.pairs):
                 copy = remote(
-                    source,
-                    target,
-                    self.sends.at[number],
-                    self.receives.at[number],
-                    flipped(self.mask),
+                    source, target, self.sends.at[number], self.receives.at[number], self.peer
                 )
                 copy.start() if action == "start" else copy.wait()
 
@@ -775,34 +773,34 @@
 
 def group_gather(block, t, sends, receives, ready, use):
     half = block.shape[1] // 2
-    x_peer, l_peer = flipped(X_BIT), flipped(L_BIT)
+    y_peer, x_peer = flipped(Y_BIT), flipped(X_BIT)
     own = block.at[t]
-    to_x = remote(own, own, sends.at[0], receives.at[0], x_peer)
+    to_y = remote(own, own, sends.at[0], receives.at[0], y_peer)
+    to_y.start()
+    to_x = remote(own, own, sends.at[1], receives.at[1], x_peer)
     to_x.start()
-    to_l = remote(own, own, sends.at[1], receives.at[1], l_peer)
-    to_l.start()
     ready()
     use(t)
+    to_y.wait_recv()
+    other = block.at[lax.bitwise_xor(t, 2), pl.ds(0, half)]
+    on_x = remote(other, other, sends.at[2], receives.at[2], x_peer)
+    on_x.start()
     to_x.wait_recv()
-    other = block.at[lax.bitwise_xor(t, 2), pl.ds(0, half)]
-    on_l = remote(other, other, sends.at[2], receives.at[2], l_peer)
-    on_l.start()
-    to_l.wait_recv()
     other = block.at[lax.bitwise_xor(t, 1), pl.ds(half, half)]
-    on_x = remote(other, other, sends.at[3], receives.at[3], x_peer)
-    on_x.start()
+    on_y = remote(other, other, sends.at[3], receives.at[3], y_peer)
+    on_y.start()
     use(lax.bitwise_xor(t, 2))
     use(lax.bitwise_xor(t, 1))
-    on_l.wait_recv()
     on_x.wait_recv()
+    on_y.wait_recv()
     use(lax.bitwise_xor(t, 3))
-    for copy in (to_x, to_l, on_l, on_x):
+    for copy in (to_y, to_x, on_x, on_y):
         copy.wait_send()
 
 
 def group_scatter(part, t, low, got, sends, receives, between=None):
     half = low.shape[1]
-    x_peer, l_peer = flipped(X_BIT), flipped(L_BIT)
+    y_peer, x_peer = flipped(Y_BIT), flipped(X_BIT)
 
     def send(slot, value, peer):
         low[slot] = value.astype(LOW)
@@ -814,27 +812,27 @@
         return got[slot].astype(WIDE)
 
     far = part(lax.bitwise_xor(t, 3))
-    far_x = send(0, far[:half], x_peer)
-    far_l = send(1, far[half:], l_peer)
-    beside_x = part(lax.bitwise_xor(t, 2))
-    near_x = send(2, beside_x[:half], x_peer)
-    beside_l = part(lax.bitwise_xor(t, 1))
-    near_l = send(3, beside_l[half:], l_peer)
+    far_y = send(0, far[:half], y_peer)
+    far_x = send(1, far[half:], x_peer)
+    beside_y = part(lax.bitwise_xor(t, 2))
+    near_y = send(2, beside_y[:half], y_peer)
+    beside_x = part(lax.bitwise_xor(t, 1))
+    near_x = send(3, beside_x[half:], x_peer)
+    far_y.wait_recv()
+    on_x = send(4, beside_x[:half] + arrived(0), x_peer)
     far_x.wait_recv()
-    on_l = send(4, beside_l[:half] + arrived(0), l_peer)
-    far_l.wait_recv()
-    on_x = send(5, beside_x[half:] + arrived(1), x_peer)
+    on_y = send(5, beside_y[half:] + arrived(1), y_peer)
     own = part(t)
     if between is not None:
         between()
+    near_y.wait_recv()
     near_x.wait_recv()
-    near_l.wait_recv()
-    on_l.wait_recv()
     on_x.wait_recv()
+    on_y.wait_recv()
     result = jnp.concatenate(
         [own[:half] + arrived(2) + arrived(4), own[half:] + arrived(3) + arrived(5)], axis=0
     )
-    for copy in (far_x, far_l, near_x, near_l, on_l, on_x):
+    for copy in (far_y, far_x, near_y, near_x, on_x, on_y):
         copy.wait_send()
     return result
 
@@ -855,7 +853,7 @@
 
 
 def slots():
-    return [(c, y, h) for c in range(2) for y in range(2) for h in range(2)]
+    return [(c, h, l) for c in range(2) for h in range(2) for l in range(2)]
 
 
 class Spread:
@@ -863,11 +861,11 @@
         self.held, self.sends, self.receives = held, sends, receives
 
     def copy(self, step):
-        y, _, c, h, _ = bits()
-        own = c * 4 + y * 2 + h
-        near = c * 4 + y * 2 + 1 - h
+        _, _, c, h, l = bits()
+        own = c * 4 + h * 2 + l
+        near = c * 4 + (1 - h) * 2 + l
         view = self.held.at[(pl.ds(own, 1), pl.ds(own, 1), pl.ds(near, 1), pl.ds(c * 4, 4))[step]]
-        peer = flipped((H_BIT, Y_BIT, Y_BIT, C_BIT)[step])
+        peer = flipped((H_BIT, L_BIT, L_BIT, C_BIT)[step])
         return remote(view, view, self.sends.at[step], self.receives.at[step], peer)
 
     def begin(self):
@@ -890,83 +888,81 @@
 
 
 def load_rows(held, target, sem, share, column, width):
-    for slot, (c, y, h) in enumerate(slots()):
-        for x in range(2):
+    for slot in range(PIECES):
+        for at in range(4):
             pltpu.make_async_copy(
-                held.at[slot, pl.ds(x * 2 * share, 2 * share), pl.ds(column, width)],
-                target.at[pl.ds((y * 16 + x * 8 + c * 4 + h * 2) * share, 2 * share), :],
+                held.at[slot, pl.ds(at * share, share), pl.ds(column, width)],
+                target.at[pl.ds((at * PIECES + slot) * share, share), :],
                 sem,
             ).start()
 
 
 def load_chunks(held, target, sem, share, column, width):
-    for slot, (c, y, h) in enumerate(slots()):
+    for slot in range(PIECES):
         for chunk in range(4):
             pltpu.make_async_copy(
                 held.at[slot, pl.ds(chunk * share, share), pl.ds(column, width)],
-                target.at[pl.ds((y * 4 + c * 2 + h) * share, share), pl.ds(chunk * width, width)],
+                target.at[pl.ds(slot * share, share), pl.ds(chunk * width, width)],
                 sem,
             ).start()
 
 
 def load_blocks(held, target, sem, first, share):
-    for slot, (c, y, h) in enumerate(slots()):
+    for slot in range(PIECES):
         pltpu.make_async_copy(
-            held.at[slot, pl.ds(first, share)],
-            target.at[pl.ds((y * 4 + c * 2 + h) * share, share), :],
+            held.at[slot, pl.ds(first, share)], target.at[pl.ds(slot * share, share), :], sem
+        ).start()
+
+
+def load_line(held, target, sem, first, width):
+    for slot in range(PIECES):
+        pltpu.make_async_copy(
+            held.at[slot, pl.ds(first, 16), pl.ds(0, width)],
+            target.at[:, pl.ds(slot * width, width)],
             sem,
         ).start()
 
 
-def load_line(held, target, sem, first, width):
-    for slot, (c, y, h) in enumerate(slots()):
-        pltpu.make_async_copy(
-            held.at[slot, pl.ds(first, 16), pl.ds(0, width)],
-            target.at[:, pl.ds((y * 4 + c * 2 + h) * width, width)],
-            sem,
-        ).start()
-
-
 def settle(target, sem):
     pltpu.make_async_copy(target, target, sem).wait()
 
 
-def relative(target, c, y, h):
-    y_me, _, c_me, h_me, _ = bits()
+def relative(target, c, h, l):
+    _, _, c_me, h_me, l_me = bits()
     return target.at[
-        lax.bitwise_xor(c_me, c), lax.bitwise_xor(y_me, y), lax.bitwise_xor(h_me, h)
+        lax.bitwise_xor(c_me, c), lax.bitwise_xor(l_me, l), lax.bitwise_xor(h_me, h)
     ]
 
 
 def store_rows(target, grads, share, column):
     width = grads.shape[1]
-    for c, y, h in slots():
-        for x in range(2):
-            row = (y * 16 + x * 8 + c * 4 + h * 2) * share
-            relative(target, c, y, h)[
-                x * 2 * share : (x + 1) * 2 * share, column : column + width
-            ] = grads[row : row + 2 * share, :].astype(LOW)
+    for slot, place in enumerate(slots()):
+        for at in range(4):
+            row = (at * PIECES + slot) * share
+            relative(target, *place)[at * share : (at + 1) * share, column : column + width] = grads[
+                row : row + share, :
+            ].astype(LOW)
 
 
 def store_chunks(target, grads, share, column):
     width = grads.shape[1] // 4
-    for c, y, h in slots():
-        row = (y * 4 + c * 2 + h) * share
+    for slot, place in enumerate(slots()):
         for chunk in range(4):
-            relative(target, c, y, h)[
+            relative(target, *place)[
                 chunk * share : (chunk + 1) * share, column : column + width
-            ] = grads[row : row + share, chunk * width : (chunk + 1) * width].astype(LOW)
+            ] = grads[slot * share : (slot + 1) * share, chunk * width : (chunk + 1) * width].astype(LOW)
 
 
 def store_blocks(target, grads, first, share):
-    for c, y, h in slots():
-        row = (y * 4 + c * 2 + h) * share
-        relative(target, c, y, h)[first : first + share, :] = grads[row : row + share, :].astype(LOW)
+    for slot, place in enumerate(slots()):
+        relative(target, *place)[first : first + share, :] = grads[
+            slot * share : (slot + 1) * share, :
+        ].astype(LOW)
 
 
 class Gather:
-    def __init__(self, parts, got_c, got_y, got_h, sends, receives):
-        self.parts, self.got = parts, (got_c, got_y, got_h)
+    def __init__(self, parts, got_c, got_l, got_h, sends, receives):
+        self.parts, self.got = parts, (got_c, got_l, got_h)
         self.sends, self.receives = sends, receives
 
     def copy(self, step):
@@ -976,19 +972,19 @@
             self.got[step],
             self.sends.at[step],
             self.receives.at[step],
-            flipped((C_BIT, Y_BIT, H_BIT)[step]),
+            flipped((C_BIT, L_BIT, H_BIT)[step]),
         )
 
     def over_c(self):
         self.copy(0).start()
 
-    def over_y(self):
+    def over_l(self):
         self.copy(0).wait_recv()
-        for y in (1, 0):
+        for l in (1, 0):
             for h in range(2):
-                summed = self.parts[0, y, h].astype(WIDE) + self.got[0][y, h].astype(WIDE)
-                self.parts[0, y, h] = summed.astype(LOW)
-            if y == 1:
+                summed = self.parts[0, l, h].astype(WIDE) + self.got[0][l, h].astype(WIDE)
+                self.parts[0, l, h] = summed.astype(LOW)
+            if l == 1:
                 self.copy(1).start()
 
     def over_h(self):
@@ -1072,12 +1068,12 @@
         (x_all, qkv, weights_low, context, residual, m_all, active, slope, outer) = rest[:kinds]
         (now, wj, wo, we, wr, hb, low_buf, got, gs, gr, ss, sr) = rest[kinds : kinds + 12]
         (bs, br, ws, ks, tokens, messages, feats, small_all, packed, wide, even, odd, taps, out_messages) = rest[kinds + 12 : kinds + 26]
-        (pres, new_feats, cot, logits_own, cs, cr, rs, fs, ms, mr, lines_out) = rest[kinds + 26 : kinds + 37]
-        (cols, hidden_lines, gathering, message) = rest[kinds + 37 : kinds + 41]
-        swap1, swap2, swap3 = (rest[kinds + 41 + 3 * k : kinds + 44 + 3 * k] for k in range(3))
+        (pres, new_feats, cot, logits_own, cs, cr, rs, fs, lines_out) = rest[kinds + 26 : kinds + 35]
+        (hidden_lines, gathering, message) = rest[kinds + 35 : kinds + 38]
+        swap1, swap2, swap3 = (rest[kinds + 38 + 3 * k : kinds + 41 + 3 * k] for k in range(3))
         y, x, c, h, l = bits()
-        t = x * 2 + l
-        slot = c * 4 + y * 2 + h
+        t = y * 2 + x
+        slot = c * 4 + h * 2 + l
 
         put_lanes(tokens, f_ref[...].astype(WIDE))
         for f in range(0, PACK, 2):
@@ -1090,16 +1086,31 @@
         def column_copies():
             copies = []
             for layer in range(layers):
-                for kind, (first, span) in enumerate(((0, 3 * part), (3 * part, inner))):
-                    target = held[3 * layer + kind].at[slot, pl.ds(t * share, share), pl.ds(0, span)]
-                    for number, mask in enumerate((0, L_BIT, X_BIT, X_BIT | L_BIT)):
-                        place = place_of(mask)
-                        source = cols.at[place[1] * 2 + place[4], layer, :, pl.ds(first, span)]
+                for number, mask in enumerate((0, X_BIT, Y_BIT, X_BIT | Y_BIT)):
+                    place = place_of(mask)
+                    user = place[0] * 2 + place[1]
+                    lines = pl.ds(pl.multiple_of(t * share, share), share)
+                    moved = [
+                        (
+                            0,
+                            jw_ref.at[layer, :, pl.ds(pl.multiple_of(which * width + user * part, part), part)],
+                            held[3 * layer].at[slot, lines, pl.ds(which * part, part)],
+                        )
+                        for which in range(3)
+                    ]
+                    moved.append(
+                        (
+                            1,
+                            ew_ref.at[layer, :, pl.ds(pl.multiple_of(user * inner, inner), inner)],
+                            held[3 * layer + 1].at[slot, lines],
+                        )
+                    )
+                    for at, (kind, source, target) in enumerate(moved):
                         if mask == 0:
-                            copy = pltpu.make_async_copy(source, target, cr.at[layer, kind, 0])
+                            copy = pltpu.make_async_copy(source, target, cr.at[layer, at, 0])
                         else:
                             copy = remote(
-                                source, target, cs.at[layer, kind, number], cr.at[layer, kind, number], flipped(mask)
+                                source, target, cs.at[layer, at, number], cr.at[layer, at, number], flipped(mask)
                             )
                         copies.append((3 * layer + kind, mask, copy))
             return copies
@@ -1107,23 +1118,22 @@
         def row_copies():
             copies = []
             for layer in range(layers):
-                for kind, (source, first) in enumerate(((rw_ref, 0), (hidden_lines, z.inner_share))):
-                    target = held[3 * layer + 2].at[slot, pl.ds(first, source.shape[1])]
-                    copies.append((3 * layer + 2, pltpu.make_async_copy(source.at[layer], target, rs.at[layer, kind])))
+                reduce_held = held[3 * layer + 2].at[slot]
+                moved = [
+                    (2, rw_ref.at[layer], reduce_held.at[pl.ds(0, z.inner_share)]),
+                    (2, hidden_lines.at[layer], reduce_held.at[pl.ds(z.inner_share, 16)]),
+                ] + [
+                    (
+                        0,
+                        ow_ref.at[layer, :, pl.ds(chunk * part, part)],
+                        held[3 * layer].at[slot, pl.ds(chunk * share, share), pl.ds(3 * part, part)],
+                    )
+                    for chunk in range(4)
+                ]
+                for at, (kind, source, target) in enumerate(moved):
+                    copies.append((3 * layer + kind, pltpu.make_async_copy(source, target, rs.at[layer, at])))
             return copies
 
-        moves = []
-        for layer in range(layers):
-            pairs = [
-                (
-                    ow_ref.at[layer, :, pl.ds(chunk * part, part)],
-                    held[3 * layer].at[
-                        c * 4 + y * 2 + l, pl.ds(chunk * share, share), pl.ds(3 * part, part)
-                    ],
-                )
-                for chunk in range(4)
-            ]
-            moves.append(Move(pairs, h == l, H_BIT | L_BIT, ms.at[layer], mr.at[layer]))
         column_all, row_all = column_copies(), row_copies()
         greet_all()
         hidden_lines[...] = jnp.zeros_like(hidden_lines)
@@ -1134,24 +1144,6 @@
         for _, copy in row_all:
             copy.start()
 
-        for x_at in range(2):
-            for l_at in range(2):
-                for layer in range(layers):
-                    for which in range(3):
-                        for y_at in range(2):
-                            cuts = [
-                                which * width + (y_at * 8 + x_at * 4 + c_at * 2 + l_at) * head for c_at in range(2)
-                            ]
-                            at = which * part + y_at * 2 * head
-                            cols[x_at * 2 + l_at, layer, :, at : at + 2 * head] = jnp.concatenate(
-                                [jw_ref[layer, :, cut : cut + head] for cut in cuts], axis=1
-                            )
-                    for c_at, y_at, h_at in slots():
-                        cut = index_of(y_at, x_at, c_at, h_at, l_at) * z.inner_share
-                        at = 3 * part + (y_at * 4 + c_at * 2 + h_at) * z.inner_share
-                        cols[x_at * 2 + l_at, layer, :, at : at + z.inner_share] = ew_ref[
-                            layer, :, cut : cut + z.inner_share
-                        ]
         same = lax.broadcasted_iota(jnp.int32, (share, share), 0) == lax.broadcasted_iota(jnp.int32, (share, share), 1)
         unit = jnp.where(same, 1.0, 0.0).astype(LOW)
         lines_low = small_ref[...].astype(WIDE)
@@ -1176,16 +1168,14 @@
             for number, _, copy in column_all:
                 if number // 3 == layer:
                     copy.start()
-            moves[layer].start()
-
-        launch(0)
+
         to_owners = Swap(lambda *place: messages.at[index_of(*place) // 2], feats, *swap1)
         to_owners.start()
         vectors = Swap(lambda *place: message, small_all, *swap2)
         vectors.start()
-        frames_move = Move([(f_ref, new_feats), (cot_ref, cot)], x == h, X_BIT | H_BIT, fs.at[0], fs.at[1])
+        frames_move = Move([(f_ref, new_feats), (cot_ref, cot)], fs.at[0], fs.at[1])
         frames_move.start()
-        for layer in range(1, layers):
+        for layer in range(layers):
             launch(layer)
 
         def own_ready(bundle):
@@ -1199,11 +1189,8 @@
             for number, copy in row_all:
                 if number == bundle:
                     copy.wait()
-            if bundle % 3 == 0:
-                moves[bundle // 3].done()
             jobs[bundle].begin()
 
-        own_ready(2)
 
         def keep(source, target, sem):
             pltpu.make_async_copy(source, target, sem).start()
@@ -1222,10 +1209,8 @@
                     taps[step, lines, at : at + end - begin] = k_ref[:, begin:end]
         keep(taps, taps_out, ks.at[kinds, 0])
 
+        to_owners.arrived()
         own_ready(0)
-        own_ready(1)
-        to_owners.arrived()
-        jobs[2].forward()
         vectors.arrived()
         for at in range(DEVICES):
             place = pl.ds((at % 4) * packs * 8 + at // 4, packs, stride=8)
@@ -1248,8 +1233,6 @@
         summed = jnp.zeros((z.length, own_width), WIDE)
         for step in range(z.steps):
             summed = summed + dot_rt(shifted(even, odd, step, z.length), taps[step])
-            if step == z.steps // 2:
-                jobs[0].forward()
         made = collect_ranks(summed, rank_lanes(bounds, count, share), count) + position
         put_lanes(packed, made)
         for at in range(DEVICES):
@@ -1258,9 +1241,7 @@
                 out_messages[at, :, q * 128 : (q + 1) * 128] = packed[q, place, :].astype(LOW)
         to_frames = Swap(lambda *place: out_messages.at[turned_of(*place)], pres, *swap3)
         to_frames.start()
-        jobs[0].over_c()
-        jobs[2].over_c()
-        own_ready(3)
+        jobs[0].forward()
 
         for q in range(width // 128):
             for k in range(per_line):
@@ -1274,19 +1255,8 @@
             at = z.at[name] + layer
             return whole[at : at + 1, :]
 
-        heads_lines = jnp.zeros((2 * layers, part), WIDE)
-        for x_at in range(2):
-            for l_at in range(2):
-                cuts = [
-                    whole[
-                        z.at["heads"] : z.at["heads"] + 2 * layers,
-                        (y_at * 16 + x_at * 8 + c_at * 4 + l_at * 2) * share : (y_at * 16 + x_at * 8 + c_at * 4 + l_at * 2 + 2) * share,
-                    ]
-                    for y_at in range(2)
-                    for c_at in range(2)
-                ]
-                heads_lines = jnp.where(t == x_at * 2 + l_at, jnp.concatenate(cuts, axis=1), heads_lines)
-        mine = lax.broadcasted_iota(jnp.int32, (8, 1), 0) == y * 4 + h * 2 + c
+        heads_lines = whole[z.at["heads"] : z.at["heads"] + 2 * layers, pl.ds(pl.multiple_of(t * part, part), part)]
+        mine = lax.broadcasted_iota(jnp.int32, (8, 1), 0) == h * 4 + l * 2 + c
         row_ends = [jnp.sum(jnp.where(mine, end, 0.0), axis=0, keepdims=True).astype(jnp.int32) for end in ends]
         across = lax.broadcasted_iota(jnp.int32, (1, count), 1)
         down = lax.broadcasted_iota(jnp.int32, (count, 1), 0)
@@ -1296,9 +1266,9 @@
 
         frames_move.done()
         to_frames.arrived()
-        jobs[1].forward()
-        own_ready(5)
-        own_ready(4)
+        jobs[0].over_c()
+        own_ready(1)
+        own_ready(2)
         for f in range(PACK):
             cut = slice(f * share, (f + 1) * share)
             for q in range(width // 128):
@@ -1332,9 +1302,9 @@
                 ).astype(LOW)
 
             group_gather(x_all.at[layer], t, gs, gr, attend_ready, attend_use)
+            second.forward()
             if layer == 0:
-                second.over_c()
-                later[0].forward()
+                own_ready(3)
             keep(x_all.at[layer], saved[0].at[layer], ks.at[0, layer])
             keep(qkv.at[layer], saved[1].at[layer], ks.at[1, layer])
             for at in range(heads):
@@ -1351,13 +1321,14 @@
             keep(context.at[layer], saved[3].at[layer], ks.at[3, layer])
             settle(wo, ws.at[1])
 
-            def advance(later=later):
-                if later:
-                    later[0].over_c()
+            def advance(second=second, third=third):
+                second.over_c()
+                third.forward()
 
             attended = group_scatter(
                 lambda j: dot(context[layer, block_rows(j, n), :], wo[...]), t, low_buf, got, ss, sr, advance
             )
+            third.over_c()
             residual[layer] = now[...] + (attended + vector("attend", layer))
             keep(residual.at[layer], saved[4].at[layer], ks.at[4, layer])
             middle = normed(residual[layer], vector("middle", layer), vector("lower", layer))
@@ -1381,7 +1352,9 @@
 
             group_gather(m_all.at[layer], t, gs, gr, feed_ready, feed_use)
             if later:
-                later[2].forward()
+                later[0].forward()
+                own_ready(4)
+                own_ready(5)
             keep(m_all.at[layer], saved[5].at[layer], ks.at[5, layer])
             keep(active.at[layer], saved[6].at[layer], ks.at[6, layer])
             keep(slope.at[layer], saved[7].at[layer], ks.at[7, layer])
@@ -1389,8 +1362,7 @@
 
             def advance_more(later=later):
                 if later:
-                    later[1].forward()
-                    later[2].over_c()
+                    later[0].over_c()
 
             fed = group_scatter(
                 lambda j: dot(active[layer, block_rows(j, n), :], wr[...]), t, low_buf, got, ss, sr, advance_more
@@ -1398,14 +1370,12 @@
             outer[layer] = now[...] + fed + vector("return", layer)
             keep(outer.at[layer], saved[8].at[layer], ks.at[8, layer])
             now[...] = normed(outer[layer], vector("final", layer), vector("upper", layer))
-            if later:
-                later[1].over_c()
         final_low = now[...].astype(LOW)
         head_turned = whole[z.at["head"] : z.at["head"] + z.vocab, :].astype(LOW)
         vocab_at = z.vectors + 2 * layers + 1
         vocab_bias = lines_low[vocab_at : vocab_at + 1, :].astype(LOW)
         logits_own[...] = dot_rt(head_turned, final_low) + dot_lt(vocab_bias, jnp.ones((1, n), LOW))
-        logits_move = Move([(logits_own, logits_ref)], x == h, X_BIT | H_BIT, fs.at[2], fs.at[3])
+        logits_move = Move([(logits_own, logits_ref)], fs.at[2], fs.at[3])
         logits_move.start()
         flow_ref[...] = dot_lt(cot[...], head_turned)
         part_ref[...] = dot(cot[...], final_low)
@@ -1439,7 +1409,7 @@
         ]
         + [jax.ShapeDtypeStruct((PIECES, z.held_rows[b % 3], width), LOW) for b in range(z.bundles)]
         + [jax.ShapeDtypeStruct(shape, kind) for shape, kind in kept],
-        in_specs=[IN_VMEM] * 9 + [ANYWHERE] * 2,
+        in_specs=[IN_VMEM] * 11,
         out_specs=[IN_VMEM] * 7 + [ANYWHERE] * (3 + z.bundles + kinds),
         scratch_shapes=[pltpu.VMEM(shape, kind) for shape, kind in kept]
         + [
@@ -1470,14 +1440,11 @@
             pltpu.VMEM((n, width), LOW),
             pltpu.VMEM((z.vocab, n), LOW),
             pltpu.VMEM((z.vocab, n), WIDE),
-            pltpu.SemaphoreType.DMA((layers, 2, 4)),
-            pltpu.SemaphoreType.DMA((layers, 2, 4)),
-            pltpu.SemaphoreType.DMA((layers, 2)),
+            pltpu.SemaphoreType.DMA((layers, 4, 4)),
+            pltpu.SemaphoreType.DMA((layers, 4, 4)),
+            pltpu.SemaphoreType.DMA((layers, 6)),
             pltpu.SemaphoreType.DMA((4, 2)),
-            pltpu.SemaphoreType.DMA((layers, 4)),
-            pltpu.SemaphoreType.DMA((layers, 4)),
             pltpu.VMEM((width // 128, z.gathered, 128), WIDE),
-            pltpu.VMEM((4, layers, share, 3 * part + inner), LOW),
             pltpu.VMEM((layers, 16, width), LOW),
             pltpu.VMEM((z.gathered, 128), WIDE),
             pltpu.VMEM((z.gathered * share // 128, 128), LOW),
@@ -1509,7 +1476,7 @@
         joint_ref, expand_ref, reduce_ref, output_ref, small_ref = rest[5:10]
         rest = rest[10:]
         parts = rest[:bundles]
-        got_c, got_y, got_h = (rest[k * bundles : (k + 1) * bundles] for k in range(1, 4))
+        got_c, got_l, got_h = (rest[k * bundles : (k + 1) * bundles] for k in range(1, 4))
         rest = rest[4 * bundles :]
         buffers = rest[:kinds]
         (x_all, qkv, weights_low, context, residual, m_all, active, slope, outer) = buffers
@@ -1520,10 +1487,10 @@
         (rs_s, rs_r, ws, ks, back, vector_sums, all_sums, all_heads, tokens, out_low, low_parts) = rest[:11]
         (wide, grads_even, grads_odd, collected, out_feats, feat_parts) = rest[11:17]
         even, odd = weights_low.at[pl.ds(0, z.lines)], weights_low.at[pl.ds(2 * count, z.lines)]
-        (own_back, columns, column_parts, output_own, small_own, fs, cs, cr, ms, mr) = rest[17:27]
-        swaps = [rest[27 + 3 * k : 30 + 3 * k] for k in range(4)]
+        (own_back, columns, joint_low, expand_low, fs, cs, cr) = rest[17:24]
+        swaps = [rest[24 + 3 * k : 27 + 3 * k] for k in range(4)]
         y, x, c, h, l = bits()
-        t = x * 2 + l
+        t = y * 2 + x
 
         def fetch(kind, layer):
             pltpu.make_async_copy(saved_refs[kind].at[layer], buffers[kind], ks.at[kind]).start()
@@ -1556,42 +1523,47 @@
 
             return block_for
 
+        greet_all()
         load_feed(layers - 1)
         load_attend(layers - 1)
-        greet_all()
         all_greeted()
         heads_swap = Swap(lanes_for(head_ref), all_heads, *swaps[0])
         heads_swap.start()
         jobs = [
-            Gather(parts[b], got_c[b], got_y[b], got_h[b], rs_s.at[b], rs_r.at[b]) for b in range(bundles)
+            Gather(parts[b], got_c[b], got_l[b], got_h[b], rs_s.at[b], rs_r.at[b]) for b in range(bundles)
         ]
 
         def column_copies(bundle):
             layer, kind = bundle // 3, bundle % 3
-            first, extent = ((0, 3 * part), (3 * part, inner))[kind]
             copies = []
-            for number, mask in enumerate((0, L_BIT, X_BIT, X_BIT | L_BIT)):
+            for number, mask in enumerate((0, X_BIT, Y_BIT, X_BIT | Y_BIT)):
                 place = place_of(mask)
-                source = columns.at[layer, pl.ds((place[1] * 2 + place[4]) * share, share), pl.ds(first, extent)]
-                target = column_parts.at[t, layer, :, pl.ds(first, extent)]
-                if mask == 0:
-                    copies.append(pltpu.make_async_copy(source, target, cr.at[layer, kind, 0]))
+                owner = place[0] * 2 + place[1]
+                lines = pl.ds(pl.multiple_of(owner * share, share), share)
+                if kind == 0:
+                    moved = [
+                        (
+                            columns.at[layer, lines, pl.ds(which * part, part)],
+                            joint_low.at[layer, :, pl.ds(pl.multiple_of(which * width + t * part, part), part)],
+                        )
+                        for which in range(3)
+                    ]
                 else:
-                    copies.append(
-                        remote(source, target, cs.at[layer, kind, number], cr.at[layer, kind, number], flipped(mask))
-                    )
+                    moved = [
+                        (
+                            columns.at[layer, lines, pl.ds(3 * part, inner)],
+                            expand_low.at[layer, :, pl.ds(pl.multiple_of(t * inner, inner), inner)],
+                        )
+                    ]
+                for at, (source, target) in enumerate(moved):
+                    at += 3 * kind
+                    if mask == 0:
+                        copies.append(pltpu.make_async_copy(source, target, cr.at[layer, at, 0]))
+                    else:
+                        copies.append(
+                            remote(source, target, cs.at[layer, at, number], cr.at[layer, at, number], flipped(mask))
+                        )
             return copies
-
-        def row_move(layer):
-            pairs = [
-                (
-                    output_own.at[layer, pl.ds(chunk * share, share)],
-                    output_ref.at[layer, :, pl.ds(chunk * part, part)],
-                )
-                for chunk in range(4)
-            ]
-            pairs.append((small_own.at[layer], small_ref.at[layer]))
-            return Move(pairs, h == l, H_BIT | L_BIT, ms.at[layer], mr.at[layer])
 
         def hand_over(bundle):
             layer, kind = bundle // 3, bundle % 3
@@ -1599,9 +1571,11 @@
             if kind == 0:
                 total = jobs[bundle].total(0, 4 * share)
                 columns[layer, :, 0 : 3 * part] = total[:, : 3 * part].astype(LOW)
-                output_own[layer] = total[:, 3 * part :]
-                small_own[layer] = jobs[bundle].total(4 * share, 4 * share + 16)[:, 0:128]
-                row_move(layer).start()
+                for chunk in range(4):
+                    output_ref[layer, :, chunk * part : (chunk + 1) * part] = total[
+                        chunk * share : (chunk + 1) * share, 3 * part :
+                    ]
+                small_ref[layer] = jobs[bundle].total(4 * share, 4 * share + 16)[:, 0:128]
             elif kind == 1:
                 columns[layer, :, 3 * part :] = jobs[bundle].total(0, 4 * share).astype(LOW)
             else:
@@ -1645,7 +1619,7 @@
 
             group_gather(fed.at[0], t, gs, gr, feed_ready, feed_use)
             if not last:
-                jobs[after].over_h()
+                jobs[after + 2].over_h()
             settle(we, ws.at[2])
             need(6)
             need(5)
@@ -1657,9 +1631,9 @@
                 store_blocks(target, dot_lt(active[...], fed[0].reshape(count, width)), 0, z.inner_share)
                 hidden_sum = jnp.sum(inner_low[...].astype(WIDE), axis=0, keepdims=True)
                 first = z.inner_share
-                for c_at, y_at, h_at in slots():
-                    at = (y_at * 4 + c_at * 2 + h_at) * z.inner_share
-                    view = relative(target, c_at, y_at, h_at)
+                for slot, place in enumerate(slots()):
+                    at = slot * z.inner_share
+                    view = relative(target, *place)
                     view[first : first + 16, :] = jnp.zeros((16, width), LOW)
                     view[first : first + 16, 0 : z.inner_share] = jnp.broadcast_to(
                         hidden_sum[:, at : at + z.inner_share], (16, z.inner_share)
@@ -1671,8 +1645,10 @@
             got_back = group_scatter(
                 lambda j: dot_rt(inner_low[block_rows(j, n), :], we[...]), t, low_buf, got, ss, sr, feed_weights
             )
-            expand_job.over_y()
-            reduce_job.over_y()
+            if not last:
+                jobs[after].over_h()
+            expand_job.over_l()
+            reduce_job.over_l()
             need(4)
             res_grad, middle_part, lower_part = normed_back(
                 residual[...], vector("middle", layer), back[...] + got_back
@@ -1698,10 +1674,8 @@
                 grad_low[block_rows(j, n), :] = dot_rt(fed[1, j], wo[...]).astype(LOW)
 
             group_gather(fed.at[1], t, gs, gr, attend_ready, attend_use)
-            expand_job.over_h()
             if not last:
                 hand_over(after + 2)
-                hand_over(after)
             if layer == 0:
                 pltpu.make_async_copy(
                     taps_ref.at[z.steps - 1], wo.at[pl.ds(0, own_width), pl.ds(0, depth)], ws.at[1]
@@ -1728,14 +1702,14 @@
             settle(wj, ws.at[0])
             need(0)
 
-            def attend_weights(attend_job=attend_job):
+            def attend_weights(attend_job=attend_job, expand_job=expand_job):
                 target = attend_job.parts
                 store_rows(target, dot_lt(x_all[...].reshape(count, width), joint[...]), share, 0)
                 store_chunks(target, dot_lt(context[...], fed[1].reshape(count, width)), share, 3 * part)
                 joint_sum = jnp.sum(joint[...].astype(WIDE), axis=0, keepdims=True)
-                for c_at, y_at, h_at in slots():
-                    at = (y_at * 4 + c_at * 2 + h_at) * share
-                    view = relative(target, c_at, y_at, h_at)
+                for slot, place in enumerate(slots()):
+                    at = slot * share
+                    view = relative(target, *place)
                     line = jnp.concatenate(
                         [
                             joint_sum[:, at : at + share],
@@ -1747,12 +1721,12 @@
                     view[4 * share : 4 * share + 16, :] = jnp.zeros((16, width), LOW)
                     view[4 * share : 4 * share + 16, 0:128] = jnp.broadcast_to(line, (16, 128)).astype(LOW)
                 attend_job.over_c()
+                expand_job.over_h()
 
             got_back = group_scatter(
                 lambda j: dot_rt(joint[block_rows(j, n), :], wj[...]), t, low_buf, got, ss, sr, attend_weights
             )
-            reduce_job.over_h()
-            attend_job.over_y()
+            attend_job.over_l()
             back[...] = back[...] + got_back
             if layer:
                 load_attend(layer - 1)
@@ -1773,7 +1747,7 @@
         low_swap.start()
         sums_swap = Swap(lanes_for(vector_sums), all_sums, *swaps[2])
         sums_swap.start()
-        mixed_move = Move([(back, own_back)], x == h, X_BIT | H_BIT, fs.at[0], fs.at[1])
+        mixed_move = Move([(back, own_back)], fs.at[0], fs.at[1])
         mixed_move.start()
         encoded = ends_ref[...]
         lane = z.named * share % 128
@@ -1789,9 +1763,11 @@
         settle(we, ws.at[2])
         settle(wr, ws.at[3])
         settle(wo.at[pl.ds(0, own_width), pl.ds(0, depth)], ws.at[1])
+        jobs[2].over_h()
+        hand_over(3)
         low_swap.arrived()
         for at, (y_at, x_at, c_at, h_at, l_at) in enumerate(itertools.product((0, 1), repeat=5)):
-            row, block = y_at * 4 + h_at * 2 + c_at, x_at * 2 + l_at
+            row, block = h_at * 4 + l_at * 2 + c_at, y_at * 2 + x_at
             place = pl.ds(block * packs * 8 + row, packs, stride=8)
             for q in range(own_width // 128):
                 collected[q, place, :] = low_parts[at, :, q * 128 : (q + 1) * 128].astype(WIDE)
@@ -1820,7 +1796,6 @@
         feats_swap = Swap(lambda *place: out_feats.at[index_of(*place)], feat_parts, *swaps[3])
         feats_swap.start()
         hand_over(1)
-        hand_over(2)
 
         kernel_ref[...] = jnp.zeros_like(kernel_ref)
         for step in range(z.steps):
@@ -1828,6 +1803,7 @@
             for f in range(PACK):
                 begin = (step + 1) * depth - f * gw
                 kernel_ref[:, begin : begin + depth] += made[f * share : (f + 1) * share, :]
+        hand_over(2)
         hand_over(0)
 
         sums_swap.arrived()
@@ -1851,27 +1827,10 @@
             for copy in column_copies(bundle):
                 copy.wait()
             layer, kind = bundle // 3, bundle % 3
-            for x_at in range(2):
-                for l_at in range(2):
-                    piece = column_parts.at[x_at * 2 + l_at, layer]
-                    if kind == 0:
-                        for which in range(3):
-                            for y_at in range(2):
-                                for c_at in range(2):
-                                    source = which * part + (y_at * 2 + c_at) * head
-                                    target = which * width + (y_at * 8 + x_at * 4 + c_at * 2 + l_at) * head
-                                    joint_ref[layer, :, target : target + head] = piece[
-                                        :, source : source + head
-                                    ].astype(WIDE)
-                    else:
-                        for c_at, y_at, h_at in slots():
-                            source = 3 * part + (y_at * 4 + c_at * 2 + h_at) * z.inner_share
-                            target = index_of(y_at, x_at, c_at, h_at, l_at) * z.inner_share
-                            expand_ref[layer, :, target : target + z.inner_share] = piece[
-                                :, source : source + z.inner_share
-                            ].astype(WIDE)
-        for layer in range(layers):
-            row_move(layer).done()
+            if kind == 0:
+                joint_ref[layer] = joint_low[layer].astype(WIDE)
+            else:
+                expand_ref[layer] = expand_low[layer].astype(WIDE)
         for swap in (heads_swap, low_swap, sums_swap, feats_swap):
             swap.sent()
 
@@ -1926,19 +1885,79 @@
             pltpu.VMEM((DEVICES, packs, depth), LOW),
             pltpu.VMEM((n, width), WIDE),
             pltpu.VMEM((layers, 4 * share, 3 * part + inner), LOW),
-            pltpu.VMEM((4, layers, share, 3 * part + inner), LOW),
-            pltpu.VMEM((layers, 4 * share, part), WIDE),
-            pltpu.VMEM((layers, 16, 128), WIDE),
+            pltpu.VMEM((layers, share, 3 * width), LOW),
+            pltpu.VMEM((layers, share, 4 * inner), LOW),
             pltpu.SemaphoreType.DMA((2, 1)),
-            pltpu.SemaphoreType.DMA((layers, 2, 4)),
-            pltpu.SemaphoreType.DMA((layers, 2, 4)),
-            pltpu.SemaphoreType.DMA((layers, 5)),
-            pltpu.SemaphoreType.DMA((layers, 5)),
+            pltpu.SemaphoreType.DMA((layers, 4, 4)),
+            pltpu.SemaphoreType.DMA((layers, 4, 4)),
         ]
         + swap_sems() * 4,
         compiler_params=kernel_params(2),
         cost_estimate=cost(220),
     )(flow, head_sums, whole, mixed, bend, ends, even, odd, taps, *held, *saved)
+
+
+def finish(z, arrays, position_part, sums, heads_sums, small_own):
+    layers, share, span = z.layers, z.share, z.taps * z.group_width
+    count = len(arrays)
+    names = ("attend", "middle", "lower", "return", "final", "upper")
+
+    def kernel(*refs):
+        sources, (position_ref, sums_ref, heads_ref, small_ref) = refs[:count], refs[count : count + 4]
+        targets = refs[count + 4 : 2 * count + 4]
+        line_refs, pair_refs = refs[2 * count + 4 : 2 * count + 8], refs[2 * count + 8 : -1]
+        head_ref = refs[-1]
+        for at in range(count):
+            if at == 0:
+                targets[at][0] = sources[at][...]
+            elif at == 1:
+                targets[at][...] = sources[at][:, PACK * z.group_width : PACK * z.group_width + span]
+            else:
+                targets[at][...] = sources[at][...]
+        _, _, _, h, l = bits()
+
+        def own(value):
+            result = value[:, 0:share]
+            for at in range(1, 4):
+                result = jnp.where(h * 2 + l == at, value[:, at * share : (at + 1) * share], result)
+            return result
+
+        mine = own(sums_ref[8 * layers :, :])
+        total = position_ref[:, 0:share]
+        for f in range(1, PACK):
+            total = total + position_ref[:, f * share : (f + 1) * share]
+        line_refs[0][...] = total
+        for number, at in enumerate((z.at["entry"], z.at["base"], z.vectors)):
+            line_refs[1 + number][...] = mine[at : at + 1]
+        for layer in range(layers):
+            here = slice(layer, layer + 1)
+            pair_refs[0][here, :] = small_ref[layer, 0:1, 0:share]
+            pair_refs[1][here, :] = small_ref[layer, 0:1, share : 2 * share]
+            for number, name in enumerate(names):
+                at = z.at[name] + layer
+                pair_refs[2 + number][here, :] = mine[at : at + 1]
+            pair_refs[-1][here, :] = sums_ref[8 * layer : 8 * layer + 1, 0 : z.inner_share]
+        head_ref[...] = own(heads_ref[...])
+
+    shapes = [array.shape for array in arrays]
+    shapes[0] = (1,) + shapes[0]
+    shapes[1] = (share, span)
+    outs = pl.pallas_call(
+        kernel,
+        out_shape=[jax.ShapeDtypeStruct(shape, WIDE) for shape in shapes]
+        + [
+            jax.ShapeDtypeStruct(shape, WIDE)
+            for shape in [(1, share)] * 4
+            + [(layers, share)] * (2 + len(names))
+            + [(layers, z.inner_share), (z.vocab, share)]
+        ],
+        in_specs=[IN_VMEM] * (count + 4),
+        out_specs=[IN_VMEM] * (count + 8 + len(names)),
+        compiler_params=pltpu.CompilerParams(vmem_limit_bytes=62 * 2**20),
+        cost_estimate=cost(5),
+    )(*arrays, position_part, sums, heads_sums, small_own)
+    lines = [line.reshape(share) for line in outs[count : count + 4]]
+    return *outs[:count], lines, outs[count + 4 : -1], outs[-1].T
 
 
 def fast_local(*arguments):
@@ -1971,7 +1990,6 @@
     vocab = head_weight.shape[1]
     taps = kernel_weight.shape[1] // (width // CONV_G)
     z = Sizes(n, width, inner_all // 4, layers, taps, vocab)
-    share = z.share
 
     small = jnp.concatenate(
         [entry_gain[None], base_shift[None], attend_bias, middle_gain, lower_shift]
@@ -2006,38 +2024,46 @@
         output_own,
         small_own,
     ) = backward(z, flow, head_sums, whole, mixed, bend, ends, *conv_saved, held, saved)
-    _, _, _, h, l = bits()
-    place = (h * 2 + l) * share
-    own_sums = lax.dynamic_slice_in_dim(sums[8 * layers :], place, share, axis=1)
-    head_own = lax.dynamic_slice_in_dim(heads_sums, place, share, axis=1).T
-
-    first = PACK * z.group_width
-
-    def own(name):
-        return own_sums[z.at[name] : z.at[name] + layers]
-
+    (
+        features_grad,
+        kernel_own,
+        joint_own,
+        expand_own,
+        reduce_own,
+        output_own,
+        lines,
+        pairs,
+        head_own,
+    ) = finish(
+        z,
+        [features_grad, kernel_wide, joint_own, expand_own, reduce_own, output_own],
+        position_part,
+        sums,
+        heads_sums,
+        small_own,
+    )
     return (
         logits.T[None],
-        features_grad[None],
-        kernel_wide[:, first : first + kernel_weight.shape[1]],
-        jnp.sum(position_part.reshape(PACK, share), axis=0),
-        own_sums[0],
-        own_sums[1],
+        features_grad,
+        kernel_own,
+        lines[0],
+        lines[1],
+        lines[2],
         joint_own,
-        small_own[:, 0, :share],
-        small_own[:, 0, share : 2 * share],
+        pairs[0],
+        pairs[1],
         output_own,
-        own("attend"),
-        own("middle"),
-        own("lower"),
+        pairs[2],
+        pairs[3],
+        pairs[4],
         expand_own,
-        sums[0 : 8 * layers : 8, : z.inner_share],
+        pairs[8],
         reduce_own,
-        own("return"),
-        own("final"),
-        own("upper"),
+        pairs[5],
+        pairs[6],
+        pairs[7],
         head_own,
-        own_sums[z.vectors],
+        lines[3],
     )
 
 

time: 450 us -> 421 us (0.936)
  Pallas kernels: 425 us -> 408 us
  local copies, waits for them, and re-layouts: 15.8 us -> 5.9 us
    pallas_call x1, Pallas kernels: 204 us -> 189 us  [forward(): pl.pallas_call(kernel, out_shape=[jax.ShapeDtypeStruct((z.vocab, n), WIDE...]
    pallas_call x1, Pallas kernels: 221 us -> 214 us  [backward(): pl.pallas_call(kernel, out_shape=[jax.ShapeDtypeStruct((n, width), WIDE),...]
    slice x5 -> x0, local copies, waits for them, and re-layouts: 5.02 us -> none  [the longest x1 2.38 us: fast_local(): kernel_wide[:, first:first + kernel_weight.shape[1]]]
    pallas_call x0 -> x1, Pallas kernels: none -> 4.91 us  [finish(): pl.pallas_call(kernel, out_shape=[jax.ShapeDtypeStruct(shape, WIDE) for s...]
where the time goes in v4:
time: 421 us; the launch traced here: 415 us
  Pallas kernels  408 us (97%)
  local copies, waits for them, and re-layouts  5.9 us (1%)
    pallas_call x1, Pallas kernels, backward(): pl.pallas_call(kernel, out_shape=[jax.ShapeDtypeStruct((n, width), WIDE),...  214 us
    pallas_call x1, Pallas kernels, forward(): pl.pallas_call(kernel, out_shape=[jax.ShapeDtypeStruct((z.vocab, n), WIDE...  189 us

profile of v4, /device:TPU:16, one launch (start us, length us, event | category | flops | bytes accessed | tf_op | source)
XLA Modules:
  0.0 414.9 jit_solution(14635019949507680807)
XLA Ops:
  0.7 3.9 concatenate.3.refs_3_
  4.6 189.2 %shard_map.373 = (f32[32,128]{1,0:T(8,128)}, f32[128,1024]{1,0:T(8,128)}, f32[32,1024]{1,0:T(8,128)}, f32[64,1024]{1,0:T(8,128)}, f32[128,1024]{1,0:T(8,128)}, /...) custom-call(bf16[128,1024]{1,0:T(8,128)(2,1)} %bitcast.22, ...), custom_call_target="tpu_custom_call" | custom-call | flops 219999993856 | bytes 1048576 | tf_op jit(solution)/shard_map/pallas_call | solution.py:1396
  193.8 213.9 %shard_map.374 = (f32[128,1024]{1,0:T(8,128)}, f32[32,9216]{1,0:T(8,128)}, f32[1,256]{1,0:T(1,128)}, f32[32,128]{1,0:T(8,128)}, f32[32,128]{1,0:T(8,128)}, /*ind...) custom-call(f32[128,1024]{1,0:T(8,128)} %get-tuple-element.77.refs_0, ...), custom_call_target="tpu_custom_call" | custom-call | flops 242000003072 | bytes 1048576 | tf_op jit(solution)/shard_map/pallas_call | solution.py:1837
  407.7 0.0 copy-start
  407.7 4.9 %shard_map.375 = (f32[1,128,1024]{2,1,0:T(8,128)}, f32[32,8192]{1,0:T(8,128)}, f32[2,32,3072]{2,1,0:T(8,128)}, f32[2,32,4096]{2,1,0:T(8,128)}, f32[2,128,1024]{2...) custom-call(f32[128,1024]{1,0:T(8,128)} %get-tuple-element.101.refs_, ...), custom_call_target="tpu_custom_call" | custom-call | flops 5500000256 | bytes 1048576 | tf_op jit(solution)/shard_map/pallas_call | solution.py:1945
  412.6 1.4 copy.43
  414.0 0.0 copy-done
  414.1 0.6 copy.45
Async XLA Ops:
  407.7 6.3 %copy-start = (f32[32,128]{1,0:T(8,128)S(1)}, f32[32,128]{1,0:T(8,128)}, u32[]{:S(2)}) copy-start(f32[32,128]{1,0:T(8,128)} %get-tuple-element.76) | copy-start | bytes 49156

commit v5 on v4

--- a/solution.py
+++ b/solution.py
@@ -1378,7 +1378,7 @@
         logits_move = Move([(logits_own, logits_ref)], fs.at[2], fs.at[3])
         logits_move.start()
         flow_ref[...] = dot_lt(cot[...], head_turned)
-        part_ref[...] = dot(cot[...], final_low)
+        part_ref[...] = dot(cot[...], final_low).astype(LOW)
         vocab_sum = dot_rt(jnp.ones((8, n), LOW), cot[...])
         vocab_sum = jnp.concatenate([vocab_sum] * (128 // z.vocab), axis=1)
         whole[z.line : z.line + 8, :] = jnp.concatenate([vocab_sum] * (width // 128), axis=1)
@@ -1398,7 +1398,7 @@
         out_shape=[
             jax.ShapeDtypeStruct((z.vocab, n), WIDE),
             jax.ShapeDtypeStruct((n, width), WIDE),
-            jax.ShapeDtypeStruct((z.vocab, width), WIDE),
+            jax.ShapeDtypeStruct((z.vocab, width), LOW),
             jax.ShapeDtypeStruct((z.gathered, width), WIDE),
             jax.ShapeDtypeStruct((n, width), WIDE),
             jax.ShapeDtypeStruct((n, width), WIDE),
@@ -1734,7 +1734,7 @@
         mixed_grad, entry_part, base_part = normed_back(mixed_ref[...], vector("entry"), back[...])
         vector_sums[z.at["entry"] : z.at["entry"] + 1, :] = entry_part
         vector_sums[z.at["base"] : z.at["base"] + 1, :] = base_part
-        back[...] = mixed_grad
+        m_all[0] = mixed_grad.astype(LOW)
         put_lanes(tokens, mixed_grad * bend_ref[...])
         for f in range(0, PACK, 4):
             for q in range(width // 128):
@@ -1746,9 +1746,7 @@
         low_swap = Swap(lambda *place: out_low.at[index_of(*place)], low_parts, *swaps[1])
         low_swap.start()
         sums_swap = Swap(lanes_for(vector_sums), all_sums, *swaps[2])
-        sums_swap.start()
-        mixed_move = Move([(back, own_back)], fs.at[0], fs.at[1])
-        mixed_move.start()
+        mixed_move = Move([(m_all.at[0], own_back)], fs.at[0], fs.at[1])
         encoded = ends_ref[...]
         lane = z.named * share % 128
         bounds = bounds_of(
@@ -1766,6 +1764,8 @@
         jobs[2].over_h()
         hand_over(3)
         low_swap.arrived()
+        sums_swap.start()
+        mixed_move.start()
         for at, (y_at, x_at, c_at, h_at, l_at) in enumerate(itertools.product((0, 1), repeat=5)):
             row, block = h_at * 4 + l_at * 2 + c_at, y_at * 2 + x_at
             place = pl.ds(block * packs * 8 + row, packs, stride=8)
@@ -1809,7 +1809,7 @@
         sums_swap.arrived()
         sums_ref[8 * layers :, :] = jnp.sum(all_sums[...], axis=0)
         heads_swap.arrived()
-        heads_ref[...] = jnp.sum(all_heads[...], axis=0)
+        heads_ref[...] = jnp.sum(all_heads[...].astype(WIDE), axis=0)
         feats_swap.arrived()
         for f in range(PACK):
             cut = slice(f * gw, (f + 1) * gw)
@@ -1822,7 +1822,7 @@
                     axis=1,
                 )
         mixed_move.done()
-        feats_ref[...] = get_lanes(tokens, width) + own_back[...]
+        feats_ref[...] = get_lanes(tokens, width) + own_back[...].astype(WIDE)
         for bundle in (4, 3, 1, 0):
             for copy in column_copies(bundle):
                 copy.wait()
@@ -1873,7 +1873,7 @@
             pltpu.VMEM((n, width), WIDE),
             pltpu.VMEM((lines, width), WIDE),
             pltpu.VMEM((DEVICES, lines, 128), WIDE),
-            pltpu.VMEM((DEVICES, z.vocab, 128), WIDE),
+            pltpu.VMEM((DEVICES, z.vocab, 128), LOW),
             pltpu.VMEM((width // 128, n, 128), WIDE),
             pltpu.VMEM((DEVICES, packs, own_width), LOW),
             pltpu.VMEM((DEVICES, packs, own_width), LOW),
@@ -1883,7 +1883,7 @@
             pltpu.VMEM((depth // 128, count, 128), WIDE),
             pltpu.VMEM((DEVICES, packs, depth), LOW),
             pltpu.VMEM((DEVICES, packs, depth), LOW),
-            pltpu.VMEM((n, width), WIDE),
+            pltpu.VMEM((n, width), LOW),
             pltpu.VMEM((layers, 4 * share, 3 * part + inner), LOW),
             pltpu.VMEM((layers, share, 3 * width), LOW),
             pltpu.VMEM((layers, share, 4 * inner), LOW),

time: 421 us -> 408 us (0.969)
  Pallas kernels: 408 us -> 395 us
    pallas_call x1, Pallas kernels: 214 us -> 201 us  [backward(): pl.pallas_call(kernel, out_shape=[jax.ShapeDtypeStruct((n, width), WIDE),...]
where the time goes in v5:
time: 408 us; the launch traced here: 402 us
  Pallas kernels  395 us (97%)
  local copies, waits for them, and re-layouts  5.9 us (1%)
    pallas_call x1, Pallas kernels, backward(): pl.pallas_call(kernel, out_shape=[jax.ShapeDtypeStruct((n, width), WIDE),...  201 us
    pallas_call x1, Pallas kernels, forward(): pl.pallas_call(kernel, out_shape=[jax.ShapeDtypeStruct((z.vocab, n), WIDE...  189 us

profile of v5, /device:TPU:16, one launch (start us, length us, event | category | flops | bytes accessed | tf_op | source)
XLA Modules:
  0.0 402.1 jit_solution(14395128407729542251)
XLA Ops:
  0.7 3.9 concatenate.3.refs_3_
  4.6 189.3 %shard_map.373 = (f32[32,128]{1,0:T(8,128)}, f32[128,1024]{1,0:T(8,128)}, bf16[32,1024]{1,0:T(8,128)(2,1)}, f32[64,1024]{1,0:T(8,128)}, f32[128,1024]{1,0:T(8,12...) custom-call(bf16[128,1024]{1,0:T(8,128)(2,1)} %bitcast.22, ...), custom_call_target="tpu_custom_call" | custom-call | flops 219999993856 | bytes 1048576 | tf_op jit(solution)/shard_map/pallas_call | solution.py:1396
  193.9 201.1 %shard_map.374 = (f32[128,1024]{1,0:T(8,128)}, f32[32,9216]{1,0:T(8,128)}, f32[1,256]{1,0:T(1,128)}, f32[32,128]{1,0:T(8,128)}, f32[32,128]{1,0:T(8,128)}, /*ind...) custom-call(f32[128,1024]{1,0:T(8,128)} %get-tuple-element.77.refs_0, ...), custom_call_target="tpu_custom_call" | custom-call | flops 242000003072 | bytes 1048576 | tf_op jit(solution)/shard_map/pallas_call | solution.py:1837
  395.0 0.0 copy-start
  395.0 4.9 %shard_map.375 = (f32[1,128,1024]{2,1,0:T(8,128)}, f32[32,8192]{1,0:T(8,128)}, f32[2,32,3072]{2,1,0:T(8,128)}, f32[2,32,4096]{2,1,0:T(8,128)}, f32[2,128,1024]{2...) custom-call(f32[128,1024]{1,0:T(8,128)} %get-tuple-element.101.refs_, ...), custom_call_target="tpu_custom_call" | custom-call | flops 5500000256 | bytes 1048576 | tf_op jit(solution)/shard_map/pallas_call | solution.py:1945
  399.9 1.4 copy.43
  401.3 0.0 copy-done
  401.3 0.6 copy.45
Async XLA Ops:
  395.0 6.3 %copy-start = (f32[32,128]{1,0:T(8,128)S(1)}, f32[32,128]{1,0:T(8,128)}, u32[]{:S(2)}) copy-start(f32[32,128]{1,0:T(8,128)} %get-tuple-element.76) | copy-start | bytes 49156
